TPU v7x, 256 devices: a whole 4x4x8 slice. The times are simulated.
256 devices in a mesh: ctx: 64 (over x, z, core), head: 4 (over y).
Axes of the slice: x: 4, y: 4, z: 8, core: 2. Of those that a mesh axis runs over, the one named last changes fastest.
Arguments:
- queries: bfloat16 [8192, 64, 576], P('ctx', 'head'), may hold values from -32 to 32
- latent: bfloat16 [8192, 576], P('ctx'), may hold values from -4 to 4
- grad_out: bfloat16 [8192, 64, 512], P('ctx', 'head'), may hold values from -0.29882812 to 0.29882812
- doc_start: int32 [8192], P('ctx'), may hold values from 0 to 8191, as said below
- block_list: int32 [64, 4], P('ctx'), may hold values from -1 to 63, as said below
Outputs:
- attended: bfloat16 [8192, 64, 512], P('ctx', 'head')
- grad_queries: float32 [8192, 64, 576], P('ctx', 'head')
- grad_latent: float32 [8192, 576], P('ctx', 'head')
Inputs may be any that keep to these rules, and one draw needn't show every extreme that they name: Documents are contiguous runs of tokens, each of at most 384 tokens and one of exactly 384; the last token of the sequence is a document of its own; doc_start[i] is the first position of token i's run. `block_list`: row b lists, ascending, every block from the one that holds doc_start[b * 128] through b, then -1; so it holds at most 4 blocks, always b, and some row holds exactly 4.
All inputs are finite; a program needn't handle non-finite values.
Results may differ from a plain program's by a relative error of at most 0.014.
Values may be sent and summed in bfloat16 or wider, within the bound.
No kernel may reach another device: no remote copies, remote signals or barrier semaphores. Data moves between devices by JAX's collectives and lax.ppermute only.
A program may use at most 128 MiB of HBM per device.

v0:
```python
import math

import jax
import jax.numpy as jnp
from jax import lax
from jax.sharding import PartitionSpec as P


def shifted(value, axis, steps):
    count = lax.axis_size(axis)
    leading, last = (max(0, -steps), min(count, count - steps))
    return lax.ppermute(value, axis, [(source, source + steps) for source in range(leading, last)])


def block_terms(
    q_rows, grad_rows, q_pos, q_start, entries, window, window_start, score_scale, grad_window
):
    block_rows = q_rows.shape[0]
    latent_width = grad_rows.shape[2]
    full_width = window.shape[1]
    list_width = entries.shape[0]
    window_rows = window.shape[0]
    valid = entries >= 0
    key_first = entries * block_rows
    row_starts = jnp.clip(key_first - window_start, 0, window_rows - block_rows)
    key_rows = jnp.concatenate(
        [
            lax.dynamic_slice_in_dim(window, row_starts[slot], block_rows, 0)
            for slot in range(list_width)
        ],
        0,
    )
    key_pos = (key_first[:, None] + jnp.arange(block_rows, dtype=jnp.int32)[None, :]).reshape(-1)
    key_valid = jnp.repeat(valid, block_rows)
    allowed = (
        (key_pos[None, :] <= q_pos[:, None])
        & (key_pos[None, :] >= q_start[:, None])
        & key_valid[None, :]
    )
    allowed = allowed[None, :, :]
    score = (
        jnp.einsum("qhc,kc->hqk", q_rows, key_rows, preferred_element_type=jnp.float32)
        * score_scale
    )
    row_top = jnp.max(jnp.where(allowed, score, -1e30), axis=2)
    terms = jnp.where(allowed, jnp.exp(score - row_top[:, :, None]), 0.0)
    lse = row_top + jnp.log(jnp.sum(terms, axis=2))
    weight = jnp.where(allowed, jnp.exp(score - lse[:, :, None]), 0.0)
    weight_b = weight.astype(jnp.bfloat16)
    value_rows = key_rows[:, :latent_width]
    attended = jnp.einsum(
        "hqk,kl->qhl", weight_b, value_rows, preferred_element_type=jnp.float32
    ).astype(jnp.bfloat16)
    delta = jnp.einsum("qhl,qhl->hq", grad_rows, attended, preferred_element_type=jnp.float32)
    grad_weight = jnp.einsum(
        "qhl,kl->hqk", grad_rows, value_rows, preferred_element_type=jnp.float32
    )
    grad_score_b = (weight * (grad_weight - delta[:, :, None])).astype(jnp.bfloat16)
    grad_query = score_scale * jnp.einsum(
        "hqk,kc->qhc", grad_score_b, key_rows, preferred_element_type=jnp.float32
    )
    grad_key = score_scale * jnp.einsum(
        "hqk,qhc->kc", grad_score_b, q_rows, preferred_element_type=jnp.float32
    )
    grad_value = jnp.einsum("hqk,qhl->kl", weight_b, grad_rows, preferred_element_type=jnp.float32)
    grad_key = grad_key + jnp.pad(grad_value, ((0, 0), (0, full_width - latent_width)))
    for slot in range(list_width):
        current = lax.dynamic_slice_in_dim(grad_window, row_starts[slot], block_rows, 0)
        update = grad_key[slot * block_rows : (slot + 1) * block_rows]
        grad_window = lax.dynamic_update_slice_in_dim(
            grad_window, current + update, row_starts[slot], 0
        )
    return (attended, grad_query, grad_window)


def send_home(partials, tok_dev, reach_devices):
    total = partials[reach_devices * tok_dev :]
    for distance in range(1, reach_devices + 1):
        slot_first = (reach_devices - distance) * tok_dev
        piece = partials[slot_first : slot_first + tok_dev]
        total = total + shifted(piece.astype(jnp.bfloat16), "ctx", -distance).astype(piece.dtype)
    return total


def shards(queries, latent, grad_out, doc_start, block_list):
    qb_dev, list_width = block_list.shape
    tok_dev = queries.shape[0]
    block_rows = tok_dev // qb_dev
    latent_width = grad_out.shape[2]
    full_width = latent.shape[1]
    score_scale = 1.0 / math.sqrt(latent_width // 4 + full_width - latent_width)
    place = lax.axis_index("ctx")
    reach_devices = (list_width - 2) // qb_dev + 1
    pieces = [latent]
    for distance in range(1, reach_devices + 1):
        pieces.insert(0, shifted(latent, "ctx", distance))
    window = jnp.concatenate(pieces, 0)
    window_start = (place - reach_devices) * tok_dev
    grad_window = jnp.zeros((window.shape[0], full_width), jnp.float32)
    q_pos = place * tok_dev + 0 + jnp.arange(block_rows, dtype=jnp.int32)
    attended, grad_query, grad_window = block_terms(
        queries,
        grad_out,
        q_pos,
        doc_start,
        block_list[0],
        window,
        window_start,
        score_scale,
        grad_window,
    )
    own_rows = send_home(grad_window, tok_dev, reach_devices)
    grad_latent = lax.psum_scatter(own_rows, "head", scatter_dimension=1, tiled=True)
    return (attended, grad_query, grad_latent)


def solution(mesh):
    placed = (
        P("ctx", "head", None),
        P("ctx", None),
        P("ctx", "head", None),
        P("ctx"),
        P("ctx", None),
    )
    return jax.shard_map(
        shards,
        mesh=mesh,
        in_specs=placed,
        out_specs=(P("ctx", "head", None), P("ctx", "head", None), P("ctx", "head")),
        check_vma=False,
    )
```

profile of v0, /device:TPU:2, one launch (start us, length us, event | category | flops | bytes accessed | tf_op | source)
XLA Modules:
  0.0 128.4 jit_solution(15248694518562661175)
XLA Ops:
  7.2 3.4 %collective-permute-start = (bf16[128,576]{0,1:T(8,128)(2,1)}, bf16[128,576]{0,1:T(8,128)(2,1)S(1)}, u32[]{:S(2)}, u32[]{:S(2)}) collective-permute-start(bf16[128,576]{0,1:T(8,128)(2,1)} %param.6), channel_id=1, source_target_pairs={{0,12},{4,16},{8,20},{12,24},{16,28},{20,32},{24,36},{28,40},{32,4... | collective-permute-start | bytes 442376 | tf_op jit(solution)/shard_map/ppermute | solution.py:12
  10.6 3.8 %collective-permute-start.1 = (bf16[128,576]{0,1:T(8,128)(2,1)}, bf16[128,576]{0,1:T(8,128)(2,1)S(1)}, u32[]{:S(2)}, u32[]{:S(2)}) collective-permute-start(bf16[128,576]{0,1:T(8,128)(2,1)} %param.6), channel_id=1, source_target_pairs={{0,8},{4,12},{8,16},{12,20},{16,24},{20,28},{24,32},{28,36},{32,40... | collective-permute-start | bytes 442376 | tf_op jit(solution)/shard_map/ppermute | solution.py:12
  14.5 3.7 %collective-permute-start.2 = (bf16[128,576]{0,1:T(8,128)(2,1)}, bf16[128,576]{0,1:T(8,128)(2,1)S(1)}, u32[]{:S(2)}, u32[]{:S(2)}) collective-permute-start(bf16[128,576]{0,1:T(8,128)(2,1)} %param.6), channel_id=1, source_target_pairs={{0,4},{4,8},{8,12},{12,16},{16,20},{20,24},{24,28},{28,32},{32,36}... | collective-permute-start | bytes 442376 | tf_op jit(solution)/shard_map/ppermute | solution.py:12
  19.6 0.9 and_and_fusion
  21.1 0.7 fusion.23
  26.9 4.6 %copy.14 = bf16[128,16,512]{0,2,1:T(8,128)(2,1)} copy(bf16[128,16,512]{2,1,0:T(8,128)(2,1)} %param.7) | data formatting | bytes 4194304 | tf_op args[2]
  34.6 2.0 %fusion.2 = (f32[16,128]{1,0:T(8,128)S(1)}, f32[512,128,16]{1,0,2:T(8,128)S(1)}) fusion(pred[128,512]{0,1:T(8,128)(4,1)S(1)} %and_and_fusion, bf16[128,16,576]{0,2,1:T(8,128)(2,1)S(1)} %copy-done, bf16[128,576]{0,1:T(8,128)(2,1)S(1)} %get-tuple-element.10, bf16[128,576]{0,1:T(8,128)(2,1)S(1)} %get-tuple-element.11, ...), kind=kOutput, calls=%fused_computation.7 | convolution fusion | flops 1213462528 | bytes 7217152 | tf_op jit(solution)/shard_map/qhc,kc->hqk/dot_general | solution.py:42
  36.7 0.9 fusion.5
  37.6 1.1 copy-done.1
  38.6 4.2 %bitcast_convert_fusion = (f32[16,128,512]{1,2,0:T(8,128)}, bf16[512,16,128]{2,0,1:T(8,128)(2,1)}) fusion(f32[512,128,16]{1,0,2:T(8,128)S(1)} %get-tuple-element.18, f32[16,128]{1,0:T(8,128)S(1)} %log_add_fusion, pred[128,512]{0,1:T(8,128)(4,1)S(1)} %and_and_fusion, bf16[512,576]{0,1:T(8,128)(2,1)S(1)} %pad_maximum_fusion), kind=kOutput, calls=%fused_computation.15 | convolution fusion | flops 1080033280 | bytes 11083776 | tf_op jit(solution)/shard_map/hqk,kl->qhl/dot_general | solution.py:51
  42.8 5.5 %copy.23 = f32[16,128,512]{2,0,1:T(8,128)} copy(f32[16,128,512]{1,2,0:T(8,128)} %get-tuple-element.19) | data formatting | bytes 8388608
  48.3 3.3 %multiply_reduce_fusion = f32[16,128]{0,1:T(8,128)S(1)} fusion(f32[16,128,512]{2,0,1:T(8,128)} %copy.23, bf16[128,16,512]{2,1,0:T(8,128)(2,1)} %param.7), kind=kLoop, calls=%fused_computation.13 | loop fusion | flops 3143680 | bytes 6299648
  51.7 4.4 %convolution_bitcast_fusion.1 = f32[512,512]{0,1:T(8,128)S(1)} fusion(bf16[128,16,512]{0,2,1:T(8,128)(2,1)} %copy.14, f32[512,128,16]{1,0,2:T(8,128)} %copy-done.1, f32[16,128]{1,0:T(8,128)S(1)} %log_add_fusion, pred[128,512]{0,1:T(8,128)(4,1)S(1)} %and_and_fusion), kind=kOutput, calls=%fused_computation.19 | convolution fusion | flops 1077936128 | bytes 7413760 | tf_op jit(solution)/shard_map/hqk,qhl->kl/dot_general | solution.py:65
  56.5 2.1 %fusion.1 = bf16[16,128,512]{1,2,0:T(8,128)(2,1)S(1)} fusion(f32[512,128,16]{1,0,2:T(8,128)S(1)} %copy-done.2, bf16[128,16,512]{0,2,1:T(8,128)(2,1)S(1)} %copy-done.3, f32[16,128]{1,0:T(8,128)S(1)} %copy.24, f32[16,128]{1,0:T(8,128)S(1)} %log_add_fusion, pred[128,512]{0,1:T(8,128)(4,1)S(1)} %and_and_fusion, bf16[512,576]{0,1:T(8,128)(2,1)S(1)} %pad_maximum_fusion), kind=kOutput, calls=%fused_computation.3 | convolution fusion | flops 1080033280 | bytes 8994816 | tf_op jit(solution)/shard_map/qhl,kl->hqk/dot_general | solution.py:55
  58.6 1.4 %fusion.10 = f32[512,576]{0,1:T(8,128)S(1)} fusion(bf16[16,128,512]{1,2,0:T(8,128)(2,1)S(1)} %fusion.1, bf16[128,16,576]{0,2,1:T(8,128)(2,1)S(1)} %copy-done, f32[512,512]{0,1:T(8,128)S(1)} %convolution_bitcast_fusion.1), kind=kOutput, calls=%fused_computation.20 | convolution fusion | flops 1208549376 | bytes 6684672 | tf_op jit(solution)/shard_map/hqk,qhc->kc/dot_general | solution.py:62
  60.0 0.8 slice.63
  61.3 3.5 %dynamic_update_slice.12 = f32[512,576]{0,1:T(8,128)S(1)} dynamic-update-slice(f32[512,576]{0,1:T(8,128)S(1)} %broadcast_in_dim.40, f32[128,576]{0,1:T(8,128)} %slice.63, s32[]{:T(128)S(6)} %select_n.29, s32[]{:T(128)} %constant.11.clone.1) | dynamic-update-slice | bytes 589828 | tf_op jit(solution)/shard_map/dynamic_update_slice | solution.py:70
  64.8 1.8 %slice_add_fusion.3 = f32[128,576]{0,1:T(8,128)} fusion(f32[512,576]{0,1:T(8,128)} %copy-done.4, f32[512,576]{0,1:T(8,128)S(1)} %dynamic_update_slice.12, s32[]{:T(128)S(6)} %select_n.30), kind=kLoop, calls=%fused_computation.31 | loop fusion | flops 73728 | bytes 884740 | tf_op jit(solution)/shard_map/add | solution.py:71
  66.7 2.9 %dynamic_update_slice.13 = f32[512,576]{0,1:T(8,128)S(1)} dynamic-update-slice(f32[512,576]{0,1:T(8,128)S(1)} %dynamic_update_slice.12, f32[128,576]{0,1:T(8,128)} %slice_add_fusion.3, s32[]{:T(128)S(6)} %select_n.30, s32[]{:T(128)} %constant.11.clone.1) | dynamic-update-slice | bytes 589828 | tf_op jit(solution)/shard_map/dynamic_update_slice | solution.py:70
  69.6 1.8 %slice_add_fusion.2 = f32[128,576]{0,1:T(8,128)} fusion(f32[512,576]{0,1:T(8,128)} %copy-done.4, f32[512,576]{0,1:T(8,128)S(1)} %dynamic_update_slice.13, s32[]{:T(128)S(6)} %select_n.31), kind=kLoop, calls=%fused_computation.30 | loop fusion | flops 73728 | bytes 884740 | tf_op jit(solution)/shard_map/add | solution.py:71
  71.4 3.7 %dynamic_update_slice.14 = f32[512,576]{0,1:T(8,128)S(1)} dynamic-update-slice(f32[512,576]{0,1:T(8,128)S(1)} %dynamic_update_slice.13, f32[128,576]{0,1:T(8,128)} %slice_add_fusion.2, s32[]{:T(128)S(6)} %select_n.31, s32[]{:T(128)} %constant.11.clone.1) | dynamic-update-slice | bytes 589828 | tf_op jit(solution)/shard_map/dynamic_update_slice | solution.py:70
  75.1 1.8 %slice_add_fusion.1 = f32[128,576]{0,1:T(8,128)} fusion(f32[512,576]{0,1:T(8,128)} %copy-done.4, f32[512,576]{0,1:T(8,128)S(1)} %dynamic_update_slice.14, s32[]{:T(128)S(6)} %select_n.32), kind=kLoop, calls=%fused_computation.29 | loop fusion | flops 73728 | bytes 884740 | tf_op jit(solution)/shard_map/add | solution.py:71
  76.9 3.5 %dynamic_update_slice.15 = f32[512,576]{0,1:T(8,128)S(1)} dynamic-update-slice(f32[512,576]{0,1:T(8,128)S(1)} %dynamic_update_slice.14, f32[128,576]{0,1:T(8,128)} %slice_add_fusion.1, s32[]{:T(128)S(6)} %select_n.32, s32[]{:T(128)} %constant.11.clone.1) | dynamic-update-slice | bytes 589828 | tf_op jit(solution)/shard_map/dynamic_update_slice | solution.py:70
  80.6 4.0 %collective-permute-start.3 = (bf16[128,576]{0,1:T(8,128)(2,1)S(1)}, bf16[128,576]{0,1:T(8,128)(2,1)S(1)}, u32[]{:S(2)}, u32[]{:S(2)}) collective-permute-start(bf16[128,576]{0,1:T(8,128)(2,1)S(1)} %get-tuple-element.6), channel_id=1, source_target_pairs={{4,0},{8,4},{12,8},{16,12},{20,16},{24,20},{28,24},{32,28},{36,32}... | collective-permute-start | bytes 442376 | tf_op jit(solution)/shard_map/ppermute | solution.py:12
  84.6 2.4 %collective-permute-start.4 = (bf16[128,576]{0,1:T(8,128)(2,1)S(1)}, bf16[128,576]{0,1:T(8,128)(2,1)S(1)}, u32[]{:S(2)}, u32[]{:S(2)}) collective-permute-start(bf16[128,576]{0,1:T(8,128)(2,1)S(1)} %get-tuple-element.8), channel_id=1, source_target_pairs={{8,0},{12,4},{16,8},{20,12},{24,16},{28,20},{32,24},{36,28},{40,32... | collective-permute-start | bytes 442376 | tf_op jit(solution)/shard_map/ppermute | solution.py:12
  87.0 3.1 %collective-permute-start.5 = (bf16[128,576]{0,1:T(8,128)(2,1)S(1)}, bf16[128,576]{0,1:T(8,128)(2,1)S(1)}, u32[]{:S(2)}, u32[]{:S(2)}) collective-permute-start(bf16[128,576]{0,1:T(8,128)(2,1)S(1)} %get-tuple-element.7), channel_id=1, source_target_pairs={{12,0},{16,4},{20,8},{24,12},{28,16},{32,20},{36,24},{40,28},{44,3... | collective-permute-start | bytes 442376 | tf_op jit(solution)/shard_map/ppermute | solution.py:12
  90.1 2.1 %collective-permute-done.4 = bf16[128,576]{0,1:T(8,128)(2,1)S(1)} collective-permute-done((bf16[128,576]{0,1:T(8,128)(2,1)S(1)}, bf16[128,576]{0,1:T(8,128)(2,1)S(1)}, u32[]{:S(2)}, u32[]{:S(2)}) %collective-permute-start.4) | collective-permute-done | bytes 147488 | tf_op jit(solution)/shard_map/ppermute | solution.py:12
  92.2 3.6 %collective-permute-done.5 = bf16[128,576]{0,1:T(8,128)(2,1)S(1)} collective-permute-done((bf16[128,576]{0,1:T(8,128)(2,1)S(1)}, bf16[128,576]{0,1:T(8,128)(2,1)S(1)}, u32[]{:S(2)}, u32[]{:S(2)}) %collective-permute-start.5) | collective-permute-done | bytes 147488 | tf_op jit(solution)/shard_map/ppermute | solution.py:12
  95.8 0.8 fusion.15
  96.6 4.6 %copy.15 = bf16[128,16,512]{2,1,0:T(8,128)(2,1)} copy(bf16[128,16,512]{0,2,1:T(8,128)(2,1)} %bitcast.80) | data formatting | bytes 4194304
  101.2 5.2 %multiply_bitcast_fusion = f32[128,16,576]{0,2,1:T(8,128)} fusion(bf16[16,128,512]{1,2,0:T(8,128)(2,1)} %copy-done.14, bf16[128,576]{0,1:T(8,128)(2,1)S(1)} %copy-done.8, bf16[128,576]{0,1:T(8,128)(2,1)S(1)} %copy-done.10, bf16[128,576]{0,1:T(8,128)(2,1)S(1)} %copy-done.12, bf16[128,576]{0,1:T(8,128)(2,1)S(1)} %copy-done.6), kind=kOutput, calls=%fused_computation | convolution fusion | flops 1211498496 | bytes 7405568 | tf_op jit(solution)/shard_map/hqk,kc->qhc/dot_general | solution.py:59
  106.4 15.2 %reduce-scatter.2.cloned.1.call-done = f32[128,144]{0,1:T(8,128)} async-done(((f32[128,576]{0,1:T(8,128)}), f32[128,144]{0,1:T(8,128)}) %reduce-scatter.2.cloned.1.call-update) | async-done | bytes 73744 | tf_op jit(solution)/shard_map/reduce_scatter | solution.py:113
  (52 shorter events, 3.8 us)
Async XLA Ops:
  7.2 27.4 %copy-start = (bf16[128,16,576]{0,2,1:T(8,128)(2,1)S(1)}, bf16[128,16,576]{0,2,1:T(8,128)(2,1)}, u32[]{:S(2)}) copy-start(bf16[128,16,576]{0,2,1:T(8,128)(2,1)} %param.5) | copy-start | bytes 7077892
  7.2 114.4 %reduce-scatter.2.cloned.1.call-start = ((), (), s32[]{:S(2)}) async-start(), calls=%async_computation.1 | async-start | bytes 368640 | tf_op jit(solution)/shard_map/reduce_scatter | solution.py:113
  7.2 26.7 %collective-permute-start = (bf16[128,576]{0,1:T(8,128)(2,1)}, bf16[128,576]{0,1:T(8,128)(2,1)S(1)}, u32[]{:S(2)}, u32[]{:S(2)}) collective-permute-start(bf16[128,576]{0,1:T(8,128)(2,1)} %param.6), channel_id=1, source_target_pairs={{0,12},{4,16},{8,20},{12,24},{16,28},{20,32},{24,36},{28,40},{32,4... | collective-permute-start | bytes 442376 | tf_op jit(solution)/shard_map/ppermute | solution.py:12
  10.6 23.4 %collective-permute-start.1 = (bf16[128,576]{0,1:T(8,128)(2,1)}, bf16[128,576]{0,1:T(8,128)(2,1)S(1)}, u32[]{:S(2)}, u32[]{:S(2)}) collective-permute-start(bf16[128,576]{0,1:T(8,128)(2,1)} %param.6), channel_id=1, source_target_pairs={{0,8},{4,12},{8,16},{12,20},{16,24},{20,28},{24,32},{28,36},{32,40... | collective-permute-start | bytes 442376 | tf_op jit(solution)/shard_map/ppermute | solution.py:12
  14.5 19.6 %collective-permute-start.2 = (bf16[128,576]{0,1:T(8,128)(2,1)}, bf16[128,576]{0,1:T(8,128)(2,1)S(1)}, u32[]{:S(2)}, u32[]{:S(2)}) collective-permute-start(bf16[128,576]{0,1:T(8,128)(2,1)} %param.6), channel_id=1, source_target_pairs={{0,4},{4,8},{8,12},{12,16},{16,20},{20,24},{24,28},{28,32},{32,36}... | collective-permute-start | bytes 442376 | tf_op jit(solution)/shard_map/ppermute | solution.py:12
  26.9 7.3 %copy-start.13 = (bf16[128,576]{0,1:T(8,128)(2,1)S(1)}, bf16[128,576]{0,1:T(8,128)(2,1)}, u32[]{:S(2)}) copy-start(bf16[128,576]{0,1:T(8,128)(2,1)} %param.6) | copy-start | bytes 442372
  34.5 2.2 %copy-start.5 = (bf16[128,576]{0,1:T(8,128)(2,1)}, bf16[128,576]{0,1:T(8,128)(2,1)S(1)}, u32[]{:S(2)}) copy-start(bf16[128,576]{0,1:T(8,128)(2,1)S(1)} %get-tuple-element.9) | copy-start | bytes 442372
  34.5 2.2 %copy-start.7 = (bf16[128,576]{0,1:T(8,128)(2,1)}, bf16[128,576]{0,1:T(8,128)(2,1)S(1)}, u32[]{:S(2)}) copy-start(bf16[128,576]{0,1:T(8,128)(2,1)S(1)} %get-tuple-element.10) | copy-start | bytes 442372
  34.5 2.2 %copy-start.9 = (bf16[128,576]{0,1:T(8,128)(2,1)}, bf16[128,576]{0,1:T(8,128)(2,1)S(1)}, u32[]{:S(2)}) copy-start(bf16[128,576]{0,1:T(8,128)(2,1)S(1)} %get-tuple-element.11) | copy-start | bytes 442372
  34.5 2.2 %copy-start.11 = (bf16[128,576]{0,1:T(8,128)(2,1)}, bf16[128,576]{0,1:T(8,128)(2,1)S(1)}, u32[]{:S(2)}) copy-start(bf16[128,576]{0,1:T(8,128)(2,1)S(1)} %get-tuple-element.12) | copy-start | bytes 442372
  36.7 2.0 %copy-start.1 = (f32[512,128,16]{1,0,2:T(8,128)}, f32[512,128,16]{1,0,2:T(8,128)S(1)}, u32[]{:S(2)}) copy-start(f32[512,128,16]{1,0,2:T(8,128)S(1)} %get-tuple-element.18) | copy-start | bytes 12582916
  51.7 4.4 %copy-start.2 = (f32[512,128,16]{1,0,2:T(8,128)S(1)}, f32[512,128,16]{1,0,2:T(8,128)}, u32[]{:S(2)}) copy-start(f32[512,128,16]{1,0,2:T(8,128)} %copy-done.1) | copy-start | bytes 12582916
  51.7 4.8 %copy-start.3 = (bf16[128,16,512]{0,2,1:T(8,128)(2,1)S(1)}, bf16[128,16,512]{0,2,1:T(8,128)(2,1)}, u32[]{:S(2)}) copy-start(bf16[128,16,512]{0,2,1:T(8,128)(2,1)} %copy.14) | copy-start | bytes 6291460
  58.6 1.4 %copy-start.14 = (bf16[16,128,512]{1,2,0:T(8,128)(2,1)}, bf16[16,128,512]{1,2,0:T(8,128)(2,1)S(1)}, u32[]{:S(2)}) copy-start(bf16[16,128,512]{1,2,0:T(8,128)(2,1)S(1)} %fusion.1) | copy-start | bytes 6291460
  60.0 1.1 copy-start.4
  80.6 9.5 %collective-permute-start.3 = (bf16[128,576]{0,1:T(8,128)(2,1)S(1)}, bf16[128,576]{0,1:T(8,128)(2,1)S(1)}, u32[]{:S(2)}, u32[]{:S(2)}) collective-permute-start(bf16[128,576]{0,1:T(8,128)(2,1)S(1)} %get-tuple-element.6), channel_id=1, source_target_pairs={{4,0},{8,4},{12,8},{16,12},{20,16},{24,20},{28,24},{32,28},{36,32}... | collective-permute-start | bytes 442376 | tf_op jit(solution)/shard_map/ppermute | solution.py:12
  84.6 7.6 %collective-permute-start.4 = (bf16[128,576]{0,1:T(8,128)(2,1)S(1)}, bf16[128,576]{0,1:T(8,128)(2,1)S(1)}, u32[]{:S(2)}, u32[]{:S(2)}) collective-permute-start(bf16[128,576]{0,1:T(8,128)(2,1)S(1)} %get-tuple-element.8), channel_id=1, source_target_pairs={{8,0},{12,4},{16,8},{20,12},{24,16},{28,20},{32,24},{36,28},{40,32... | collective-permute-start | bytes 442376 | tf_op jit(solution)/shard_map/ppermute | solution.py:12
  87.0 8.8 %collective-permute-start.5 = (bf16[128,576]{0,1:T(8,128)(2,1)S(1)}, bf16[128,576]{0,1:T(8,128)(2,1)S(1)}, u32[]{:S(2)}, u32[]{:S(2)}) collective-permute-start(bf16[128,576]{0,1:T(8,128)(2,1)S(1)} %get-tuple-element.7), channel_id=1, source_target_pairs={{12,0},{16,4},{20,8},{24,12},{28,16},{32,20},{36,24},{40,28},{44,3... | collective-permute-start | bytes 442376 | tf_op jit(solution)/shard_map/ppermute | solution.py:12
  96.6 4.6 %copy-start.6 = (bf16[128,576]{0,1:T(8,128)(2,1)S(1)}, bf16[128,576]{0,1:T(8,128)(2,1)}, u32[]{:S(2)}) copy-start(bf16[128,576]{0,1:T(8,128)(2,1)} %copy-done.5) | copy-start | bytes 442372
  96.6 4.6 %copy-start.8 = (bf16[128,576]{0,1:T(8,128)(2,1)S(1)}, bf16[128,576]{0,1:T(8,128)(2,1)}, u32[]{:S(2)}) copy-start(bf16[128,576]{0,1:T(8,128)(2,1)} %copy-done.7) | copy-start | bytes 442372
  96.6 4.6 %copy-start.10 = (bf16[128,576]{0,1:T(8,128)(2,1)S(1)}, bf16[128,576]{0,1:T(8,128)(2,1)}, u32[]{:S(2)}) copy-start(bf16[128,576]{0,1:T(8,128)(2,1)} %copy-done.9) | copy-start | bytes 442372
  96.6 4.6 %copy-start.12 = (bf16[128,576]{0,1:T(8,128)(2,1)S(1)}, bf16[128,576]{0,1:T(8,128)(2,1)}, u32[]{:S(2)}) copy-start(bf16[128,576]{0,1:T(8,128)(2,1)} %copy-done.11) | copy-start | bytes 442372
Sparse Core Ops, SparseCore 0:
  96.7 24.8 reduce-scatter.1
where the time goes:
time: 130 us; the launch traced here: 128 us
  local copies, waits for them, and re-layouts  32.3 us (25%)
  between operations  22 us (17%)
  waiting for transfers between devices  20.8 us (16%)
  starting transfers between devices  20.4 us (16%)
  matrix products  19.3 us (15%)
  other arithmetic  13.6 us (10%)
    ppermute x6, starting transfers between devices, shifted(): lax.ppermute(value, axis, [(source, source + steps) for source in range(l...  20.4 us
    unnamed x36, local copies, waits for them, and re-layouts  16.5 us
    reduce_scatter x1, waiting for transfers between devices, shards(): lax.psum_scatter(own_rows, 'head', scatter_dimension=1, tiled=True)  15.2 us
    dynamic_update_slice x4, local copies, waits for them, and re-layouts, block_terms(): lax.dynamic_update_slice_in_dim(grad_window, current + update, row_starts...  13.6 us
    ppermute x6, waiting for transfers between devices, shifted(): lax.ppermute(value, axis, [(source, source + steps) for source in range(l...  5.66 us
    add x3, other arithmetic, block_terms(): current + update  5.5 us
    dot_general x1, matrix products, block_terms(): jnp.einsum('hqk,kc->qhc', grad_score_b, key_rows, preferred_element_type=...  5.17 us
    dot_general x1, matrix products, block_terms(): jnp.einsum('hqk,qhl->kl', weight_b, grad_rows, preferred_element_type=jnp...  4.36 us
  transfers between devices with their start and end apart: 7, of which 3 were waited for; matrix products, arithmetic and copies ran while one was open for 14% of the time, Pallas kernels for 0%

commit v1 on v0

v1 whole, which is shorter than its diff:
```python
import functools
import math

import jax
import jax.numpy as jnp
from jax import lax
from jax.experimental import pallas as pl
from jax.experimental.pallas import tpu as pltpu
from jax.sharding import PartitionSpec as P

F32 = jnp.float32
BF16 = jnp.bfloat16
GROUP = 4
NN = (((1,), (0,)), ((), ()))
NT = (((1,), (1,)), ((), ()))


def shifted(value, axis, steps):
    count = lax.axis_size(axis)
    return lax.ppermute(value, axis, [(s, (s + steps) % count) for s in range(count)])


def dot(a, b, dims=NN):
    return lax.dot_general(a, b, dims, preferred_element_type=F32)


def lanes(ref, count):
    return jnp.concatenate([ref[n] for n in range(count)], axis=1)


def backward_kernel(
    scale, place_ref, entries_ref, start_ref, *refs
):
    list_width = entries_ref.shape[1]
    key_refs = refs[:list_width]
    q_ref, g_ref, weight_ref, score_ref, out_ref, rows_ref, bias_ref, acc_ref = refs[list_width:]
    step = pl.program_id(0)
    width, block = key_refs[0].shape
    latent_width = g_ref.shape[1]
    keys = list_width * block
    place = place_ref[0]

    @pl.when(step == 0)
    def _():
        q_pos = place * block + lax.broadcasted_iota(jnp.int32, (block, block), 1)
        q_start = start_ref[...]
        for slot in range(list_width):
            rows_ref[slot * block : (slot + 1) * block, :] = key_refs[slot][...].T
            entry = place - (list_width - 1) + slot
            listed = entry < 0
            for n in range(list_width):
                listed = listed | (entries_ref[0, n] == entry)
            listed = listed & (entry >= 0)
            first = jnp.where(listed, entry * block, 1 << 24)
            k_pos = first + lax.broadcasted_iota(jnp.int32, (block, block), 0)
            allowed = (k_pos <= q_pos) & (k_pos >= q_start)
            bias_ref[slot * block : (slot + 1) * block, :] = jnp.where(allowed, 0.0, -1e30)
        acc_ref[...] = jnp.zeros_like(acc_ref)

    q_cols = lanes(q_ref, GROUP)
    g_cols = lanes(g_ref, GROUP)
    score = dot(rows_ref[...], q_cols)
    grad_weight = dot(rows_ref[:, :latent_width], g_cols)
    bias = jnp.concatenate([bias_ref[...]] * GROUP, axis=1)
    score = score * (scale * math.log2(math.e)) + bias
    top = jnp.max(score, axis=0, keepdims=True)
    terms = jnp.exp2(score - top)
    weight = terms * (1.0 / jnp.sum(terms, axis=0, keepdims=True))
    delta = jnp.sum(weight * grad_weight, axis=0, keepdims=True)
    grad_score = ((weight * scale) * (grad_weight - delta)).astype(BF16)
    weight_b = weight.astype(BF16)
    weight_ref[0] = weight_b
    score_ref[0] = grad_score
    acc_ref[...] += dot(q_cols, grad_score, NT)
    acc_ref[:latent_width, :] += dot(g_cols, weight_b, NT)

    @pl.when(step == pl.num_programs(0) - 1)
    def _():
        out_ref[...] = acc_ref[...].astype(BF16)


def forward_kernel(*refs):
    key_refs = refs[:-6]
    weight_ref, score_ref, att_ref, gq_ref, cols_ref, rows_ref = refs[-6:]
    block = key_refs[0].shape[1]
    latent_width = att_ref.shape[2]

    @pl.when(pl.program_id(0) == 0)
    def _():
        for slot, key_ref in enumerate(key_refs):
            cols_ref[:, slot * block : (slot + 1) * block] = key_ref[...]
            rows_ref[slot * block : (slot + 1) * block, :] = key_ref[:latent_width, :].T

    grad = dot(cols_ref[...], score_ref[0])
    for n in range(GROUP):
        gq_ref[n] = grad[:, n * block : (n + 1) * block]
    att = dot(weight_ref[0].T, rows_ref[...])
    for n in range(GROUP):
        att_ref[n] = att[n * block : (n + 1) * block, :].astype(BF16)


def shards(queries, latent, grad_out, doc_start, block_list):
    list_width = block_list.shape[1]
    block, heads, width = queries.shape
    latent_width = grad_out.shape[2]
    scale = 1.0 / math.sqrt(latent_width // 4 + width - latent_width)
    ctx = lax.axis_index("ctx").astype(jnp.int32)
    keys = list_width * block
    steps = heads // GROUP
    rows = GROUP * block

    latent_t = latent.T
    window = [shifted(latent_t, "ctx", d) for d in range(list_width - 1, 0, -1)] + [latent_t]
    q_t = queries.transpose(1, 2, 0)
    g_t = grad_out.transpose(1, 2, 0)

    whole = lambda shape: pl.BlockSpec(shape, lambda i: (0,) * len(shape))
    by_step = lambda *tail: pl.BlockSpec((1, *tail), lambda i: (i,) + (0,) * len(tail))
    by_group = lambda *tail: pl.BlockSpec((GROUP, *tail), lambda i: (i,) + (0,) * len(tail))
    smem = pl.BlockSpec(memory_space=pltpu.SMEM)
    weight, grad_score, partial = pl.pallas_call(
        functools.partial(backward_kernel, scale),
        grid=(steps,),
        in_specs=[smem, smem, whole((1, block))]
        + [whole((width, block))] * list_width
        + [by_group(width, block), by_group(latent_width, block)],
        out_specs=[by_step(keys, rows), by_step(keys, rows), whole((width, keys))],
        out_shape=[
            jax.ShapeDtypeStruct((steps, keys, rows), BF16),
            jax.ShapeDtypeStruct((steps, keys, rows), BF16),
            jax.ShapeDtypeStruct((width, keys), BF16),
        ],
        scratch_shapes=[
            pltpu.VMEM((keys, width), BF16),
            pltpu.VMEM((keys, block), F32),
            pltpu.VMEM((width, keys), F32),
        ],
        compiler_params=pltpu.CompilerParams(vmem_limit_bytes=40 << 20),
        cost_estimate=pl.CostEstimate(
            flops=2 * heads * block * keys * 2 * (width + latent_width),
            bytes_accessed=12 << 20,
            transcendentals=heads * block * keys,
        ),
        name="backward",
    )(ctx.reshape(1), block_list, doc_start.reshape(1, block), *window, q_t, g_t)

    head = lax.axis_index("head")
    parts = lax.axis_size("head")
    share = width // parts
    pieces = partial.reshape(parts, share, keys)
    piece = lambda n: lax.dynamic_index_in_dim(pieces, (head + n) % parts, 0, keepdims=False)
    arrived = [shifted(piece(n), "head", n) for n in range(1, parts)]
    own = piece(0).astype(F32)
    for part in arrived:
        own = own + part.astype(F32)
    total = own[:, keys - block :]
    for d in range(1, list_width):
        first = keys - (d + 1) * block
        total = total + shifted(own[:, first : first + block].astype(BF16), "ctx", -d).astype(F32)

    att, gq = pl.pallas_call(
        forward_kernel,
        grid=(steps,),
        in_specs=[whole((width, block))] * list_width + [by_step(keys, rows), by_step(keys, rows)],
        out_specs=[by_group(block, latent_width), by_group(width, block)],
        out_shape=[
            jax.ShapeDtypeStruct((heads, block, latent_width), BF16),
            jax.ShapeDtypeStruct((heads, width, block), F32),
        ],
        scratch_shapes=[pltpu.VMEM((width, keys), BF16), pltpu.VMEM((keys, latent_width), BF16)],
        compiler_params=pltpu.CompilerParams(vmem_limit_bytes=40 << 20),
        cost_estimate=pl.CostEstimate(
            flops=2 * heads * block * keys * (width + latent_width),
            bytes_accessed=12 << 20,
            transcendentals=0,
        ),
        name="forward",
    )(*window, weight, grad_score)
    return (att.transpose(1, 0, 2), gq.transpose(2, 0, 1), total.T)


def solution(mesh):
    placed = (
        P("ctx", "head", None),
        P("ctx", None),
        P("ctx", "head", None),
        P("ctx"),
        P("ctx", None),
    )
    return jax.shard_map(
        shards,
        mesh=mesh,
        in_specs=placed,
        out_specs=(P("ctx", "head", None), P("ctx", "head", None), P("ctx", "head")),
        check_vma=False,
    )
```

time: 130 us -> 57.9 us (0.45)
  the two profiles are of different devices: /device:TPU:2 before, /device:TPU:1 now
where the time goes in v1:
time: 57.9 us; the launch traced here: 57.7 us
  starting transfers between devices  18.6 us (32%)
  local copies, waits for them, and re-layouts  12.7 us (22%)
  Pallas kernels  12.7 us (22%)
  waiting for transfers between devices  11.3 us (20%)
  other arithmetic  1.71 us (3%)
  between operations  0.72 us (1%)
    ppermute x9, starting transfers between devices, shifted(): lax.ppermute(value, axis, [(s, (s + steps) % count) for s in range(count)])  18.6 us
    unnamed x18, local copies, waits for them, and re-layouts  11.9 us
    ppermute x9, waiting for transfers between devices, shifted(): lax.ppermute(value, axis, [(s, (s + steps) % count) for s in range(count)])  11.3 us
    pallas_call x1, Pallas kernels, shards(): pl.pallas_call(functools.partial(backward_kernel, scale), grid=(steps,),...  8.68 us
    pallas_call x1, Pallas kernels, shards(): pl.pallas_call(forward_kernel, grid=(steps,), in_specs=[whole((width, blo...  3.97 us
  transfers between devices with their start and end apart: 9, of which 5 were waited for; matrix products, arithmetic and copies ran while one was open for 10% of the time, Pallas kernels for 7%

profile of v1, /device:TPU:1, one launch (start us, length us, event | category | flops | bytes accessed | tf_op | source)
XLA Modules:
  0.0 57.7 jit_solution(5446715136304598570)
XLA Ops:
  0.6 3.1 %collective-permute-start.2 = (bf16[576,128]{1,0:T(8,128)(2,1)}, bf16[576,128]{1,0:T(8,128)(2,1)S(1)}, u32[]{:S(2)}, u32[]{:S(2)}) collective-permute-start(bf16[576,128]{1,0:T(8,128)(2,1)} %bitcast.25), channel_id=1, source_target_pairs={{0,4},{4,8},{8,12},{12,16},{16,20},{20,24},{24,28},{28,32},{32,36}... | collective-permute-start | bytes 442376 | tf_op jit(solution)/shard_map/ppermute | solution.py:20
  3.7 1.6 %collective-permute-start.1 = (bf16[576,128]{1,0:T(8,128)(2,1)}, bf16[576,128]{1,0:T(8,128)(2,1)S(1)}, u32[]{:S(2)}, u32[]{:S(2)}) collective-permute-start(bf16[576,128]{1,0:T(8,128)(2,1)} %bitcast.26), channel_id=1, source_target_pairs={{0,8},{4,12},{8,16},{12,20},{16,24},{20,28},{24,32},{28,36},{32,40... | collective-permute-start | bytes 442376 | tf_op jit(solution)/shard_map/ppermute | solution.py:20
  5.4 1.7 %collective-permute-start = (bf16[576,128]{1,0:T(8,128)(2,1)}, bf16[576,128]{1,0:T(8,128)(2,1)S(1)}, u32[]{:S(2)}, u32[]{:S(2)}) collective-permute-start(bf16[576,128]{1,0:T(8,128)(2,1)} %bitcast.27), channel_id=1, source_target_pairs={{0,12},{4,16},{8,20},{12,24},{16,28},{20,32},{24,36},{28,40},{32,4... | collective-permute-start | bytes 442376 | tf_op jit(solution)/shard_map/ppermute | solution.py:20
  7.1 3.5 %copy.8 = bf16[128,16,512]{0,2,1:T(8,128)(2,1)S(1)} copy(bf16[128,16,512]{2,1,0:T(8,128)(2,1)} %param.7) | data formatting | bytes 4194304 | tf_op args[2]
  10.6 0.0 collective-permute-done.2.refs_2_
  10.6 5.2 %collective-permute-done.1.refs_1_ = bf16[576,128]{1,0:T(8,128)(2,1)S(1)} collective-permute-done((bf16[576,128]{1,0:T(8,128)(2,1)}, bf16[576,128]{1,0:T(8,128)(2,1)S(1)}, u32[]{:S(2)}, u32[]{:S(2)}) %collective-permute-start.1) | collective-permute-done | bytes 147488 | tf_op jit(solution)/shard_map/ppermute | solution.py:20
  15.9 1.9 %collective-permute-done.refs_0_ = bf16[576,128]{1,0:T(8,128)(2,1)S(1)} collective-permute-done((bf16[576,128]{1,0:T(8,128)(2,1)}, bf16[576,128]{1,0:T(8,128)(2,1)S(1)}, u32[]{:S(2)}, u32[]{:S(2)}) %collective-permute-start) | collective-permute-done | bytes 147488 | tf_op jit(solution)/shard_map/ppermute | solution.py:20
  17.7 0.0 copy-done.3
  17.7 0.0 copy-start
  17.7 1.7 %copy-done = bf16[128,16,576]{0,2,1:T(8,128)(2,1)S(1)} copy-done((bf16[128,16,576]{0,2,1:T(8,128)(2,1)S(1)}, bf16[128,16,576]{0,2,1:T(8,128)(2,1)}, u32[]{:S(2)}) %copy-start) | copy-done | bytes 2359320
  19.4 8.7 %backward.1 = (bf16[4,512,512]{2,1,0:T(8,128)(2,1)S(1)}, bf16[4,512,512]{2,1,0:T(8,128)(2,1)S(1)}, bf16[576,512]{1,0:T(8,128)(2,1)S(1)}) custom-call(s32[1]{0:T(128)} %bitcast.1.place_ref, s32[1,4]{1,0:T(1,128)S(1)} %copy-done.2, s32[1,128]{1,0:T(1,128)S(1)} %bitcast.30, bf16[576,128]{1,0:T(8,128)(2,1)S(1)} %collective-permute-done.refs_0_, ...), custom_call_target="tpu_custom_call" | custom-call | flops 4563402752 | bytes 12582912 | tf_op jit(solution)/shard_map/backward/pallas_call | solution.py:121
  28.1 0.0 copy-start.4
  28.1 1.3 %copy-done.4 = bf16[4,512,512]{2,1,0:T(8,128)(2,1)} copy-done((bf16[4,512,512]{2,1,0:T(8,128)(2,1)}, bf16[4,512,512]{2,1,0:T(8,128)(2,1)S(1)}, u32[]{:S(2)}) %copy-start.4) | copy-done | bytes 2097176
  29.4 1.3 %copy-done.6 = bf16[4,512,512]{2,1,0:T(8,128)(2,1)} copy-done((bf16[4,512,512]{2,1,0:T(8,128)(2,1)}, bf16[4,512,512]{2,1,0:T(8,128)(2,1)S(1)}, u32[]{:S(2)}) %copy-start.6) | copy-done | bytes 2097176
  30.7 0.8 %dynamic-slice_bitcast_fusion.2 = (bf16[144,512]{1,0:T(8,128)(2,1)}, bf16[144,512]{1,0:T(8,128)(2,1)}, bf16[144,512]{1,0:T(8,128)(2,1)}) fusion(bf16[4,144,512]{2,1,0:T(8,128)(2,1)S(1)} %bitcast.22, s32[]{:T(128)S(6)} %select_n.35, s32[]{:T(128)S(6)} %select_n.39, s32[]{:T(128)S(6)} %select_n.37), kind=kLoop, calls=%fused_computation.5 | loop fusion | bytes 884748 | tf_op jit(solution)/shard_map/jit(dynamic_index_in_dim)/squeeze | solution.py:151
  31.5 1.3 %collective-permute-start.3 = (bf16[144,512]{1,0:T(8,128)(2,1)}, bf16[144,512]{1,0:T(8,128)(2,1)S(1)}, u32[]{:S(2)}, u32[]{:S(2)}) collective-permute-start(bf16[144,512]{1,0:T(8,128)(2,1)} %get-tuple-element.18), channel_id=1, source_target_pairs={{0,1},{1,2},{2,3},{3,0},{4,5},{5,6},{6,7},{7,4},{8,9},{9,10},{10,1... | collective-permute-start | bytes 442376 | tf_op jit(solution)/shard_map/ppermute | solution.py:20
  32.8 1.4 %collective-permute-start.5 = (bf16[144,512]{1,0:T(8,128)(2,1)}, bf16[144,512]{1,0:T(8,128)(2,1)}, u32[]{:S(2)}, u32[]{:S(2)}) collective-permute-start(bf16[144,512]{1,0:T(8,128)(2,1)} %get-tuple-element.19), channel_id=1, source_target_pairs={{0,3},{1,0},{2,1},{3,2},{4,7},{5,4},{6,5},{7,6},{8,11},{9,8},{10,9... | collective-permute-start | bytes 442376 | tf_op jit(solution)/shard_map/ppermute | solution.py:20
  34.2 1.6 %collective-permute-start.4 = (bf16[144,512]{1,0:T(8,128)(2,1)}, bf16[144,512]{1,0:T(8,128)(2,1)}, u32[]{:S(2)}, u32[]{:S(2)}) collective-permute-start(bf16[144,512]{1,0:T(8,128)(2,1)} %get-tuple-element.20), channel_id=1, source_target_pairs={{0,2},{1,3},{2,0},{3,1},{4,6},{5,7},{6,4},{7,5},{8,10},{9,11},{10,... | collective-permute-start | bytes 442376 | tf_op jit(solution)/shard_map/ppermute | solution.py:20
  35.9 1.1 %collective-permute-done.3 = bf16[144,512]{1,0:T(8,128)(2,1)S(1)} collective-permute-done((bf16[144,512]{1,0:T(8,128)(2,1)}, bf16[144,512]{1,0:T(8,128)(2,1)S(1)}, u32[]{:S(2)}, u32[]{:S(2)}) %collective-permute-start.3) | collective-permute-done | bytes 147488 | tf_op jit(solution)/shard_map/ppermute | solution.py:20
  37.0 0.1 collective-permute-done.5
  37.1 3.0 %collective-permute-done.4 = bf16[144,512]{1,0:T(8,128)(2,1)} collective-permute-done((bf16[144,512]{1,0:T(8,128)(2,1)}, bf16[144,512]{1,0:T(8,128)(2,1)}, u32[]{:S(2)}, u32[]{:S(2)}) %collective-permute-start.4) | collective-permute-done | bytes 147488 | tf_op jit(solution)/shard_map/ppermute | solution.py:20
  40.1 1.1 %fusion.5 = (bf16[144,512]{1,0:T(8,128)(2,1)S(1)}, f32[144,512]{1,0:T(8,128)S(1)}) fusion(bf16[144,512]{1,0:T(8,128)(2,1)} %collective-permute-done.5, bf16[144,512]{1,0:T(8,128)(2,1)} %collective-permute-done.4, bf16[144,512]{1,0:T(8,128)(2,1)S(1)} %collective-permute-done.3, bf16[4,144,512]{2,1,0:T(8,128)(2,1)S(1)} %bitcast.23, s32[]{:T(128)S(6)} %select_n.33), kind=kLoop, calls=%fused_computation.10 | loop fusion | flops 589824 | bytes 1032196 | tf_op jit(solution)/shard_map/convert.3
  41.2 5.3 %collective-permute-start.6 = (bf16[144,128]{1,0:T(8,128)(2,1)S(1)}, bf16[144,128]{1,0:T(8,128)(2,1)S(1)}, u32[]{:S(2)}, u32[]{:S(2)}) collective-permute-start(bf16[144,128]{1,0:T(8,128)(2,1)S(1)} %get-tuple-element.21), channel_id=1, source_target_pairs={{0,252},{4,0},{8,4},{12,8},{16,12},{20,16},{24,20},{28,24},{32,28}... | collective-permute-start | bytes 110600 | tf_op jit(solution)/shard_map/ppermute | solution.py:20
  46.5 1.7 %collective-permute-start.8 = (bf16[144,128]{1,0:T(8,128)(2,1)S(1)}, bf16[144,128]{1,0:T(8,128)(2,1)S(1)}, u32[]{:S(2)}, u32[]{:S(2)}) collective-permute-start(bf16[144,128]{1,0:T(8,128)(2,1)S(1)} %get-tuple-element.22), channel_id=1, source_target_pairs={{0,244},{4,248},{8,252},{12,0},{16,4},{20,8},{24,12},{28,16},{32,2... | collective-permute-start | bytes 110600 | tf_op jit(solution)/shard_map/ppermute | solution.py:20
  48.2 0.8 %collective-permute-start.7 = (bf16[144,128]{1,0:T(8,128)(2,1)S(1)}, bf16[144,128]{1,0:T(8,128)(2,1)S(1)}, u32[]{:S(2)}, u32[]{:S(2)}) collective-permute-start(bf16[144,128]{1,0:T(8,128)(2,1)S(1)} %get-tuple-element.23), channel_id=1, source_target_pairs={{0,248},{4,252},{8,0},{12,4},{16,8},{20,12},{24,16},{28,20},{32,24... | collective-permute-start | bytes 110600 | tf_op jit(solution)/shard_map/ppermute | solution.py:20
  49.0 1.6 %copy-done.7 = bf16[4,512,512]{2,1,0:T(8,128)(2,1)S(1)} copy-done((bf16[4,512,512]{2,1,0:T(8,128)(2,1)S(1)}, bf16[4,512,512]{2,1,0:T(8,128)(2,1)}, u32[]{:S(2)}) %copy-start.7) | copy-done | bytes 2097176
  50.6 4.0 %forward.1 = (bf16[16,128,512]{2,1,0:T(8,128)(2,1)S(1)}, f32[16,576,128]{2,1,0:T(8,128)}) custom-call(bf16[576,128]{1,0:T(8,128)(2,1)S(1)} %collective-permute-done.refs_0_, bf16[576,128]{1,0:T(8,128)(2,1)S(1)} %collective-permute-done.1.refs_1_, bf16[576,128]{1,0:T(8,128)(2,1)S(1)} %collective-permute-done.2.refs_2_, bf16[576,128]{1,0:T(8,128)(2,1)S(1)} %bitcast.29, ...), custom_call_target="tpu_custom_call" | custom-call | flops 2281701376 | bytes 12582912 | tf_op jit(solution)/shard_map/forward/pallas_call | solution.py:161
  54.5 2.5 %copy.9 = bf16[128,16,512]{2,1,0:T(8,128)(2,1)} copy(bf16[128,16,512]{2,0,1:T(8,128)(2,1)S(1)} %bitcast.21) | data formatting | bytes 4194304
  57.0 0.0 collective-permute-done.6
  57.0 0.0 collective-permute-done.8
  57.0 0.0 collective-permute-done.7
  57.0 0.7 %fusion.4 = f32[128,144]{0,1:T(8,128)} fusion(f32[144,512]{1,0:T(8,128)S(1)} %get-tuple-element.17, bf16[144,128]{1,0:T(8,128)(2,1)S(1)} %collective-permute-done.8, bf16[144,128]{1,0:T(8,128)(2,1)S(1)} %collective-permute-done.7, bf16[144,128]{1,0:T(8,128)(2,1)S(1)} %collective-permute-done.6), kind=kLoop, calls=%fused_computation.9 | loop fusion | flops 110592 | bytes 258048 | tf_op jit(solution)/shard_map/transpose | solution.py:179
  (10 shorter events, 0.0 us)
Async XLA Ops:
  0.6 10.0 %collective-permute-start.2 = (bf16[576,128]{1,0:T(8,128)(2,1)}, bf16[576,128]{1,0:T(8,128)(2,1)S(1)}, u32[]{:S(2)}, u32[]{:S(2)}) collective-permute-start(bf16[576,128]{1,0:T(8,128)(2,1)} %bitcast.25), channel_id=1, source_target_pairs={{0,4},{4,8},{8,12},{12,16},{16,20},{20,24},{24,28},{28,32},{32,36}... | collective-permute-start | bytes 442376 | tf_op jit(solution)/shard_map/ppermute | solution.py:20
  3.7 12.1 %collective-permute-start.1 = (bf16[576,128]{1,0:T(8,128)(2,1)}, bf16[576,128]{1,0:T(8,128)(2,1)S(1)}, u32[]{:S(2)}, u32[]{:S(2)}) collective-permute-start(bf16[576,128]{1,0:T(8,128)(2,1)} %bitcast.26), channel_id=1, source_target_pairs={{0,8},{4,12},{8,16},{12,20},{16,24},{20,28},{24,32},{28,36},{32,40... | collective-permute-start | bytes 442376 | tf_op jit(solution)/shard_map/ppermute | solution.py:20
  5.4 12.4 %collective-permute-start = (bf16[576,128]{1,0:T(8,128)(2,1)}, bf16[576,128]{1,0:T(8,128)(2,1)S(1)}, u32[]{:S(2)}, u32[]{:S(2)}) collective-permute-start(bf16[576,128]{1,0:T(8,128)(2,1)} %bitcast.27), channel_id=1, source_target_pairs={{0,12},{4,16},{8,20},{12,24},{16,28},{20,32},{24,36},{28,40},{32,4... | collective-permute-start | bytes 442376 | tf_op jit(solution)/shard_map/ppermute | solution.py:20
  7.1 10.6 %copy-start.1 = (bf16[128,576]{0,1:T(8,128)(2,1)S(1)}, bf16[128,576]{0,1:T(8,128)(2,1)}, u32[]{:S(2)}) copy-start(bf16[128,576]{0,1:T(8,128)(2,1)} %param.6) | copy-start | bytes 442372
  7.1 10.6 %copy-start.2 = (s32[1,4]{1,0:T(1,128)S(1)}, s32[1,4]{1,0:T(1,128)}, u32[]{:S(2)}) copy-start(s32[1,4]{1,0:T(1,128)} %entries_ref.1) | copy-start | bytes 52
  7.1 10.6 %copy-start.3 = (s32[128]{0:T(128)S(1)}, s32[128]{0:T(128)}, u32[]{:S(2)}) copy-start(s32[128]{0:T(128)} %param.8) | copy-start | bytes 1540
  17.7 1.7 %copy-start = (bf16[128,16,576]{0,2,1:T(8,128)(2,1)S(1)}, bf16[128,16,576]{0,2,1:T(8,128)(2,1)}, u32[]{:S(2)}) copy-start(bf16[128,16,576]{0,2,1:T(8,128)(2,1)} %param.5) | copy-start | bytes 7077892
  28.1 1.3 %copy-start.4 = (bf16[4,512,512]{2,1,0:T(8,128)(2,1)}, bf16[4,512,512]{2,1,0:T(8,128)(2,1)S(1)}, u32[]{:S(2)}) copy-start(bf16[4,512,512]{2,1,0:T(8,128)(2,1)S(1)} %get-tuple-element.8.refs_4_) | copy-start | bytes 6291460
  29.4 1.3 %copy-start.6 = (bf16[4,512,512]{2,1,0:T(8,128)(2,1)}, bf16[4,512,512]{2,1,0:T(8,128)(2,1)S(1)}, u32[]{:S(2)}) copy-start(bf16[4,512,512]{2,1,0:T(8,128)(2,1)S(1)} %get-tuple-element.9.refs_5_) | copy-start | bytes 6291460
  30.7 18.2 %copy-start.5 = (bf16[4,512,512]{2,1,0:T(8,128)(2,1)S(1)}, bf16[4,512,512]{2,1,0:T(8,128)(2,1)}, u32[]{:S(2)}) copy-start(bf16[4,512,512]{2,1,0:T(8,128)(2,1)} %copy-done.4) | copy-start | bytes 6291460
  31.5 5.5 %collective-permute-start.3 = (bf16[144,512]{1,0:T(8,128)(2,1)}, bf16[144,512]{1,0:T(8,128)(2,1)S(1)}, u32[]{:S(2)}, u32[]{:S(2)}) collective-permute-start(bf16[144,512]{1,0:T(8,128)(2,1)} %get-tuple-element.18), channel_id=1, source_target_pairs={{0,1},{1,2},{2,3},{3,0},{4,5},{5,6},{6,7},{7,4},{8,9},{9,10},{10,1... | collective-permute-start | bytes 442376 | tf_op jit(solution)/shard_map/ppermute | solution.py:20
  32.8 4.3 %collective-permute-start.5 = (bf16[144,512]{1,0:T(8,128)(2,1)}, bf16[144,512]{1,0:T(8,128)(2,1)}, u32[]{:S(2)}, u32[]{:S(2)}) collective-permute-start(bf16[144,512]{1,0:T(8,128)(2,1)} %get-tuple-element.19), channel_id=1, source_target_pairs={{0,3},{1,0},{2,1},{3,2},{4,7},{5,4},{6,5},{7,6},{8,11},{9,8},{10,9... | collective-permute-start | bytes 442376 | tf_op jit(solution)/shard_map/ppermute | solution.py:20
  34.2 5.9 %collective-permute-start.4 = (bf16[144,512]{1,0:T(8,128)(2,1)}, bf16[144,512]{1,0:T(8,128)(2,1)}, u32[]{:S(2)}, u32[]{:S(2)}) collective-permute-start(bf16[144,512]{1,0:T(8,128)(2,1)} %get-tuple-element.20), channel_id=1, source_target_pairs={{0,2},{1,3},{2,0},{3,1},{4,6},{5,7},{6,4},{7,5},{8,10},{9,11},{10,... | collective-permute-start | bytes 442376 | tf_op jit(solution)/shard_map/ppermute | solution.py:20
  41.2 15.8 %collective-permute-start.6 = (bf16[144,128]{1,0:T(8,128)(2,1)S(1)}, bf16[144,128]{1,0:T(8,128)(2,1)S(1)}, u32[]{:S(2)}, u32[]{:S(2)}) collective-permute-start(bf16[144,128]{1,0:T(8,128)(2,1)S(1)} %get-tuple-element.21), channel_id=1, source_target_pairs={{0,252},{4,0},{8,4},{12,8},{16,12},{20,16},{24,20},{28,24},{32,28}... | collective-permute-start | bytes 110600 | tf_op jit(solution)/shard_map/ppermute | solution.py:20
  46.5 10.5 %collective-permute-start.8 = (bf16[144,128]{1,0:T(8,128)(2,1)S(1)}, bf16[144,128]{1,0:T(8,128)(2,1)S(1)}, u32[]{:S(2)}, u32[]{:S(2)}) collective-permute-start(bf16[144,128]{1,0:T(8,128)(2,1)S(1)} %get-tuple-element.22), channel_id=1, source_target_pairs={{0,244},{4,248},{8,252},{12,0},{16,4},{20,8},{24,12},{28,16},{32,2... | collective-permute-start | bytes 110600 | tf_op jit(solution)/shard_map/ppermute | solution.py:20
  48.2 8.8 %collective-permute-start.7 = (bf16[144,128]{1,0:T(8,128)(2,1)S(1)}, bf16[144,128]{1,0:T(8,128)(2,1)S(1)}, u32[]{:S(2)}, u32[]{:S(2)}) collective-permute-start(bf16[144,128]{1,0:T(8,128)(2,1)S(1)} %get-tuple-element.23), channel_id=1, source_target_pairs={{0,248},{4,252},{8,0},{12,4},{16,8},{20,12},{24,16},{28,20},{32,24... | collective-permute-start | bytes 110600 | tf_op jit(solution)/shard_map/ppermute | solution.py:20
  49.0 1.6 %copy-start.7 = (bf16[4,512,512]{2,1,0:T(8,128)(2,1)S(1)}, bf16[4,512,512]{2,1,0:T(8,128)(2,1)}, u32[]{:S(2)}) copy-start(bf16[4,512,512]{2,1,0:T(8,128)(2,1)} %copy-done.6) | copy-start | bytes 6291460

commit v2 on v1

v2 whole, which is shorter than its diff:
```python
import functools
import math

import jax
import jax.numpy as jnp
from jax import lax
from jax.experimental import pallas as pl
from jax.experimental.pallas import tpu as pltpu
from jax.sharding import PartitionSpec as P

F32 = jnp.float32
BF16 = jnp.bfloat16
SLOTS = 4
GROUP = 8
PART = 4
MIB = 1 << 20
NN = (((1,), (0,)), ((), ()))
NT = (((1,), (1,)), ((), ()))


def moved(value, axis, target):
    count = lax.axis_size(axis)
    return lax.ppermute(value, axis, [(s, target(s) % count) for s in range(count)])


def dot(a, b, dims=NN):
    return lax.dot_general(a, b, dims, preferred_element_type=F32)


def lanes(ref, first, count):
    return jnp.concatenate([ref[first + n] for n in range(count)], axis=1)


def fetch_kernel(q_ref, after_ref, out_ref, sems):
    del after_ref
    chunks = sems.shape[0]
    size = q_ref.shape[0] // chunks
    copies = [
        pltpu.make_async_copy(
            q_ref.at[pl.ds(n * size, size)], out_ref.at[pl.ds(n * size, size)], sems.at[n]
        )
        for n in range(chunks)
    ]
    for copy in copies:
        copy.start()
    for copy in copies:
        copy.wait()


def backward_kernel(scale, parts, place_ref, entries_ref, start_ref, *refs):
    key_refs = refs[:SLOTS]
    q_ref, g_ref, weight_ref, score_ref = refs[SLOTS : SLOTS + 4]
    piece_refs = refs[SLOTS + 4 : SLOTS + 4 + parts]
    rows_ref, bias_ref, acc_ref = refs[SLOTS + 4 + parts :]
    width, block = key_refs[0].shape
    heads, latent_width, _ = g_ref.shape
    place = place_ref[0]
    head = place_ref[1]

    parity = lax.rem(place, 2)
    offsets = (1 + 2 * parity, 3 - 2 * parity, 2, 0)
    q_pos = place * block + lax.broadcasted_iota(jnp.int32, (block, block), 1)
    q_start = start_ref[...]
    for slot in range(SLOTS):
        span = slice(slot * block, (slot + 1) * block)
        rows_ref[span, :] = key_refs[slot][...].T
        entry = place - offsets[slot]
        listed = entries_ref[0, 0] == entry
        for n in range(1, entries_ref.shape[1]):
            listed = listed | (entries_ref[0, n] == entry)
        listed = listed & (entry >= 0)
        first = jnp.where(listed, entry * block, 1 << 24)
        k_pos = first + lax.broadcasted_iota(jnp.int32, (block, block), 0)
        allowed = (k_pos <= q_pos) & (k_pos >= q_start)
        bias_ref[span, :] = jnp.where(allowed, 0.0, -1e30)

    bias = jnp.concatenate([bias_ref[...]] * GROUP, axis=1)
    for group in range(heads // GROUP):
        q_cols = lanes(q_ref, group * GROUP, GROUP)
        g_cols = lanes(g_ref, group * GROUP, GROUP)
        score = dot(rows_ref[...], q_cols) * (scale * math.log2(math.e)) + bias
        grad_weight = dot(rows_ref[:, :latent_width], g_cols)
        top = jnp.max(score, axis=0, keepdims=True)
        terms = jnp.exp2(score - top)
        weight = terms * (1.0 / jnp.sum(terms, axis=0, keepdims=True))
        delta = jnp.sum(weight * grad_weight, axis=0, keepdims=True)
        grad_score = ((weight * scale) * (grad_weight - delta)).astype(BF16)
        weight = weight.astype(BF16)
        size = PART * block
        for n in range(GROUP // PART):
            weight_ref[group * (GROUP // PART) + n] = weight[:, n * size : (n + 1) * size]
            score_ref[group * (GROUP // PART) + n] = grad_score[:, n * size : (n + 1) * size]
        from_score = dot(q_cols, grad_score, NT)
        from_weight = dot(g_cols, weight, NT)
        if group == 0:
            acc_ref[...] = from_score
        else:
            acc_ref[...] += from_score
        acc_ref[:latent_width, :] += from_weight

    share = width // parts
    for n, piece_ref in enumerate(piece_refs):
        first = pl.multiple_of(lax.rem(head + n, parts) * share, share)
        piece_ref[...] = acc_ref[pl.ds(first, share), :].astype(BF16)


def forward_kernel(*refs):
    key_refs = refs[:SLOTS]
    weight_ref, score_ref, att_ref, gq_ref, cols_ref, rows_ref = refs[SLOTS:]
    block = key_refs[0].shape[1]
    latent_width = att_ref.shape[2]
    step = pl.program_id(0)

    @pl.when(step == 0)
    def _():
        for slot, key_ref in enumerate(key_refs):
            cols_ref[:, slot * block : (slot + 1) * block] = key_ref[...]
            rows_ref[slot * block : (slot + 1) * block, :] = key_ref[:latent_width, :].T

    grad = dot(cols_ref[...], score_ref[step])
    for n in range(PART):
        gq_ref[n] = grad[:, n * block : (n + 1) * block]
    att = dot(weight_ref[step].T, rows_ref[...])
    for n in range(PART):
        att_ref[n] = att[n * block : (n + 1) * block, :].astype(BF16)


def merge_kernel(*refs):
    pieces = refs[:-5]
    swap_ref, cross_ref, back_ref, own_ref = refs[-4:]
    total = pieces[0][...].astype(F32)
    for piece in pieces[1:]:
        total = total + piece[...].astype(F32)
    block = own_ref.shape[1]
    swap_ref[...] = total[:, :block].astype(BF16)
    cross_ref[...] = total[:, block : 2 * block].astype(BF16)
    back_ref[...] = total[:, 2 * block : 3 * block]
    own_ref[...] = total[:, 3 * block :]


def add_kernel(*refs):
    total = refs[0][...]
    for ref in refs[1:-1]:
        total = total + ref[...].astype(F32)
    refs[-1][...] = total.astype(refs[-1].dtype)


def shards(queries, latent, grad_out, doc_start, block_list):
    block, heads, width = queries.shape
    latent_width = grad_out.shape[2]
    scale = 1.0 / math.sqrt(latent_width // 4 + width - latent_width)
    parts = lax.axis_size("head")
    share = width // parts
    keys = SLOTS * block
    steps = heads // PART
    rows = PART * block
    place = jnp.stack([lax.axis_index("ctx"), lax.axis_index("head")]).astype(jnp.int32)
    vmem = pl.BlockSpec(memory_space=pltpu.VMEM)
    smem = pl.BlockSpec(memory_space=pltpu.SMEM)
    anywhere = pl.BlockSpec(memory_space=pl.ANY)
    keep = lambda x: pltpu.with_memory_space_constraint(x, pltpu.VMEM)
    limit = lambda n: pltpu.CompilerParams(vmem_limit_bytes=n * MIB)

    latent_t = latent.T
    crossed = moved(latent_t, "ctx", lambda s: s + 3 if s % 2 else s + 1)
    back = moved(latent_t, "ctx", lambda s: s + 2)
    g_t = grad_out.transpose(1, 2, 0)
    back, g_t = lax.optimization_barrier((back, g_t))
    swapped = moved(back, "ctx", lambda s: s ^ 1)
    window = [swapped, crossed, back, latent_t]

    q_t = pl.pallas_call(
        fetch_kernel,
        in_specs=[anywhere, anywhere],
        out_specs=vmem,
        out_shape=pltpu.VMEM((heads, width, block), BF16),
        scratch_shapes=[pltpu.SemaphoreType.DMA((8,))],
        compiler_params=limit(1),
        name="fetch",
    )(pltpu.with_memory_space_constraint(queries.transpose(1, 2, 0), pltpu.HBM), g_t)

    weight, grad_score, *pieces = pl.pallas_call(
        functools.partial(backward_kernel, scale, parts),
        in_specs=[smem, smem] + [vmem] * (SLOTS + 3),
        out_specs=[vmem] * (2 + parts),
        out_shape=[pltpu.VMEM((steps, keys, rows), BF16)] * 2
        + [jax.ShapeDtypeStruct((share, keys), BF16)] * parts,
        scratch_shapes=[
            pltpu.VMEM((keys, width), BF16),
            pltpu.VMEM((keys, block), F32),
            pltpu.VMEM((width, keys), F32),
        ],
        compiler_params=limit(20),
        cost_estimate=pl.CostEstimate(
            flops=2 * heads * block * keys * 2 * (width + latent_width),
            bytes_accessed=12 * MIB,
            transcendentals=heads * block * keys,
        ),
        name="backward",
    )(place, block_list, doc_start.reshape(1, block), *window, keep(q_t), g_t)

    arrived = [
        moved(piece, "head", lambda s, n=n: s + n) for n, piece in enumerate(pieces) if n
    ]

    by_group = lambda *tail: pl.BlockSpec((PART, *tail), lambda i: (i,) + (0,) * len(tail))
    att, gq = pl.pallas_call(
        forward_kernel,
        grid=(steps,),
        in_specs=[vmem] * (SLOTS + 2),
        out_specs=[by_group(block, latent_width), by_group(width, block)],
        out_shape=[
            jax.ShapeDtypeStruct((heads, block, latent_width), BF16),
            jax.ShapeDtypeStruct((heads, width, block), F32),
        ],
        scratch_shapes=[pltpu.VMEM((width, keys), BF16), pltpu.VMEM((keys, latent_width), BF16)],
        compiler_params=limit(20),
        cost_estimate=pl.CostEstimate(
            flops=2 * heads * block * keys * (width + latent_width),
            bytes_accessed=12 * MIB,
            transcendentals=0,
        ),
        name="forward",
    )(*window, keep(weight), keep(grad_score))

    to_swap, to_cross, to_back, own = pl.pallas_call(
        merge_kernel,
        in_specs=[vmem] * parts + [anywhere],
        out_specs=[vmem] * 4,
        out_shape=[jax.ShapeDtypeStruct((share, block), t) for t in (BF16, BF16, F32, F32)],
        compiler_params=limit(4),
        name="merge",
    )(pieces[0], *arrived, att)
    from_swap = moved(to_swap, "ctx", lambda s: s ^ 1)
    from_cross = moved(to_cross, "ctx", lambda s: s - 1 if s % 2 else s - 3)
    to_back = pl.pallas_call(
        add_kernel,
        in_specs=[vmem] * 2,
        out_specs=vmem,
        out_shape=jax.ShapeDtypeStruct((share, block), BF16),
        compiler_params=limit(1),
        name="add",
    )(to_back, from_swap)
    from_back = moved(to_back, "ctx", lambda s: s - 2)
    total = pl.pallas_call(
        add_kernel,
        in_specs=[vmem] * 3,
        out_specs=vmem,
        out_shape=jax.ShapeDtypeStruct((share, block), F32),
        compiler_params=limit(1),
        name="total",
    )(own, from_cross, from_back)
    return (att.transpose(1, 0, 2), gq.transpose(2, 0, 1), total.T)


def solution(mesh):
    placed = (
        P("ctx", "head", None),
        P("ctx", None),
        P("ctx", "head", None),
        P("ctx"),
        P("ctx", None),
    )
    return jax.shard_map(
        shards,
        mesh=mesh,
        in_specs=placed,
        out_specs=(P("ctx", "head", None), P("ctx", "head", None), P("ctx", "head")),
        check_vma=False,
    )
```

time: 57.9 us -> 43.2 us (0.75)
  local copies, waits for them, and re-layouts: 12.7 us -> 5.96 us
  waiting for transfers between devices: 11.3 us -> 4.88 us
  other arithmetic: 1.71 us -> 0.07 us
  starting transfers between devices: 18.6 us -> 17.8 us
  Pallas kernels: 12.7 us -> 13.3 us
    ppermute x9, waiting for transfers between devices: 11.3 us -> 4.88 us  [moved(): lax.ppermute(value, axis, [(s, target(s) % count) for s in range(count)])]
    unnamed x18 -> x8, local copies, waits for them, and re-layouts: 11.9 us -> 5.96 us
    another operation x1, other arithmetic: 1.06 us -> 0.07 us  [shards(): jnp.stack([lax.axis_index('ctx'), lax.axis_index('head')]).astype(jnp.int32)]
    ppermute x9, starting transfers between devices: 18.6 us -> 17.8 us  [moved(): lax.ppermute(value, axis, [(s, target(s) % count) for s in range(count)])]
    squeeze x1 -> x0, local copies, waits for them, and re-layouts: 0.77 us -> none  [shards(): lax.dynamic_index_in_dim(pieces, (head + n) % parts, 0, keepdims=False)]
    transpose x1 -> x0, other arithmetic: 0.65 us -> none  [shards(): return (att.transpose(1, 0, 2), gq.transpose(2, 0, 1), total.T)]
    pallas_call x2 -> x6, Pallas kernels: 12.7 us -> 13.3 us  [the longest x1 6.89 us: shards(): pl.pallas_call(functools.partial(backward_kernel, scale, parts), in_specs...]
  transfers between devices with their start and end apart: 9 -> 9, of which waited for: 5 -> 3; matrix products, arithmetic and copies ran while one was open for 10% -> 14% of each run, Pallas kernels for 7% -> 13%
where the time goes in v2:
time: 43.2 us; the launch traced here: 42.7 us
  starting transfers between devices  17.8 us (41%)
  Pallas kernels  13.3 us (31%)
  local copies, waits for them, and re-layouts  5.96 us (14%)
  waiting for transfers between devices  4.88 us (11%)
  between operations  0.71 us (2%)
    ppermute x9, starting transfers between devices, moved(): lax.ppermute(value, axis, [(s, target(s) % count) for s in range(count)])  17.8 us
    pallas_call x1, Pallas kernels, shards(): pl.pallas_call(functools.partial(backward_kernel, scale, parts), in_specs...  6.89 us
    unnamed x8, local copies, waits for them, and re-layouts  5.96 us
    ppermute x9, waiting for transfers between devices, moved(): lax.ppermute(value, axis, [(s, target(s) % count) for s in range(count)])  4.88 us
    pallas_call x1, Pallas kernels, shards(): pl.pallas_call(forward_kernel, grid=(steps,), in_specs=[vmem] * (SLOTS +...  3.98 us
    pallas_call x1, Pallas kernels, shards(): pl.pallas_call(fetch_kernel, in_specs=[anywhere, anywhere], out_specs=vme...  1.69 us
  transfers between devices with their start and end apart: 9, of which 3 were waited for; matrix products, arithmetic and copies ran while one was open for 14% of the time, Pallas kernels for 13%

profile of v2, /device:TPU:1, one launch (start us, length us, event | category | flops | bytes accessed | tf_op | source)
XLA Modules:
  0.0 42.7 jit_solution(1071770661501350517)
XLA Ops:
  0.6 2.5 %collective-permute-start = (bf16[576,128]{1,0:T(8,128)(2,1)}, bf16[576,128]{1,0:T(8,128)(2,1)S(1)}, u32[]{:S(2)}, u32[]{:S(2)}) collective-permute-start(bf16[576,128]{1,0:T(8,128)(2,1)} %bitcast.12), channel_id=1, source_target_pairs={{0,8},{4,12},{8,16},{12,20},{16,24},{20,28},{24,32},{28,36},{32,40... | collective-permute-start | bytes 442376 | tf_op jit(solution)/shard_map/ppermute | solution.py:23
  3.2 3.8 %collective-permute-start.2 = (bf16[576,128]{1,0:T(8,128)(2,1)}, bf16[576,128]{1,0:T(8,128)(2,1)S(1)}, u32[]{:S(2)}, u32[]{:S(2)}) collective-permute-start(bf16[576,128]{1,0:T(8,128)(2,1)} %bitcast.13), channel_id=1, source_target_pairs={{0,4},{4,16},{8,12},{12,24},{16,20},{20,32},{24,28},{28,40},{32,36... | collective-permute-start | bytes 442376 | tf_op jit(solution)/shard_map/ppermute | solution.py:23
  7.0 3.5 %copy.8 = bf16[128,16,512]{0,2,1:T(8,128)(2,1)S(1)} copy(bf16[128,16,512]{2,1,0:T(8,128)(2,1)} %param.7) | data formatting | bytes 4194304 | tf_op args[2]
  10.5 2.6 %collective-permute-done.refs_2_ = bf16[576,128]{1,0:T(8,128)(2,1)S(1)} collective-permute-done((bf16[576,128]{1,0:T(8,128)(2,1)}, bf16[576,128]{1,0:T(8,128)(2,1)S(1)}, u32[]{:S(2)}, u32[]{:S(2)}) %collective-permute-start) | collective-permute-done | bytes 147488 | tf_op jit(solution)/shard_map/ppermute | solution.py:23
  13.1 2.5 %collective-permute-start.1 = (bf16[576,128]{1,0:T(8,128)(2,1)S(1)}, bf16[576,128]{1,0:T(8,128)(2,1)S(1)}, u32[]{:S(2)}, u32[]{:S(2)}) collective-permute-start(bf16[576,128]{1,0:T(8,128)(2,1)S(1)} %collective-permute-done.refs_2_), channel_id=1, source_target_pairs={{0,4},{4,0},{8,12},{12,8},{16,20},{20,16},{24,28},{28,24},{32,36},... | collective-permute-start | bytes 442376 | tf_op jit(solution)/shard_map/ppermute | solution.py:23
  15.6 0.1 pad_add_fusion.place_ref
  15.7 0.0 copy-start
  15.7 0.0 copy-start.1
  15.7 0.0 copy-start.2
  15.7 1.7 %fetch.1.refs_4_ = bf16[16,576,128]{2,1,0:T(8,128)(2,1)S(1)} custom-call(bf16[16,576,128]{2,1,0:T(8,128)(2,1)} %bitcast.17, bf16[16,512,128]{2,1,0:T(8,128)(2,1)S(1)} %bitcast.10), custom_call_target="tpu_custom_call" | custom-call | tf_op jit(solution)/shard_map/fetch/pallas_call | solution.py:172
  17.4 0.0 collective-permute-done.2.refs_1_
  17.4 0.0 collective-permute-done.1.refs_0_
  17.4 0.0 copy-done
  17.4 0.0 copy-done.1
  17.4 0.0 copy-done.2
  17.5 6.9 %backward.1 = (bf16[4,512,512]{2,1,0:T(8,128)(2,1)S(1)}, bf16[4,512,512]{2,1,0:T(8,128)(2,1)S(1)}, bf16[144,512]{1,0:T(8,128)(2,1)S(1)}, bf16[144,512]{1,0:T(8,1...) custom-call(s32[2]{0:T(128)S(1)} %pad_add_fusion.place_ref, s32[1,4]{1,0:T(1,128)S(1)} %copy-done.1, ...), custom_call_target="tpu_custom_call" | custom-call | flops 4563402752 | bytes 12582912 | tf_op jit(solution)/shard_map/backward/pallas_call | solution.py:182
  24.4 1.4 %collective-permute-start.3 = (bf16[144,512]{1,0:T(8,128)(2,1)S(1)}, bf16[144,512]{1,0:T(8,128)(2,1)S(1)}, u32[]{:S(2)}, u32[]{:S(2)}) collective-permute-start(bf16[144,512]{1,0:T(8,128)(2,1)S(1)} %get-tuple-element.24), channel_id=1, source_target_pairs={{0,1},{1,2},{2,3},{3,0},{4,5},{5,6},{6,7},{7,4},{8,9},{9,10},{10,1... | collective-permute-start | bytes 442376 | tf_op jit(solution)/shard_map/ppermute | solution.py:23
  25.7 2.6 %collective-permute-start.4 = (bf16[144,512]{1,0:T(8,128)(2,1)S(1)}, bf16[144,512]{1,0:T(8,128)(2,1)S(1)}, u32[]{:S(2)}, u32[]{:S(2)}) collective-permute-start(bf16[144,512]{1,0:T(8,128)(2,1)S(1)} %get-tuple-element.25), channel_id=1, source_target_pairs={{0,2},{1,3},{2,0},{3,1},{4,6},{5,7},{6,4},{7,5},{8,10},{9,11},{10,... | collective-permute-start | bytes 442376 | tf_op jit(solution)/shard_map/ppermute | solution.py:23
  28.4 1.1 %collective-permute-start.5 = (bf16[144,512]{1,0:T(8,128)(2,1)S(1)}, bf16[144,512]{1,0:T(8,128)(2,1)S(1)}, u32[]{:S(2)}, u32[]{:S(2)}) collective-permute-start(bf16[144,512]{1,0:T(8,128)(2,1)S(1)} %get-tuple-element.26), channel_id=1, source_target_pairs={{0,3},{1,0},{2,1},{3,2},{4,7},{5,4},{6,5},{7,6},{8,11},{9,8},{10,9... | collective-permute-start | bytes 442376 | tf_op jit(solution)/shard_map/ppermute | solution.py:23
  29.4 4.0 %forward.1 = (bf16[16,128,512]{2,1,0:T(8,128)(2,1)S(1)}, f32[16,576,128]{2,1,0:T(8,128)}) custom-call(bf16[576,128]{1,0:T(8,128)(2,1)S(1)} %collective-permute-done.1.refs_0_, bf16[576,128]{1,0:T(8,128)(2,1)S(1)} %collective-permute-done.2.refs_1_, bf16[576,128]{1,0:T(8,128)(2,1)S(1)} %collective-permute-done.refs_2_, bf16[576,128]{1,0:T(8,128)(2,1)S(1)} %bitcast.15, ...), custom_call_target="tpu_custom_call" | custom-call | flops 2281701376 | bytes 12582912 | tf_op jit(solution)/shard_map/forward/pallas_call | solution.py:207
  33.4 0.0 collective-permute-done.3.refs_1_
  33.4 1.5 %collective-permute-done.4.refs_2_ = bf16[144,512]{1,0:T(8,128)(2,1)S(1)} collective-permute-done((bf16[144,512]{1,0:T(8,128)(2,1)S(1)}, bf16[144,512]{1,0:T(8,128)(2,1)S(1)}, u32[]{:S(2)}, u32[]{:S(2)}) %collective-permute-start.4) | collective-permute-done | bytes 147488 | tf_op jit(solution)/shard_map/ppermute | solution.py:23
  34.9 0.0 collective-permute-done.5.refs_3_
  34.9 0.1 merge.1
  34.9 1.5 %collective-permute-start.7 = (bf16[144,128]{1,0:T(8,128)(2,1)S(1)}, bf16[144,128]{1,0:T(8,128)(2,1)S(1)}, u32[]{:S(2)}, u32[]{:S(2)}) collective-permute-start(bf16[144,128]{1,0:T(8,128)(2,1)S(1)} %get-tuple-element.30), channel_id=1, source_target_pairs={{0,4},{4,0},{8,12},{12,8},{16,20},{20,16},{24,28},{28,24},{32,36},... | collective-permute-start | bytes 110600 | tf_op jit(solution)/shard_map/ppermute | solution.py:23
  36.5 0.1 collective-permute-start.6
  36.6 0.8 %collective-permute-done.7.refs_1_ = bf16[144,128]{1,0:T(8,128)(2,1)S(1)} collective-permute-done((bf16[144,128]{1,0:T(8,128)(2,1)S(1)}, bf16[144,128]{1,0:T(8,128)(2,1)S(1)}, u32[]{:S(2)}, u32[]{:S(2)}) %collective-permute-start.7) | collective-permute-done | bytes 36896 | tf_op jit(solution)/shard_map/ppermute | solution.py:23
  37.4 2.2 %collective-permute-start.8 = (bf16[144,128]{1,0:T(8,128)(2,1)S(1)}, bf16[144,128]{1,0:T(8,128)(2,1)S(1)}, u32[]{:S(2)}, u32[]{:S(2)}) collective-permute-start(bf16[144,128]{1,0:T(8,128)(2,1)S(1)} %add.3), channel_id=1, source_target_pairs={{0,248},{4,252},{8,0},{12,4},{16,8},{20,12},{24,16},{28,20},{32,24... | collective-permute-start | bytes 110600 | tf_op jit(solution)/shard_map/ppermute | solution.py:23
  39.6 2.5 %copy.9 = bf16[128,16,512]{2,1,0:T(8,128)(2,1)} copy(bf16[128,16,512]{2,0,1:T(8,128)(2,1)S(1)} %bitcast.9) | data formatting | bytes 4194304
  42.1 0.0 collective-permute-done.6.refs_1_
  42.1 0.0 collective-permute-done.8.refs_2_
  42.1 0.6 %total.1 = f32[144,128]{1,0:T(8,128)} custom-call(f32[144,128]{1,0:T(8,128)S(1)} %get-tuple-element.27.refs_0_, bf16[144,128]{1,0:T(8,128)(2,1)S(1)} %collective-permute-done.6.refs_1_, bf16[144,128]{1,0:T(8,128)(2,1)S(1)} %collective-permute-done.8.refs_2_), custom_call_target="tpu_custom_call" | custom-call | tf_op jit(solution)/shard_map/total/pallas_call | solution.py:245
  (1 shorter events, 0.0 us)
Async XLA Ops:
  0.6 12.5 %collective-permute-start = (bf16[576,128]{1,0:T(8,128)(2,1)}, bf16[576,128]{1,0:T(8,128)(2,1)S(1)}, u32[]{:S(2)}, u32[]{:S(2)}) collective-permute-start(bf16[576,128]{1,0:T(8,128)(2,1)} %bitcast.12), channel_id=1, source_target_pairs={{0,8},{4,12},{8,16},{12,20},{16,24},{20,28},{24,32},{28,36},{32,40... | collective-permute-start | bytes 442376 | tf_op jit(solution)/shard_map/ppermute | solution.py:23
  3.2 14.2 %collective-permute-start.2 = (bf16[576,128]{1,0:T(8,128)(2,1)}, bf16[576,128]{1,0:T(8,128)(2,1)S(1)}, u32[]{:S(2)}, u32[]{:S(2)}) collective-permute-start(bf16[576,128]{1,0:T(8,128)(2,1)} %bitcast.13), channel_id=1, source_target_pairs={{0,4},{4,16},{8,12},{12,24},{16,20},{20,32},{24,28},{28,40},{32,36... | collective-permute-start | bytes 442376 | tf_op jit(solution)/shard_map/ppermute | solution.py:23
  13.1 4.3 %collective-permute-start.1 = (bf16[576,128]{1,0:T(8,128)(2,1)S(1)}, bf16[576,128]{1,0:T(8,128)(2,1)S(1)}, u32[]{:S(2)}, u32[]{:S(2)}) collective-permute-start(bf16[576,128]{1,0:T(8,128)(2,1)S(1)} %collective-permute-done.refs_2_), channel_id=1, source_target_pairs={{0,4},{4,0},{8,12},{12,8},{16,20},{20,16},{24,28},{28,24},{32,36},... | collective-permute-start | bytes 442376 | tf_op jit(solution)/shard_map/ppermute | solution.py:23
  15.7 1.7 %copy-start = (bf16[128,576]{0,1:T(8,128)(2,1)S(1)}, bf16[128,576]{0,1:T(8,128)(2,1)}, u32[]{:S(2)}) copy-start(bf16[128,576]{0,1:T(8,128)(2,1)} %param.6) | copy-start | bytes 442372
  15.7 1.7 %copy-start.1 = (s32[1,4]{1,0:T(1,128)S(1)}, s32[1,4]{1,0:T(1,128)}, u32[]{:S(2)}) copy-start(s32[1,4]{1,0:T(1,128)} %entries_ref.1) | copy-start | bytes 52
  15.7 1.7 %copy-start.2 = (s32[128]{0:T(128)S(1)}, s32[128]{0:T(128)}, u32[]{:S(2)}) copy-start(s32[128]{0:T(128)} %param.8) | copy-start | bytes 1540
  24.4 9.0 %collective-permute-start.3 = (bf16[144,512]{1,0:T(8,128)(2,1)S(1)}, bf16[144,512]{1,0:T(8,128)(2,1)S(1)}, u32[]{:S(2)}, u32[]{:S(2)}) collective-permute-start(bf16[144,512]{1,0:T(8,128)(2,1)S(1)} %get-tuple-element.24), channel_id=1, source_target_pairs={{0,1},{1,2},{2,3},{3,0},{4,5},{5,6},{6,7},{7,4},{8,9},{9,10},{10,1... | collective-permute-start | bytes 442376 | tf_op jit(solution)/shard_map/ppermute | solution.py:23
  25.7 9.1 %collective-permute-start.4 = (bf16[144,512]{1,0:T(8,128)(2,1)S(1)}, bf16[144,512]{1,0:T(8,128)(2,1)S(1)}, u32[]{:S(2)}, u32[]{:S(2)}) collective-permute-start(bf16[144,512]{1,0:T(8,128)(2,1)S(1)} %get-tuple-element.25), channel_id=1, source_target_pairs={{0,2},{1,3},{2,0},{3,1},{4,6},{5,7},{6,4},{7,5},{8,10},{9,11},{10,... | collective-permute-start | bytes 442376 | tf_op jit(solution)/shard_map/ppermute | solution.py:23
  28.4 6.5 %collective-permute-start.5 = (bf16[144,512]{1,0:T(8,128)(2,1)S(1)}, bf16[144,512]{1,0:T(8,128)(2,1)S(1)}, u32[]{:S(2)}, u32[]{:S(2)}) collective-permute-start(bf16[144,512]{1,0:T(8,128)(2,1)S(1)} %get-tuple-element.26), channel_id=1, source_target_pairs={{0,3},{1,0},{2,1},{3,2},{4,7},{5,4},{6,5},{7,6},{8,11},{9,8},{10,9... | collective-permute-start | bytes 442376 | tf_op jit(solution)/shard_map/ppermute | solution.py:23
  34.9 2.4 %collective-permute-start.7 = (bf16[144,128]{1,0:T(8,128)(2,1)S(1)}, bf16[144,128]{1,0:T(8,128)(2,1)S(1)}, u32[]{:S(2)}, u32[]{:S(2)}) collective-permute-start(bf16[144,128]{1,0:T(8,128)(2,1)S(1)} %get-tuple-element.30), channel_id=1, source_target_pairs={{0,4},{4,0},{8,12},{12,8},{16,20},{20,16},{24,28},{28,24},{32,36},... | collective-permute-start | bytes 110600 | tf_op jit(solution)/shard_map/ppermute | solution.py:23
  36.5 5.6 %collective-permute-start.6 = (bf16[144,128]{1,0:T(8,128)(2,1)S(1)}, bf16[144,128]{1,0:T(8,128)(2,1)S(1)}, u32[]{:S(2)}, u32[]{:S(2)}) collective-permute-start(bf16[144,128]{1,0:T(8,128)(2,1)S(1)} %get-tuple-element.28), channel_id=1, source_target_pairs={{0,244},{4,0},{8,252},{12,8},{16,4},{20,16},{24,12},{28,24},{32,20... | collective-permute-start | bytes 110600 | tf_op jit(solution)/shard_map/ppermute | solution.py:23
  37.4 4.7 %collective-permute-start.8 = (bf16[144,128]{1,0:T(8,128)(2,1)S(1)}, bf16[144,128]{1,0:T(8,128)(2,1)S(1)}, u32[]{:S(2)}, u32[]{:S(2)}) collective-permute-start(bf16[144,128]{1,0:T(8,128)(2,1)S(1)} %add.3), channel_id=1, source_target_pairs={{0,248},{4,252},{8,0},{12,4},{16,8},{20,12},{24,16},{28,20},{32,24... | collective-permute-start | bytes 110600 | tf_op jit(solution)/shard_map/ppermute | solution.py:23

commit v3 on v2

v3 whole, which is shorter than its diff:
```python
import functools
import math

import jax
import jax.numpy as jnp
from jax import lax
from jax.experimental import pallas as pl
from jax.experimental.pallas import tpu as pltpu
from jax.sharding import PartitionSpec as P

F32 = jnp.float32
BF16 = jnp.bfloat16
SLOTS = 4
PART = 4
MIB = 1 << 20
NN = (((1,), (0,)), ((), ()))
NT = (((1,), (1,)), ((), ()))


def moved(value, axis, target):
    count = lax.axis_size(axis)
    return lax.ppermute(value, axis, [(s, target(s) % count) for s in range(count)])


def dot(a, b, dims=NN):
    return lax.dot_general(a, b, dims, preferred_element_type=F32)


def lanes(ref):
    return jnp.concatenate([ref[n] for n in range(ref.shape[0])], axis=1)


def mask_kernel(entries_ref, start_ref, mask_ref, token_ref):
    place = lax.axis_index("ctx")
    parity = lax.rem(place, 2)
    block = start_ref.shape[1]
    q_pos = place * block + lax.broadcasted_iota(jnp.int32, (block, block), 1)
    for slot, offset in enumerate((1 + 2 * parity, 3 - 2 * parity, 2, 0)):
        entry = place - offset
        listed = entries_ref[0, 0] == entry
        for n in range(1, entries_ref.shape[1]):
            listed = listed | (entries_ref[0, n] == entry)
        first = jnp.where(listed & (entry >= 0), entry * block, 1 << 24)
        k_pos = first + lax.broadcasted_iota(jnp.int32, (block, block), 0)
        allowed = (k_pos <= q_pos) & (k_pos >= start_ref[...])
        mask_ref[slot * block : (slot + 1) * block, :] = jnp.where(allowed, 0.0, -1e30)
    token_ref[...] = jnp.zeros_like(token_ref)


def scores_of(scale, keys, mask, q_cols, g_cols):
    heads = q_cols.shape[1] // mask.shape[1]
    mask = jnp.concatenate([mask] * heads, axis=1)
    score = dot(keys, q_cols) * (scale * math.log2(math.e)) + mask
    return score, dot(keys[:, : g_cols.shape[0]], g_cols)


def own_kernel(
    scale, mask_ref, key_ref, g_ref, from_ref, _, score_ref, grad_ref, q_ref, token_ref, sems
):
    chunks = sems.shape[0]
    size = from_ref.shape[0] // chunks
    copies = [
        pltpu.make_async_copy(
            from_ref.at[pl.ds(n * size, size)], q_ref.at[pl.ds(n * size, size)], sems.at[n]
        )
        for n in range(chunks)
    ]
    for copy in copies:
        copy.start()
    keys = key_ref[...].T
    first = mask_ref.shape[0] - keys.shape[0]
    mask = mask_ref[first:, :]
    span = size * mask.shape[1]
    for n, copy in enumerate(copies):
        copy.wait()
        heads = slice(n * size, (n + 1) * size)
        score, grad_weight = scores_of(scale, keys, mask, lanes(q_ref[heads]), lanes(g_ref[heads]))
        score_ref[:, n * span : (n + 1) * span] = score
        grad_ref[:, n * span : (n + 1) * span] = grad_weight
    token_ref[...] = jnp.zeros_like(token_ref)


def back_kernel(scale, mask_ref, key_ref, g_ref, q_ref, _, score_ref, grad_ref):
    block = key_ref.shape[1]
    mask = mask_ref[2 * block : 3 * block, :]
    score, grad_weight = scores_of(scale, key_ref[...].T, mask, lanes(q_ref), lanes(g_ref))
    score_ref[...] = score
    grad_ref[...] = grad_weight


def weights_kernel(scale, mask_ref, *refs):
    swap_ref, cross_ref, q_ref, g_ref, *known, weight_ref, score_ref, out_ref, grad_ref = refs
    keys = jnp.concatenate([swap_ref[...].T, cross_ref[...].T], axis=0)
    mask = mask_ref[: keys.shape[0], :]
    q_cols = lanes(q_ref)
    g_cols = lanes(g_ref)
    parts = [scores_of(scale, keys, mask, q_cols, g_cols)]
    parts += [(known[n][...], known[n + 1][...]) for n in range(0, len(known), 2)]
    top = functools.reduce(jnp.maximum, [jnp.max(s, axis=0, keepdims=True) for s, _ in parts])
    terms = [jnp.exp2(s - top) for s, _ in parts]
    total = sum(jnp.sum(t, axis=0, keepdims=True) for t in terms)
    inverse = 1.0 / total
    delta = inverse * sum(
        jnp.sum(t * g, axis=0, keepdims=True) for t, (_, g) in zip(terms, parts, strict=True)
    )
    size = weight_ref.shape[2]
    first = 0
    for t, (_, grad_weight) in zip(terms, parts, strict=True):
        weight = t * inverse
        grad_score = (weight * (grad_weight - delta)).astype(BF16)
        weight = weight.astype(BF16)
        if first == 0:
            width = g_cols.shape[0]
            grad_ref[...] = dot(q_cols, grad_score, NT) * scale
            grad_ref[:width, :] += dot(g_cols, weight, NT)
            out_ref[...] = grad_ref[...].astype(BF16)
        last = first + t.shape[0]
        for n in range(weight_ref.shape[0]):
            weight_ref[n, first:last, :] = weight[:, n * size : (n + 1) * size]
            score_ref[n, first:last, :] = grad_score[:, n * size : (n + 1) * size]
        first = last


def keys_kernel(scale, q_ref, g_ref, weight_ref, score_ref, grad_ref):
    first = weight_ref.shape[1] // 2
    steps = range(weight_ref.shape[0])
    width = g_ref.shape[1]
    grad_score = jnp.concatenate([score_ref[n, first:, :] for n in steps], axis=1)
    weight = jnp.concatenate([weight_ref[n, first:, :] for n in steps], axis=1)
    grad_ref[...] = dot(lanes(q_ref), grad_score, NT) * scale
    grad_ref[:width, :] += dot(lanes(g_ref), weight, NT)


def split_kernel(kept_ref, swap_ref, *refs):
    piece_refs = refs[:-1]
    total_ref = refs[-1]
    parts = len(piece_refs)
    block = kept_ref.shape[1] // 2
    odd = lax.rem(lax.axis_index("ctx"), 2) == 1
    crossed = swap_ref[:, block:].astype(F32)
    total_ref[:, :block] = jnp.where(odd, crossed, 0.0)
    total_ref[:, block : 2 * block] = kept_ref[:, :block] + swap_ref[:, :block].astype(F32)
    total_ref[:, 2 * block :] = kept_ref[:, block:] + jnp.where(odd, 0.0, crossed)
    share = total_ref.shape[0] // parts
    for n, piece_ref in enumerate(piece_refs):
        first = pl.multiple_of(lax.rem(lax.axis_index("head") + n, parts) * share, share)
        piece_ref[...] = total_ref[pl.ds(first, share), :].astype(piece_ref.dtype)


def forward_kernel(scale, *refs):
    key_refs = refs[:SLOTS]
    weight_ref, score_ref, att_ref, gq_ref, cols_ref, rows_ref = refs[SLOTS:]
    block = key_refs[0].shape[1]
    latent_width = att_ref.shape[2]
    step = pl.program_id(0)

    @pl.when(step == 0)
    def _():
        for slot, key_ref in enumerate(key_refs):
            cols_ref[:, slot * block : (slot + 1) * block] = key_ref[...]
            rows_ref[slot * block : (slot + 1) * block, :] = key_ref[:latent_width, :].T

    grad = dot(cols_ref[...], score_ref[step]) * scale
    for n in range(PART):
        gq_ref[n] = grad[:, n * block : (n + 1) * block]
    att = dot(weight_ref[step].T, rows_ref[...])
    for n in range(PART):
        att_ref[n] = att[n * block : (n + 1) * block, :].astype(BF16)


def merge_kernel(own_ref, *refs):
    far_ref, back_ref, rest_ref = refs[-3:]
    total = own_ref[...]
    for ref in refs[:-4]:
        total = total + ref[...].astype(F32)
    block = rest_ref.shape[1]
    far_ref[...] = total[:, :block].astype(BF16)
    back_ref[...] = total[:, block : 2 * block].astype(BF16)
    rest_ref[...] = total[:, 2 * block :]


def add_kernel(*refs):
    total = refs[0][...]
    for ref in refs[1:-1]:
        total = total + ref[...].astype(F32)
    refs[-1][...] = total.astype(refs[-1].dtype)


def shards(queries, latent, grad_out, doc_start, block_list):
    block, heads, width = queries.shape
    latent_width = grad_out.shape[2]
    scale = 1.0 / math.sqrt(latent_width // 4 + width - latent_width)
    parts = lax.axis_size("head")
    share = width // parts
    keys = SLOTS * block
    steps = heads // PART
    rows = PART * block
    vmem = pl.BlockSpec(memory_space=pltpu.VMEM)
    smem = pl.BlockSpec(memory_space=pltpu.SMEM)
    anywhere = pl.BlockSpec(memory_space=pl.ANY)
    keep = lambda x: pltpu.with_memory_space_constraint(x, pltpu.VMEM)
    limit = lambda n: pltpu.CompilerParams(vmem_limit_bytes=n * MIB)

    latent_t = latent.T
    back = moved(latent_t, "ctx", lambda s: s + 2)
    mask, token = pl.pallas_call(
        mask_kernel,
        in_specs=[smem, vmem],
        out_specs=[vmem] * 2,
        out_shape=[pltpu.VMEM((keys, block), F32), jax.ShapeDtypeStruct((8, 128), F32)],
        compiler_params=limit(2),
        name="mask",
    )(block_list, doc_start.reshape(1, block))
    mask = keep(mask)
    latent_c, token = lax.optimization_barrier((latent_t, token))
    crossed = moved(latent_c, "ctx", lambda s: s + 3 if s % 2 else s + 1)

    g_t = keep(grad_out.transpose(1, 2, 0))
    block_cost = pl.CostEstimate(
        flops=2 * heads * block * block * (width + latent_width),
        bytes_accessed=4 * MIB,
        transcendentals=0,
    )
    own_score, own_grad, q_t, token = pl.pallas_call(
        functools.partial(own_kernel, scale),
        in_specs=[vmem] * 3 + [anywhere] * 2,
        out_specs=[vmem] * 4,
        out_shape=[pltpu.VMEM((block, heads * block), F32)] * 2
        + [pltpu.VMEM((heads, width, block), BF16), jax.ShapeDtypeStruct((8, 128), F32)],
        scratch_shapes=[pltpu.SemaphoreType.DMA((heads // PART,))],
        compiler_params=limit(16),
        cost_estimate=block_cost,
        name="own",
    )(
        mask,
        keep(latent_t),
        g_t,
        pltpu.with_memory_space_constraint(queries.transpose(1, 2, 0), pltpu.HBM),
        token,
    )
    own_score, own_grad, q_t = keep(own_score), keep(own_grad), keep(q_t)
    back, token = lax.optimization_barrier((back, token))
    swapped = moved(back, "ctx", lambda s: s ^ 1)
    back_score, back_grad = pl.pallas_call(
        functools.partial(back_kernel, scale),
        in_specs=[vmem] * 4 + [anywhere],
        out_specs=[vmem] * 2,
        out_shape=[pltpu.VMEM((block, heads * block), F32)] * 2,
        compiler_params=limit(16),
        cost_estimate=block_cost,
        name="back",
    )(mask, keep(back), g_t, q_t, token)
    back_score, back_grad = keep(back_score), keep(back_grad)
    window = [keep(swapped), keep(crossed), keep(back), keep(latent_t)]

    weight, grad_score, to_swap = pl.pallas_call(
        functools.partial(weights_kernel, scale),
        in_specs=[vmem] * 9,
        out_specs=[vmem] * 3,
        out_shape=[pltpu.VMEM((steps, keys, rows), BF16)] * 2
        + [pltpu.VMEM((width, keys // 2), BF16)],
        scratch_shapes=[pltpu.VMEM((width, keys // 2), F32)],
        compiler_params=limit(28),
        cost_estimate=pl.CostEstimate(
            flops=2 * heads * block * keys * (width + latent_width),
            bytes_accessed=12 * MIB,
            transcendentals=heads * block * keys,
        ),
        name="weights",
    )(mask, *window[:2], q_t, g_t, back_score, back_grad, own_score, own_grad)
    weight, grad_score = keep(weight), keep(grad_score)
    from_swap = moved(to_swap, "ctx", lambda s: s ^ 1)

    kept = pl.pallas_call(
        functools.partial(keys_kernel, scale),
        in_specs=[vmem] * 4,
        out_specs=vmem,
        out_shape=pltpu.VMEM((width, keys // 2), F32),
        compiler_params=limit(16),
        cost_estimate=pl.CostEstimate(
            flops=heads * block * keys * (width + latent_width),
            bytes_accessed=8 * MIB,
            transcendentals=0,
        ),
        name="keys",
    )(q_t, g_t, weight, grad_score)

    own, *pieces = pl.pallas_call(
        split_kernel,
        in_specs=[vmem] * 2,
        out_specs=[vmem] * parts,
        out_shape=[
            pltpu.VMEM((share, 3 * block), BF16 if n else F32) for n in range(parts)
        ],
        scratch_shapes=[pltpu.VMEM((width, 3 * block), F32)],
        compiler_params=limit(4),
        name="split",
    )(keep(kept), keep(from_swap))
    arrived = [moved(piece, "head", lambda s, n=n: s + n + 1) for n, piece in enumerate(pieces)]

    by_group = lambda *tail: pl.BlockSpec((PART, *tail), lambda i: (i,) + (0,) * len(tail))
    att, gq = pl.pallas_call(
        functools.partial(forward_kernel, scale),
        grid=(steps,),
        in_specs=[vmem] * (SLOTS + 2),
        out_specs=[by_group(block, latent_width), by_group(width, block)],
        out_shape=[
            jax.ShapeDtypeStruct((heads, block, latent_width), BF16),
            jax.ShapeDtypeStruct((heads, width, block), F32),
        ],
        scratch_shapes=[pltpu.VMEM((width, keys), BF16), pltpu.VMEM((keys, latent_width), BF16)],
        compiler_params=limit(20),
        cost_estimate=pl.CostEstimate(
            flops=2 * heads * block * keys * (width + latent_width),
            bytes_accessed=12 * MIB,
            transcendentals=0,
        ),
        name="forward",
    )(*window, weight, grad_score)

    to_far, to_back, rest = pl.pallas_call(
        merge_kernel,
        in_specs=[vmem] * parts + [anywhere],
        out_specs=[vmem] * 3,
        out_shape=[pltpu.VMEM((share, block), t) for t in (BF16, BF16, F32)],
        compiler_params=limit(4),
        name="merge",
    )(keep(own), *map(keep, arrived), att)
    from_back = moved(to_back, "ctx", lambda s: s - 2)
    from_far = moved(to_far, "ctx", lambda s: s - 4)
    total = pl.pallas_call(
        add_kernel,
        in_specs=[vmem] * 3,
        out_specs=vmem,
        out_shape=jax.ShapeDtypeStruct((share, block), F32),
        compiler_params=limit(1),
        name="total",
    )(*map(keep, (rest, from_back, from_far)))
    return (att.transpose(1, 0, 2), gq.transpose(2, 0, 1), total.T)


def solution(mesh):
    placed = (
        P("ctx", "head", None),
        P("ctx", None),
        P("ctx", "head", None),
        P("ctx"),
        P("ctx", None),
    )
    return jax.shard_map(
        shards,
        mesh=mesh,
        in_specs=placed,
        out_specs=(P("ctx", "head", None), P("ctx", "head", None), P("ctx", "head")),
        check_vma=False,
    )
```

time: 43.2 us -> 40.2 us (0.931)
  waiting for transfers between devices: 4.88 us -> 0.8 us
  local copies, waits for them, and re-layouts: 5.96 us -> 7.26 us
  starting transfers between devices: 17.8 us -> 17.1 us
  Pallas kernels: 13.3 us -> 13.9 us
    ppermute x9, waiting for transfers between devices: 4.88 us -> 0.8 us  [moved(): lax.ppermute(value, axis, [(s, target(s) % count) for s in range(count)])]
    unnamed x8, local copies, waits for them, and re-layouts: 5.96 us -> 7.26 us
    ppermute x9, starting transfers between devices: 17.8 us -> 17.1 us  [moved(): lax.ppermute(value, axis, [(s, target(s) % count) for s in range(count)])]
    pallas_call x4 -> x7, Pallas kernels: 12.6 us -> 13.2 us  [the longest x1 3.98 us: shards(): pl.pallas_call(functools.partial(forward_kernel, scale), grid=(steps,), i...]
  transfers between devices with their start and end apart: 9 -> 9, of which waited for: 3 -> 2; matrix products, arithmetic and copies ran while one was open for 14% -> 15% of each run, Pallas kernels for 13% -> 23%
where the time goes in v3:
time: 40.2 us; the launch traced here: 39.9 us
  starting transfers between devices  17.1 us (43%)
  Pallas kernels  13.9 us (35%)
  local copies, waits for them, and re-layouts  7.26 us (18%)
  waiting for transfers between devices  0.8 us (2%)
  between operations  0.74 us (2%)
    ppermute x9, starting transfers between devices, moved(): lax.ppermute(value, axis, [(s, target(s) % count) for s in range(count)])  17.1 us
    unnamed x8, local copies, waits for them, and re-layouts  7.26 us
    pallas_call x1, Pallas kernels, shards(): pl.pallas_call(functools.partial(forward_kernel, scale), grid=(steps,), i...  3.98 us
    pallas_call x1, Pallas kernels, shards(): pl.pallas_call(functools.partial(weights_kernel, scale), in_specs=[vmem]...  3.78 us
    pallas_call x1, Pallas kernels, shards(): pl.pallas_call(functools.partial(own_kernel, scale), in_specs=[vmem] * 3...  2.46 us
    pallas_call x1, Pallas kernels, shards(): pl.pallas_call(functools.partial(keys_kernel, scale), in_specs=[vmem] * 4...  1.35 us
    pallas_call x1, Pallas kernels, shards(): pl.pallas_call(functools.partial(back_kernel, scale), in_specs=[vmem] * 4...  0.86 us
  transfers between devices with their start and end apart: 9, of which 2 were waited for; matrix products, arithmetic and copies ran while one was open for 15% of the time, Pallas kernels for 23%

profile of v3, /device:TPU:1, one launch (start us, length us, event | category | flops | bytes accessed | tf_op | source)
XLA Modules:
  0.0 39.9 jit_solution(16340949995235256228)
XLA Ops:
  0.6 2.5 %collective-permute-start = (bf16[576,128]{1,0:T(8,128)(2,1)}, bf16[576,128]{1,0:T(8,128)(2,1)S(1)}, u32[]{:S(2)}, u32[]{:S(2)}) collective-permute-start(bf16[576,128]{1,0:T(8,128)(2,1)} %bitcast.12), channel_id=1, source_target_pairs={{0,8},{4,12},{8,16},{12,20},{16,24},{20,28},{24,32},{28,36},{32,40... | collective-permute-start | bytes 442376 | tf_op jit(solution)/shard_map/ppermute | solution.py:22
  3.2 0.7 %copy-done.1 = s32[1,4]{1,0:T(1,128)S(1)} copy-done((s32[1,4]{1,0:T(1,128)S(1)}, s32[1,4]{1,0:T(1,128)}, u32[]{:S(2)}) %copy-start.1) | copy-done | bytes 40
  3.8 0.7 %copy-done.2 = s32[128]{0:T(128)S(1)} copy-done((s32[128]{0:T(128)S(1)}, s32[128]{0:T(128)}, u32[]{:S(2)}) %copy-start.2) | copy-done | bytes 536
  4.5 0.6 %mask.1 = (f32[512,128]{1,0:T(8,128)S(1)}, f32[8,128]{1,0:T(8,128)S(1)}) custom-call(s32[1,4]{1,0:T(1,128)S(1)} %copy-done.1, s32[1,128]{1,0:T(1,128)S(1)} %bitcast.16), custom_call_target="tpu_custom_call" | custom-call | tf_op jit(solution)/shard_map/mask/pallas_call | solution.py:206
  5.1 0.0 copy-start
  5.1 3.9 %collective-permute-start.2 = (bf16[576,128]{1,0:T(8,128)(2,1)}, bf16[576,128]{1,0:T(8,128)(2,1)S(1)}, u32[]{:S(2)}, u32[]{:S(2)}) collective-permute-start(bf16[576,128]{1,0:T(8,128)(2,1)} %bitcast.13), channel_id=1, source_target_pairs={{0,4},{4,16},{8,12},{12,24},{16,20},{20,32},{24,28},{28,40},{32,36... | collective-permute-start | bytes 442376 | tf_op jit(solution)/shard_map/ppermute | solution.py:22
  9.0 3.5 %copy.8 = bf16[128,16,512]{0,2,1:T(8,128)(2,1)S(1)} copy(bf16[128,16,512]{2,1,0:T(8,128)(2,1)} %param.7) | data formatting | bytes 4194304 | tf_op args[2]
  12.5 2.5 %own.1 = (f32[128,2048]{1,0:T(8,128)S(1)}, f32[128,2048]{1,0:T(8,128)S(1)}, bf16[16,576,128]{2,1,0:T(8,128)(2,1)S(1)}, f32[8,128]{1,0:T(8,128)S(1)}) custom-call(f32[512,128]{1,0:T(8,128)S(1)} %get-tuple-element.27.mask_ref, bf16[576,128]{1,0:T(8,128)(2,1)S(1)} %bitcast.14, bf16[16,512,128]{2,1,0:T(8,128)(2,1)S(1)} %bitcast.7, ...), custom_call_target="tpu_custom_call" | custom-call | flops 570425344 | bytes 4194304 | tf_op jit(solution)/shard_map/own/pallas_call | solution.py:224
  15.0 0.0 collective-permute-done.key_ref.refs_2_
  15.0 0.1 collective-permute-start.1
  15.1 0.9 %back.1 = (f32[128,2048]{1,0:T(8,128)S(1)}, f32[128,2048]{1,0:T(8,128)S(1)}) custom-call(f32[512,128]{1,0:T(8,128)S(1)} %get-tuple-element.27.mask_ref, bf16[576,128]{1,0:T(8,128)(2,1)S(1)} %collective-permute-done.key_ref.refs_2_, bf16[16,512,128]{2,1,0:T(8,128)(2,1)S(1)} %bitcast.8, bf16[16,576,128]{2,1,0:T(8,128)(2,1)S(1)} %get-tuple-element.33.q_ref.refs_2_, ...), custom_call_target="tpu_custom_call" | custom-call | flops 570425344 | bytes 4194304 | tf_op jit(solution)/shard_map/back/pallas_call | solution.py:244
  15.9 0.0 collective-permute-done.2.refs_1_
  15.9 0.5 %collective-permute-done.1.refs_0_ = bf16[576,128]{1,0:T(8,128)(2,1)S(1)} collective-permute-done((bf16[576,128]{1,0:T(8,128)(2,1)S(1)}, bf16[576,128]{1,0:T(8,128)(2,1)S(1)}, u32[]{:S(2)}, u32[]{:S(2)}) %collective-permute-start.1) | collective-permute-done | bytes 147488 | tf_op jit(solution)/shard_map/ppermute | solution.py:22
  16.4 3.8 %weights.1 = (bf16[4,512,512]{2,1,0:T(8,128)(2,1)S(1)}, bf16[4,512,512]{2,1,0:T(8,128)(2,1)S(1)}, bf16[576,256]{1,0:T(8,128)(2,1)S(1)}) custom-call(f32[512,128]{1,0:T(8,128)S(1)} %get-tuple-element.27.mask_ref, bf16[576,128]{1,0:T(8,128)(2,1)S(1)} %collective-permute-done.1.refs_0_, bf16[576,128]{1,0:T(8,128)(2,1)S(1)} %collective-permute-done.2.refs_1_, ...), custom_call_target="tpu_custom_call" | custom-call | flops 2281701376 | bytes 12582912 | tf_op jit(solution)/shard_map/weights/pallas_call | solution.py:256
  20.2 2.1 %collective-permute-start.3 = (bf16[576,256]{1,0:T(8,128)(2,1)S(1)}, bf16[576,256]{1,0:T(8,128)(2,1)S(1)}, u32[]{:S(2)}, u32[]{:S(2)}) collective-permute-start(bf16[576,256]{1,0:T(8,128)(2,1)S(1)} %get-tuple-element.43), channel_id=1, source_target_pairs={{0,4},{4,0},{8,12},{12,8},{16,20},{20,16},{24,28},{28,24},{32,36},... | collective-permute-start | bytes 884744 | tf_op jit(solution)/shard_map/ppermute | solution.py:22
  22.3 1.3 %keys.1.kept_ref = f32[576,256]{1,0:T(8,128)S(1)} custom-call(bf16[16,576,128]{2,1,0:T(8,128)(2,1)S(1)} %get-tuple-element.33.q_ref.refs_2_, bf16[16,512,128]{2,1,0:T(8,128)(2,1)S(1)} %bitcast.10, bf16[4,512,512]{2,1,0:T(8,128)(2,1)S(1)} %get-tuple-element.39.refs_4_.weight_ref, bf16[4,512,512]{2,1,0:T(8,128)(2,1)S(1)} %get-tuple-element.40.refs_5_.score_ref), custom_call_target="tpu_custom_call" | custom-call | flops 1140850688 | bytes 8388608 | tf_op jit(solution)/shard_map/keys/pallas_call | solution.py:274
  23.7 0.0 collective-permute-done.3.swap_ref
  23.7 0.2 split.1
  23.9 1.4 %collective-permute-start.4 = (bf16[144,384]{1,0:T(8,128)(2,1)S(1)}, bf16[144,384]{1,0:T(8,128)(2,1)S(1)}, u32[]{:S(2)}, u32[]{:S(2)}) collective-permute-start(bf16[144,384]{1,0:T(8,128)(2,1)S(1)} %get-tuple-element.45), channel_id=1, source_target_pairs={{0,1},{1,2},{2,3},{3,0},{4,5},{5,6},{6,7},{7,4},{8,9},{9,10},{10,1... | collective-permute-start | bytes 331784 | tf_op jit(solution)/shard_map/ppermute | solution.py:22
  25.3 2.6 %collective-permute-start.5 = (bf16[144,384]{1,0:T(8,128)(2,1)S(1)}, bf16[144,384]{1,0:T(8,128)(2,1)S(1)}, u32[]{:S(2)}, u32[]{:S(2)}) collective-permute-start(bf16[144,384]{1,0:T(8,128)(2,1)S(1)} %get-tuple-element.46), channel_id=1, source_target_pairs={{0,2},{1,3},{2,0},{3,1},{4,6},{5,7},{6,4},{7,5},{8,10},{9,11},{10,... | collective-permute-start | bytes 331784 | tf_op jit(solution)/shard_map/ppermute | solution.py:22
  27.9 1.1 %collective-permute-start.6 = (bf16[144,384]{1,0:T(8,128)(2,1)S(1)}, bf16[144,384]{1,0:T(8,128)(2,1)S(1)}, u32[]{:S(2)}, u32[]{:S(2)}) collective-permute-start(bf16[144,384]{1,0:T(8,128)(2,1)S(1)} %get-tuple-element.47), channel_id=1, source_target_pairs={{0,3},{1,0},{2,1},{3,2},{4,7},{5,4},{6,5},{7,6},{8,11},{9,8},{10,9... | collective-permute-start | bytes 331784 | tf_op jit(solution)/shard_map/ppermute | solution.py:22
  28.9 4.0 %forward.1 = (bf16[16,128,512]{2,1,0:T(8,128)(2,1)S(1)}, f32[16,576,128]{2,1,0:T(8,128)}) custom-call(bf16[576,128]{1,0:T(8,128)(2,1)S(1)} %collective-permute-done.1.refs_0_, bf16[576,128]{1,0:T(8,128)(2,1)S(1)} %collective-permute-done.2.refs_1_, bf16[576,128]{1,0:T(8,128)(2,1)S(1)} %collective-permute-done.key_ref.refs_2_, bf16[576,128]{1,0:T(8,128)(2,1)S(1)} %bitcast.15, ...), custom_call_target="tpu_custom_call" | custom-call | flops 2281701376 | bytes 12582912 | tf_op jit(solution)/shard_map/forward/pallas_call | solution.py:302
  32.9 0.0 collective-permute-done.4.refs_0_
  32.9 0.3 collective-permute-done.5.refs_1_
  33.2 0.0 collective-permute-done.6.refs_2_
  33.2 0.1 merge.1
  33.3 1.3 %collective-permute-start.7 = (bf16[144,128]{1,0:T(8,128)(2,1)S(1)}, bf16[144,128]{1,0:T(8,128)(2,1)S(1)}, u32[]{:S(2)}, u32[]{:S(2)}) collective-permute-start(bf16[144,128]{1,0:T(8,128)(2,1)S(1)} %get-tuple-element.49), channel_id=1, source_target_pairs={{0,248},{4,252},{8,0},{12,4},{16,8},{20,12},{24,16},{28,20},{32,24... | collective-permute-start | bytes 110600 | tf_op jit(solution)/shard_map/ppermute | solution.py:22
  34.6 2.1 %collective-permute-start.8 = (bf16[144,128]{1,0:T(8,128)(2,1)S(1)}, bf16[144,128]{1,0:T(8,128)(2,1)S(1)}, u32[]{:S(2)}, u32[]{:S(2)}) collective-permute-start(bf16[144,128]{1,0:T(8,128)(2,1)S(1)} %get-tuple-element.50), channel_id=1, source_target_pairs={{0,240},{4,244},{8,248},{12,252},{16,0},{20,4},{24,8},{28,12},{32,... | collective-permute-start | bytes 110600 | tf_op jit(solution)/shard_map/ppermute | solution.py:22
  36.7 2.5 %copy.9 = bf16[128,16,512]{2,1,0:T(8,128)(2,1)} copy(bf16[128,16,512]{2,0,1:T(8,128)(2,1)S(1)} %bitcast.11) | data formatting | bytes 4194304
  39.2 0.0 collective-permute-done.7.refs_1_
  39.2 0.0 collective-permute-done.8.refs_2_
  39.2 0.6 %total.1 = f32[144,128]{1,0:T(8,128)} custom-call(f32[144,128]{1,0:T(8,128)S(1)} %get-tuple-element.48.refs_0_, bf16[144,128]{1,0:T(8,128)(2,1)S(1)} %collective-permute-done.7.refs_1_, bf16[144,128]{1,0:T(8,128)(2,1)S(1)} %collective-permute-done.8.refs_2_), custom_call_target="tpu_custom_call" | custom-call | tf_op jit(solution)/shard_map/total/pallas_call | solution.py:331
  (3 shorter events, 0.0 us)
Async XLA Ops:
  0.6 14.3 %collective-permute-start = (bf16[576,128]{1,0:T(8,128)(2,1)}, bf16[576,128]{1,0:T(8,128)(2,1)S(1)}, u32[]{:S(2)}, u32[]{:S(2)}) collective-permute-start(bf16[576,128]{1,0:T(8,128)(2,1)} %bitcast.12), channel_id=1, source_target_pairs={{0,8},{4,12},{8,16},{12,20},{16,24},{20,28},{24,32},{28,36},{32,40... | collective-permute-start | bytes 442376 | tf_op jit(solution)/shard_map/ppermute | solution.py:22
  3.2 0.7 %copy-start.1 = (s32[1,4]{1,0:T(1,128)S(1)}, s32[1,4]{1,0:T(1,128)}, u32[]{:S(2)}) copy-start(s32[1,4]{1,0:T(1,128)} %entries_ref.1) | copy-start | bytes 52
  3.8 0.7 %copy-start.2 = (s32[128]{0:T(128)S(1)}, s32[128]{0:T(128)}, u32[]{:S(2)}) copy-start(s32[128]{0:T(128)} %param.8) | copy-start | bytes 1540
  5.1 7.4 %copy-start = (bf16[128,576]{0,1:T(8,128)(2,1)S(1)}, bf16[128,576]{0,1:T(8,128)(2,1)}, u32[]{:S(2)}) copy-start(bf16[128,576]{0,1:T(8,128)(2,1)} %param.6) | copy-start | bytes 442372
  5.1 10.8 %collective-permute-start.2 = (bf16[576,128]{1,0:T(8,128)(2,1)}, bf16[576,128]{1,0:T(8,128)(2,1)S(1)}, u32[]{:S(2)}, u32[]{:S(2)}) collective-permute-start(bf16[576,128]{1,0:T(8,128)(2,1)} %bitcast.13), channel_id=1, source_target_pairs={{0,4},{4,16},{8,12},{12,24},{16,20},{20,32},{24,28},{28,40},{32,36... | collective-permute-start | bytes 442376 | tf_op jit(solution)/shard_map/ppermute | solution.py:22
  15.0 1.5 %collective-permute-start.1 = (bf16[576,128]{1,0:T(8,128)(2,1)S(1)}, bf16[576,128]{1,0:T(8,128)(2,1)S(1)}, u32[]{:S(2)}, u32[]{:S(2)}) collective-permute-start(bf16[576,128]{1,0:T(8,128)(2,1)S(1)} %collective-permute-done.key_ref.refs_2_), channel_id=1, source_target_pairs={{0,4},{4,0},{8,12},{12,8},{16,20},{20,16},{24,28},{28,24},{32,36},... | collective-permute-start | bytes 442376 | tf_op jit(solution)/shard_map/ppermute | solution.py:22
  20.2 3.5 %collective-permute-start.3 = (bf16[576,256]{1,0:T(8,128)(2,1)S(1)}, bf16[576,256]{1,0:T(8,128)(2,1)S(1)}, u32[]{:S(2)}, u32[]{:S(2)}) collective-permute-start(bf16[576,256]{1,0:T(8,128)(2,1)S(1)} %get-tuple-element.43), channel_id=1, source_target_pairs={{0,4},{4,0},{8,12},{12,8},{16,20},{20,16},{24,28},{28,24},{32,36},... | collective-permute-start | bytes 884744 | tf_op jit(solution)/shard_map/ppermute | solution.py:22
  23.9 9.0 %collective-permute-start.4 = (bf16[144,384]{1,0:T(8,128)(2,1)S(1)}, bf16[144,384]{1,0:T(8,128)(2,1)S(1)}, u32[]{:S(2)}, u32[]{:S(2)}) collective-permute-start(bf16[144,384]{1,0:T(8,128)(2,1)S(1)} %get-tuple-element.45), channel_id=1, source_target_pairs={{0,1},{1,2},{2,3},{3,0},{4,5},{5,6},{6,7},{7,4},{8,9},{9,10},{10,1... | collective-permute-start | bytes 331784 | tf_op jit(solution)/shard_map/ppermute | solution.py:22
  25.3 8.0 %collective-permute-start.5 = (bf16[144,384]{1,0:T(8,128)(2,1)S(1)}, bf16[144,384]{1,0:T(8,128)(2,1)S(1)}, u32[]{:S(2)}, u32[]{:S(2)}) collective-permute-start(bf16[144,384]{1,0:T(8,128)(2,1)S(1)} %get-tuple-element.46), channel_id=1, source_target_pairs={{0,2},{1,3},{2,0},{3,1},{4,6},{5,7},{6,4},{7,5},{8,10},{9,11},{10,... | collective-permute-start | bytes 331784 | tf_op jit(solution)/shard_map/ppermute | solution.py:22
  27.9 5.4 %collective-permute-start.6 = (bf16[144,384]{1,0:T(8,128)(2,1)S(1)}, bf16[144,384]{1,0:T(8,128)(2,1)S(1)}, u32[]{:S(2)}, u32[]{:S(2)}) collective-permute-start(bf16[144,384]{1,0:T(8,128)(2,1)S(1)} %get-tuple-element.47), channel_id=1, source_target_pairs={{0,3},{1,0},{2,1},{3,2},{4,7},{5,4},{6,5},{7,6},{8,11},{9,8},{10,9... | collective-permute-start | bytes 331784 | tf_op jit(solution)/shard_map/ppermute | solution.py:22
  33.3 5.9 %collective-permute-start.7 = (bf16[144,128]{1,0:T(8,128)(2,1)S(1)}, bf16[144,128]{1,0:T(8,128)(2,1)S(1)}, u32[]{:S(2)}, u32[]{:S(2)}) collective-permute-start(bf16[144,128]{1,0:T(8,128)(2,1)S(1)} %get-tuple-element.49), channel_id=1, source_target_pairs={{0,248},{4,252},{8,0},{12,4},{16,8},{20,12},{24,16},{28,20},{32,24... | collective-permute-start | bytes 110600 | tf_op jit(solution)/shard_map/ppermute | solution.py:22
  34.6 4.6 %collective-permute-start.8 = (bf16[144,128]{1,0:T(8,128)(2,1)S(1)}, bf16[144,128]{1,0:T(8,128)(2,1)S(1)}, u32[]{:S(2)}, u32[]{:S(2)}) collective-permute-start(bf16[144,128]{1,0:T(8,128)(2,1)S(1)} %get-tuple-element.50), channel_id=1, source_target_pairs={{0,240},{4,244},{8,248},{12,252},{16,0},{20,4},{24,8},{28,12},{32,... | collective-permute-start | bytes 110600 | tf_op jit(solution)/shard_map/ppermute | solution.py:22

commit v4 on v3

--- a/solution.py
+++ b/solution.py
@@ -12,6 +12,7 @@
 BF16 = jnp.bfloat16
 SLOTS = 4
 PART = 4
+COPIES = (4, 2)
 MIB = 1 << 20
 NN = (((1,), (0,)), ((), ()))
 NT = (((1,), (1,)), ((), ()))
@@ -30,7 +31,7 @@
     return jnp.concatenate([ref[n] for n in range(ref.shape[0])], axis=1)
 
 
-def mask_kernel(entries_ref, start_ref, mask_ref, token_ref):
+def write_mask(mask_ref, entries_ref, start_ref):
     place = lax.axis_index("ctx")
     parity = lax.rem(place, 2)
     block = start_ref.shape[1]
@@ -44,48 +45,74 @@
         k_pos = first + lax.broadcasted_iota(jnp.int32, (block, block), 0)
         allowed = (k_pos <= q_pos) & (k_pos >= start_ref[...])
         mask_ref[slot * block : (slot + 1) * block, :] = jnp.where(allowed, 0.0, -1e30)
-    token_ref[...] = jnp.zeros_like(token_ref)
-
-
-def scores_of(scale, keys, mask, q_cols, g_cols):
+
+
+def scores_of(scale, keys, mask, q_cols):
     heads = q_cols.shape[1] // mask.shape[1]
     mask = jnp.concatenate([mask] * heads, axis=1)
-    score = dot(keys, q_cols) * (scale * math.log2(math.e)) + mask
-    return score, dot(keys[:, : g_cols.shape[0]], g_cols)
-
-
-def own_kernel(
-    scale, mask_ref, key_ref, g_ref, from_ref, _, score_ref, grad_ref, q_ref, token_ref, sems
-):
-    chunks = sems.shape[0]
-    size = from_ref.shape[0] // chunks
-    copies = [
+    return dot(keys, q_cols) * (scale * math.log2(math.e)) + mask
+
+
+def own_kernel(scale, key_from, entries_from, start_from, g_from, q_from, *refs):
+    score_ref, grad_ref, q_ref, g_ref, mask_ref, key_ref, token_ref = refs[:7]
+    entries_ref, start_ref, buffer_ref, sems = refs[7:]
+    tokens, heads, latent_width = g_from.shape
+    g_chunks, q_chunks = COPIES
+    tables = [
+        pltpu.make_async_copy(entries_from, entries_ref, sems.at[0]),
+        pltpu.make_async_copy(start_from, start_ref, sems.at[1]),
+        pltpu.make_async_copy(key_from, key_ref, sems.at[2]),
+    ]
+    size = tokens // g_chunks
+    g_copies = [
         pltpu.make_async_copy(
-            from_ref.at[pl.ds(n * size, size)], q_ref.at[pl.ds(n * size, size)], sems.at[n]
+            g_from.at[pl.ds(n * size, size)], buffer_ref.at[pl.ds(n * size, size)], sems.at[3 + n]
         )
-        for n in range(chunks)
+        for n in range(g_chunks)
     ]
-    for copy in copies:
+    part_heads = heads // q_chunks
+    q_copies = [
+        pltpu.make_async_copy(
+            q_from.at[pl.ds(n * part_heads, part_heads)],
+            q_ref.at[pl.ds(n * part_heads, part_heads)],
+            sems.at[3 + g_chunks + n],
+        )
+        for n in range(q_chunks)
+    ]
+    for copy in tables + g_copies + q_copies:
         copy.start()
+    token_ref[...] = jnp.zeros_like(token_ref)
+    for copy in tables:
+        copy.wait()
     keys = key_ref[...].T
-    first = mask_ref.shape[0] - keys.shape[0]
-    mask = mask_ref[first:, :]
-    span = size * mask.shape[1]
-    for n, copy in enumerate(copies):
+    write_mask(mask_ref, entries_ref, start_ref)
+    mask = mask_ref[mask_ref.shape[0] - keys.shape[0] :, :]
+
+    few = 256 // heads
+    order = regroup(few, heads)
+    for n, copy in enumerate(g_copies):
         copy.wait()
-        heads = slice(n * size, (n + 1) * size)
-        score, grad_weight = scores_of(scale, keys, mask, lanes(q_ref[heads]), lanes(g_ref[heads]))
-        score_ref[:, n * span : (n + 1) * span] = score
-        grad_ref[:, n * span : (n + 1) * span] = grad_weight
-    token_ref[...] = jnp.zeros_like(token_ref)
-
-
-def back_kernel(scale, mask_ref, key_ref, g_ref, q_ref, _, score_ref, grad_ref):
+        for first in range(n * size, (n + 1) * size, few):
+            part = buffer_ref[first : first + few].reshape(few * heads, latent_width)
+            part = dot(order, part).astype(BF16)
+            for h in range(heads):
+                g_ref[h * tokens + first : h * tokens + first + few, :] = part[
+                    h * few : (h + 1) * few
+                ]
+    grad_ref[...] = dot(keys[:, :latent_width], g_ref[...], NT)
+    span = part_heads * tokens
+    for n, copy in enumerate(q_copies):
+        copy.wait()
+        q_cols = lanes(q_ref[n * part_heads : (n + 1) * part_heads])
+        score_ref[:, n * span : (n + 1) * span] = scores_of(scale, keys, mask, q_cols)
+
+
+def back_kernel(scale, mask_ref, key_ref, q_ref, g_ref, _, score_ref, grad_ref):
     block = key_ref.shape[1]
     mask = mask_ref[2 * block : 3 * block, :]
-    score, grad_weight = scores_of(scale, key_ref[...].T, mask, lanes(q_ref), lanes(g_ref))
-    score_ref[...] = score
-    grad_ref[...] = grad_weight
+    keys = key_ref[...].T
+    score_ref[...] = scores_of(scale, keys, mask, lanes(q_ref))
+    grad_ref[...] = dot(keys[:, : g_ref.shape[1]], g_ref[...], NT)
 
 
 def weights_kernel(scale, mask_ref, *refs):
@@ -93,8 +120,8 @@
     keys = jnp.concatenate([swap_ref[...].T, cross_ref[...].T], axis=0)
     mask = mask_ref[: keys.shape[0], :]
     q_cols = lanes(q_ref)
-    g_cols = lanes(g_ref)
-    parts = [scores_of(scale, keys, mask, q_cols, g_cols)]
+    width = g_ref.shape[1]
+    parts = [(scores_of(scale, keys, mask, q_cols), dot(keys[:, :width], g_ref[...], NT))]
     parts += [(known[n][...], known[n + 1][...]) for n in range(0, len(known), 2)]
     top = functools.reduce(jnp.maximum, [jnp.max(s, axis=0, keepdims=True) for s, _ in parts])
     terms = [jnp.exp2(s - top) for s, _ in parts]
@@ -110,9 +137,8 @@
         grad_score = (weight * (grad_weight - delta)).astype(BF16)
         weight = weight.astype(BF16)
         if first == 0:
-            width = g_cols.shape[0]
             grad_ref[...] = dot(q_cols, grad_score, NT) * scale
-            grad_ref[:width, :] += dot(g_cols, weight, NT)
+            grad_ref[:width, :] += dot(weight, g_ref[...]).T
             out_ref[...] = grad_ref[...].astype(BF16)
         last = first + t.shape[0]
         for n in range(weight_ref.shape[0]):
@@ -128,7 +154,7 @@
     grad_score = jnp.concatenate([score_ref[n, first:, :] for n in steps], axis=1)
     weight = jnp.concatenate([weight_ref[n, first:, :] for n in steps], axis=1)
     grad_ref[...] = dot(lanes(q_ref), grad_score, NT) * scale
-    grad_ref[:width, :] += dot(lanes(g_ref), weight, NT)
+    grad_ref[:width, :] += dot(weight, g_ref[...]).T
 
 
 def split_kernel(kept_ref, swap_ref, *refs):
@@ -147,25 +173,61 @@
         piece_ref[...] = total_ref[pl.ds(first, share), :].astype(piece_ref.dtype)
 
 
+def regroup(few, heads):
+    row = lax.broadcasted_iota(jnp.int32, (few * heads, few * heads), 0)
+    col = lax.broadcasted_iota(jnp.int32, (few * heads, few * heads), 1)
+    order = (row // few == col % heads) & (row % few == col // heads)
+    return order.astype(F32).astype(BF16)
+
+
 def forward_kernel(scale, *refs):
     key_refs = refs[:SLOTS]
-    weight_ref, score_ref, att_ref, gq_ref, cols_ref, rows_ref = refs[SLOTS:]
+    weight_ref, score_ref, att_to, gq_to, cols_ref, rows_ref = refs[SLOTS : SLOTS + 6]
+    by_head_ref, att_ref, gq_ref, sems = refs[SLOTS + 6 :]
     block = key_refs[0].shape[1]
-    latent_width = att_ref.shape[2]
-    step = pl.program_id(0)
-
-    @pl.when(step == 0)
-    def _():
-        for slot, key_ref in enumerate(key_refs):
-            cols_ref[:, slot * block : (slot + 1) * block] = key_ref[...]
-            rows_ref[slot * block : (slot + 1) * block, :] = key_ref[:latent_width, :].T
-
-    grad = dot(cols_ref[...], score_ref[step]) * scale
-    for n in range(PART):
-        gq_ref[n] = grad[:, n * block : (n + 1) * block]
-    att = dot(weight_ref[step].T, rows_ref[...])
-    for n in range(PART):
-        att_ref[n] = att[n * block : (n + 1) * block, :].astype(BF16)
+    tokens, heads, latent_width = att_ref.shape
+    steps = heads // PART
+    copies = []
+
+    def send(source, target, first, count):
+        span = pl.ds(first, count)
+        copies.append(
+            pltpu.make_async_copy(source.at[span], target.at[span], sems.at[len(copies)])
+        )
+        copies[-1].start()
+
+    def grad_queries(step):
+        grad = dot(cols_ref[...], score_ref[step]) * scale
+        for n in range(PART):
+            gq_ref[step * PART + n] = grad[:, n * block : (n + 1) * block]
+        send(gq_ref, gq_to, step * PART, PART)
+
+    for slot, key_ref in enumerate(key_refs):
+        cols_ref[:, slot * block : (slot + 1) * block] = key_ref[...]
+        rows_ref[slot * block : (slot + 1) * block, :] = key_ref[:latent_width, :].T
+    grad_queries(0)
+    span = PART * block
+    for step in range(steps):
+        att = dot(weight_ref[step].T, rows_ref[...])
+        by_head_ref[step * span : (step + 1) * span, :] = att.astype(BF16)
+    few = 256 // heads
+    order = regroup(few, heads)
+    size = tokens // steps
+    for chunk in range(steps):
+        for first in range(chunk * size, (chunk + 1) * size, few):
+            part = jnp.concatenate(
+                [by_head_ref[h * tokens + first : h * tokens + first + few, :] for h in range(heads)],
+                axis=0,
+            )
+            part = lax.dot_general(
+                order, part, (((0,), (0,)), ((), ())), preferred_element_type=F32
+            )
+            att_ref[first : first + few] = part.astype(BF16).reshape(few, heads, latent_width)
+        send(att_ref, att_to, chunk * size, size)
+    for step in range(1, steps):
+        grad_queries(step)
+    for copy in copies:
+        copy.wait()
 
 
 def merge_kernel(own_ref, *refs):
@@ -203,41 +265,43 @@
 
     latent_t = latent.T
     back = moved(latent_t, "ctx", lambda s: s + 2)
-    mask, token = pl.pallas_call(
-        mask_kernel,
-        in_specs=[smem, vmem],
-        out_specs=[vmem] * 2,
-        out_shape=[pltpu.VMEM((keys, block), F32), jax.ShapeDtypeStruct((8, 128), F32)],
-        compiler_params=limit(2),
-        name="mask",
-    )(block_list, doc_start.reshape(1, block))
-    mask = keep(mask)
-    latent_c, token = lax.optimization_barrier((latent_t, token))
-    crossed = moved(latent_c, "ctx", lambda s: s + 3 if s % 2 else s + 1)
-
-    g_t = keep(grad_out.transpose(1, 2, 0))
+    crossed = moved(latent_t, "ctx", lambda s: s + 3 if s % 2 else s + 1)
+
     block_cost = pl.CostEstimate(
         flops=2 * heads * block * block * (width + latent_width),
         bytes_accessed=4 * MIB,
         transcendentals=0,
     )
-    own_score, own_grad, q_t, token = pl.pallas_call(
+    in_hbm = lambda x: pltpu.with_memory_space_constraint(x, pltpu.HBM)
+    own_score, own_grad, q_t, g_rows, mask, own_t, token = pl.pallas_call(
         functools.partial(own_kernel, scale),
-        in_specs=[vmem] * 3 + [anywhere] * 2,
-        out_specs=[vmem] * 4,
+        in_specs=[anywhere] * 5,
+        out_specs=[vmem] * 7,
         out_shape=[pltpu.VMEM((block, heads * block), F32)] * 2
-        + [pltpu.VMEM((heads, width, block), BF16), jax.ShapeDtypeStruct((8, 128), F32)],
-        scratch_shapes=[pltpu.SemaphoreType.DMA((heads // PART,))],
+        + [
+            pltpu.VMEM((heads, width, block), BF16),
+            pltpu.VMEM((heads * block, latent_width), BF16),
+            pltpu.VMEM((keys, block), F32),
+            pltpu.VMEM((width, block), BF16),
+            jax.ShapeDtypeStruct((8, 128), F32),
+        ],
+        scratch_shapes=[
+            pltpu.SMEM(block_list.shape, jnp.int32),
+            pltpu.VMEM((1, block), jnp.int32),
+            pltpu.VMEM((block, heads, latent_width), BF16),
+            pltpu.SemaphoreType.DMA((3 + sum(COPIES),)),
+        ],
         compiler_params=limit(16),
         cost_estimate=block_cost,
         name="own",
     )(
-        mask,
-        keep(latent_t),
-        g_t,
-        pltpu.with_memory_space_constraint(queries.transpose(1, 2, 0), pltpu.HBM),
-        token,
+        in_hbm(latent_t),
+        in_hbm(block_list),
+        in_hbm(doc_start.reshape(1, block)),
+        in_hbm(grad_out),
+        in_hbm(queries.transpose(1, 2, 0)),
     )
+    g_rows, mask, own_t = keep(g_rows), keep(mask), keep(own_t)
     own_score, own_grad, q_t = keep(own_score), keep(own_grad), keep(q_t)
     back, token = lax.optimization_barrier((back, token))
     swapped = moved(back, "ctx", lambda s: s ^ 1)
@@ -249,9 +313,9 @@
         compiler_params=limit(16),
         cost_estimate=block_cost,
         name="back",
-    )(mask, keep(back), g_t, q_t, token)
+    )(mask, keep(back), q_t, g_rows, token)
     back_score, back_grad = keep(back_score), keep(back_grad)
-    window = [keep(swapped), keep(crossed), keep(back), keep(latent_t)]
+    window = [keep(swapped), keep(crossed), keep(back), own_t]
 
     weight, grad_score, to_swap = pl.pallas_call(
         functools.partial(weights_kernel, scale),
@@ -267,7 +331,7 @@
             transcendentals=heads * block * keys,
         ),
         name="weights",
-    )(mask, *window[:2], q_t, g_t, back_score, back_grad, own_score, own_grad)
+    )(mask, *window[:2], q_t, g_rows, back_score, back_grad, own_score, own_grad)
     weight, grad_score = keep(weight), keep(grad_score)
     from_swap = moved(to_swap, "ctx", lambda s: s ^ 1)
 
@@ -283,7 +347,7 @@
             transcendentals=0,
         ),
         name="keys",
-    )(q_t, g_t, weight, grad_score)
+    )(q_t, g_rows, weight, grad_score)
 
     own, *pieces = pl.pallas_call(
         split_kernel,
@@ -298,18 +362,23 @@
     )(keep(kept), keep(from_swap))
     arrived = [moved(piece, "head", lambda s, n=n: s + n + 1) for n, piece in enumerate(pieces)]
 
-    by_group = lambda *tail: pl.BlockSpec((PART, *tail), lambda i: (i,) + (0,) * len(tail))
     att, gq = pl.pallas_call(
         functools.partial(forward_kernel, scale),
-        grid=(steps,),
         in_specs=[vmem] * (SLOTS + 2),
-        out_specs=[by_group(block, latent_width), by_group(width, block)],
+        out_specs=[anywhere] * 2,
         out_shape=[
-            jax.ShapeDtypeStruct((heads, block, latent_width), BF16),
-            jax.ShapeDtypeStruct((heads, width, block), F32),
+            pltpu.HBM((block, heads, latent_width), BF16),
+            pltpu.HBM((heads, width, block), F32),
         ],
-        scratch_shapes=[pltpu.VMEM((width, keys), BF16), pltpu.VMEM((keys, latent_width), BF16)],
-        compiler_params=limit(20),
+        scratch_shapes=[
+            pltpu.VMEM((width, keys), BF16),
+            pltpu.VMEM((keys, latent_width), BF16),
+            pltpu.VMEM((heads * block, latent_width), BF16),
+            pltpu.VMEM((block, heads, latent_width), BF16),
+            pltpu.VMEM((heads, width, block), F32),
+            pltpu.SemaphoreType.DMA((2 * steps,)),
+        ],
+        compiler_params=limit(28),
         cost_estimate=pl.CostEstimate(
             flops=2 * heads * block * keys * (width + latent_width),
             bytes_accessed=12 * MIB,
@@ -325,9 +394,9 @@
         out_shape=[pltpu.VMEM((share, block), t) for t in (BF16, BF16, F32)],
         compiler_params=limit(4),
         name="merge",
-    )(keep(own), *map(keep, arrived), att)
+    )(keep(own), *map(keep, arrived), in_hbm(att))
     from_back = moved(to_back, "ctx", lambda s: s - 2)
-    from_far = moved(to_far, "ctx", lambda s: s - 4)
+    from_far = moved(to_far, "ctx", lambda s: s - 4 if s % 2 else s - 2)
     total = pl.pallas_call(
         add_kernel,
         in_specs=[vmem] * 3,
@@ -336,7 +405,7 @@
         compiler_params=limit(1),
         name="total",
     )(*map(keep, (rest, from_back, from_far)))
-    return (att.transpose(1, 0, 2), gq.transpose(2, 0, 1), total.T)
+    return (att, gq.transpose(2, 0, 1), total.T)
 
 
 def solution(mesh):

time: 40.2 us -> 39.3 us (0.978)
  local copies, waits for them, and re-layouts: 7.26 us -> 0 us
  waiting for transfers between devices: 0.8 us -> 3.83 us
  starting transfers between devices: 17.1 us -> 19 us
  Pallas kernels: 13.9 us -> 15.7 us
    unnamed x8 -> x0, local copies, waits for them, and re-layouts: 7.26 us -> none
    ppermute x9, waiting for transfers between devices: 0.8 us -> 3.83 us  [moved(): lax.ppermute(value, axis, [(s, target(s) % count) for s in range(count)])]
    ppermute x9, starting transfers between devices: 17.1 us -> 19 us  [moved(): lax.ppermute(value, axis, [(s, target(s) % count) for s in range(count)])]
    pallas_call x3 -> x2, Pallas kernels: 7.04 us -> 8.27 us  [the longest x1 4.38 us: shards(): pl.pallas_call(functools.partial(forward_kernel, scale), in_specs=[vmem]...]
  transfers between devices with their start and end apart: 9 -> 9, of which waited for: 2 -> 2; matrix products, arithmetic and copies ran while one was open for 15% -> 0% of each run, Pallas kernels for 23% -> 28%
where the time goes in v4:
time: 39.3 us; the launch traced here: 39.2 us
  starting transfers between devices  19 us (48%)
  Pallas kernels  15.7 us (40%)
  waiting for transfers between devices  3.83 us (10%)
  between operations  0.73 us (2%)
    ppermute x9, starting transfers between devices, moved(): lax.ppermute(value, axis, [(s, target(s) % count) for s in range(count)])  19 us
    pallas_call x1, Pallas kernels, shards(): pl.pallas_call(functools.partial(forward_kernel, scale), in_specs=[vmem]...  4.38 us
    pallas_call x1, Pallas kernels, shards(): pl.pallas_call(functools.partial(own_kernel, scale), in_specs=[anywhere]...  3.9 us
    ppermute x9, waiting for transfers between devices, moved(): lax.ppermute(value, axis, [(s, target(s) % count) for s in range(count)])  3.83 us
    pallas_call x1, Pallas kernels, shards(): pl.pallas_call(functools.partial(weights_kernel, scale), in_specs=[vmem]...  3.81 us
    pallas_call x1, Pallas kernels, shards(): pl.pallas_call(functools.partial(keys_kernel, scale), in_specs=[vmem] * 4...  1.42 us
    pallas_call x1, Pallas kernels, shards(): pl.pallas_call(functools.partial(back_kernel, scale), in_specs=[vmem] * 4...  1.26 us
  transfers between devices with their start and end apart: 9, of which 2 were waited for; matrix products, arithmetic and copies ran while one was open for 0% of the time, Pallas kernels for 28%

profile of v4, /device:TPU:1, one launch (start us, length us, event | category | flops | bytes accessed | tf_op | source)
XLA Modules:
  0.0 39.2 jit_solution(13959461479163101651)
XLA Ops:
  0.6 2.5 %collective-permute-start = (bf16[576,128]{1,0:T(8,128)(2,1)}, bf16[576,128]{1,0:T(8,128)(2,1)S(1)}, u32[]{:S(2)}, u32[]{:S(2)}) collective-permute-start(bf16[576,128]{1,0:T(8,128)(2,1)} %bitcast.6), channel_id=1, source_target_pairs={{0,8},{4,12},{8,16},{12,20},{16,24},{20,28},{24,32},{28,36},{32,40... | collective-permute-start | bytes 442376 | tf_op jit(solution)/shard_map/ppermute | solution.py:23
  3.2 3.8 %collective-permute-start.2 = (bf16[576,128]{1,0:T(8,128)(2,1)}, bf16[576,128]{1,0:T(8,128)(2,1)S(1)}, u32[]{:S(2)}, u32[]{:S(2)}) collective-permute-start(bf16[576,128]{1,0:T(8,128)(2,1)} %bitcast.7), channel_id=1, source_target_pairs={{0,4},{4,16},{8,12},{12,24},{16,20},{20,32},{24,28},{28,40},{32,36... | collective-permute-start | bytes 442376 | tf_op jit(solution)/shard_map/ppermute | solution.py:23
  7.0 3.9 %own.1 = (f32[128,2048]{1,0:T(8,128)S(1)}, f32[128,2048]{1,0:T(8,128)S(1)}, bf16[16,576,128]{2,1,0:T(8,128)(2,1)S(1)}, bf16[2048,512]{1,0:T(8,128)(2,1)S(1)}, f3...) custom-call(bf16[576,128]{1,0:T(8,128)(2,1)} %bitcast.8, s32[1,4]{1,0:T(1,128)} %entries_from.1, ...), custom_call_target="tpu_custom_call" | custom-call | flops 570425344 | bytes 4194304 | tf_op jit(solution)/shard_map/own/pallas_call | solution.py:276
  10.9 2.2 %collective-permute-done.key_ref.refs_2_ = bf16[576,128]{1,0:T(8,128)(2,1)S(1)} collective-permute-done((bf16[576,128]{1,0:T(8,128)(2,1)}, bf16[576,128]{1,0:T(8,128)(2,1)S(1)}, u32[]{:S(2)}, u32[]{:S(2)}) %collective-permute-start) | collective-permute-done | bytes 147488 | tf_op jit(solution)/shard_map/ppermute | solution.py:23
  13.1 2.5 %collective-permute-start.1 = (bf16[576,128]{1,0:T(8,128)(2,1)S(1)}, bf16[576,128]{1,0:T(8,128)(2,1)S(1)}, u32[]{:S(2)}, u32[]{:S(2)}) collective-permute-start(bf16[576,128]{1,0:T(8,128)(2,1)S(1)} %collective-permute-done.key_ref.refs_2_), channel_id=1, source_target_pairs={{0,4},{4,0},{8,12},{12,8},{16,20},{20,16},{24,28},{28,24},{32,36},... | collective-permute-start | bytes 442376 | tf_op jit(solution)/shard_map/ppermute | solution.py:23
  15.6 1.3 %back.1 = (f32[128,2048]{1,0:T(8,128)S(1)}, f32[128,2048]{1,0:T(8,128)S(1)}) custom-call(f32[512,128]{1,0:T(8,128)S(1)} %get-tuple-element.29.mask_ref, bf16[576,128]{1,0:T(8,128)(2,1)S(1)} %collective-permute-done.key_ref.refs_2_, bf16[16,576,128]{2,1,0:T(8,128)(2,1)S(1)} %get-tuple-element.30.q_ref.refs_2_, ...), custom_call_target="tpu_custom_call" | custom-call | flops 570425344 | bytes 4194304 | tf_op jit(solution)/shard_map/back/pallas_call | solution.py:308
  16.9 0.0 collective-permute-done.2.refs_1_
  16.9 0.0 collective-permute-done.1.refs_0_
  16.9 3.8 %weights.1 = (bf16[4,512,512]{2,1,0:T(8,128)(2,1)S(1)}, bf16[4,512,512]{2,1,0:T(8,128)(2,1)S(1)}, bf16[576,256]{1,0:T(8,128)(2,1)S(1)}) custom-call(f32[512,128]{1,0:T(8,128)S(1)} %get-tuple-element.29.mask_ref, bf16[576,128]{1,0:T(8,128)(2,1)S(1)} %collective-permute-done.1.refs_0_, bf16[576,128]{1,0:T(8,128)(2,1)S(1)} %collective-permute-done.2.refs_1_, ...), custom_call_target="tpu_custom_call" | custom-call | flops 2281701376 | bytes 12582912 | tf_op jit(solution)/shard_map/weights/pallas_call | solution.py:320
  20.7 1.2 %collective-permute-start.3 = (bf16[576,256]{1,0:T(8,128)(2,1)S(1)}, bf16[576,256]{1,0:T(8,128)(2,1)S(1)}, u32[]{:S(2)}, u32[]{:S(2)}) collective-permute-start(bf16[576,256]{1,0:T(8,128)(2,1)S(1)} %get-tuple-element.41), channel_id=1, source_target_pairs={{0,4},{4,0},{8,12},{12,8},{16,20},{20,16},{24,28},{28,24},{32,36},... | collective-permute-start | bytes 884744 | tf_op jit(solution)/shard_map/ppermute | solution.py:23
  21.9 1.4 %keys.1.kept_ref = f32[576,256]{1,0:T(8,128)S(1)} custom-call(bf16[16,576,128]{2,1,0:T(8,128)(2,1)S(1)} %get-tuple-element.30.q_ref.refs_2_, bf16[2048,512]{1,0:T(8,128)(2,1)S(1)} %get-tuple-element.31.g_ref.refs_3_, bf16[4,512,512]{2,1,0:T(8,128)(2,1)S(1)} %get-tuple-element.37.refs_4_.weight_ref, bf16[4,512,512]{2,1,0:T(8,128)(2,1)S(1)} %get-tuple-element.38.refs_5_.score_ref), custom_call_target="tpu_custom_call" | custom-call | flops 1140850688 | bytes 8388608 | tf_op jit(solution)/shard_map/keys/pallas_call | solution.py:338
  23.4 0.0 collective-permute-done.3.swap_ref
  23.4 0.2 split.1
  23.5 1.4 %collective-permute-start.4 = (bf16[144,384]{1,0:T(8,128)(2,1)S(1)}, bf16[144,384]{1,0:T(8,128)(2,1)S(1)}, u32[]{:S(2)}, u32[]{:S(2)}) collective-permute-start(bf16[144,384]{1,0:T(8,128)(2,1)S(1)} %get-tuple-element.43), channel_id=1, source_target_pairs={{0,1},{1,2},{2,3},{3,0},{4,5},{5,6},{6,7},{7,4},{8,9},{9,10},{10,1... | collective-permute-start | bytes 331784 | tf_op jit(solution)/shard_map/ppermute | solution.py:23
  24.9 2.6 %collective-permute-start.5 = (bf16[144,384]{1,0:T(8,128)(2,1)S(1)}, bf16[144,384]{1,0:T(8,128)(2,1)S(1)}, u32[]{:S(2)}, u32[]{:S(2)}) collective-permute-start(bf16[144,384]{1,0:T(8,128)(2,1)S(1)} %get-tuple-element.44), channel_id=1, source_target_pairs={{0,2},{1,3},{2,0},{3,1},{4,6},{5,7},{6,4},{7,5},{8,10},{9,11},{10,... | collective-permute-start | bytes 331784 | tf_op jit(solution)/shard_map/ppermute | solution.py:23
  27.5 1.1 %collective-permute-start.6 = (bf16[144,384]{1,0:T(8,128)(2,1)S(1)}, bf16[144,384]{1,0:T(8,128)(2,1)S(1)}, u32[]{:S(2)}, u32[]{:S(2)}) collective-permute-start(bf16[144,384]{1,0:T(8,128)(2,1)S(1)} %get-tuple-element.45), channel_id=1, source_target_pairs={{0,3},{1,0},{2,1},{3,2},{4,7},{5,4},{6,5},{7,6},{8,11},{9,8},{10,9... | collective-permute-start | bytes 331784 | tf_op jit(solution)/shard_map/ppermute | solution.py:23
  28.6 4.4 %forward.1 = (bf16[128,16,512]{2,1,0:T(8,128)(2,1)}, f32[16,576,128]{2,1,0:T(8,128)}) custom-call(bf16[576,128]{1,0:T(8,128)(2,1)S(1)} %collective-permute-done.1.refs_0_, bf16[576,128]{1,0:T(8,128)(2,1)S(1)} %collective-permute-done.2.refs_1_, bf16[576,128]{1,0:T(8,128)(2,1)S(1)} %collective-permute-done.key_ref.refs_2_, ...), custom_call_target="tpu_custom_call" | custom-call | flops 2281701376 | bytes 12582912 | tf_op jit(solution)/shard_map/forward/pallas_call | solution.py:365
  33.0 0.0 collective-permute-done.4.refs_0_
  33.0 0.0 collective-permute-done.5.refs_1_
  33.0 0.0 collective-permute-done.6.refs_2_
  33.0 0.1 merge.1
  33.1 1.4 %collective-permute-start.7 = (bf16[144,128]{1,0:T(8,128)(2,1)S(1)}, bf16[144,128]{1,0:T(8,128)(2,1)S(1)}, u32[]{:S(2)}, u32[]{:S(2)}) collective-permute-start(bf16[144,128]{1,0:T(8,128)(2,1)S(1)} %get-tuple-element.47), channel_id=1, source_target_pairs={{0,248},{4,252},{8,0},{12,4},{16,8},{20,12},{24,16},{28,20},{32,24... | collective-permute-start | bytes 110600 | tf_op jit(solution)/shard_map/ppermute | solution.py:23
  34.5 2.4 %collective-permute-start.8 = (bf16[144,128]{1,0:T(8,128)(2,1)S(1)}, bf16[144,128]{1,0:T(8,128)(2,1)S(1)}, u32[]{:S(2)}, u32[]{:S(2)}) collective-permute-start(bf16[144,128]{1,0:T(8,128)(2,1)S(1)} %get-tuple-element.48), channel_id=1, source_target_pairs={{0,248},{4,244},{8,0},{12,252},{16,8},{20,4},{24,16},{28,12},{32,2... | collective-permute-start | bytes 110600 | tf_op jit(solution)/shard_map/ppermute | solution.py:23
  36.9 0.0 collective-permute-done.7.refs_1_
  36.9 1.6 %collective-permute-done.8.refs_2_ = bf16[144,128]{1,0:T(8,128)(2,1)S(1)} collective-permute-done((bf16[144,128]{1,0:T(8,128)(2,1)S(1)}, bf16[144,128]{1,0:T(8,128)(2,1)S(1)}, u32[]{:S(2)}, u32[]{:S(2)}) %collective-permute-start.8) | collective-permute-done | bytes 36896 | tf_op jit(solution)/shard_map/ppermute | solution.py:23
  38.6 0.6 %total.1 = f32[144,128]{1,0:T(8,128)} custom-call(f32[144,128]{1,0:T(8,128)S(1)} %get-tuple-element.46.refs_0_, bf16[144,128]{1,0:T(8,128)(2,1)S(1)} %collective-permute-done.7.refs_1_, bf16[144,128]{1,0:T(8,128)(2,1)S(1)} %collective-permute-done.8.refs_2_), custom_call_target="tpu_custom_call" | custom-call | tf_op jit(solution)/shard_map/total/pallas_call | solution.py:400
Async XLA Ops:
  0.6 12.5 %collective-permute-start = (bf16[576,128]{1,0:T(8,128)(2,1)}, bf16[576,128]{1,0:T(8,128)(2,1)S(1)}, u32[]{:S(2)}, u32[]{:S(2)}) collective-permute-start(bf16[576,128]{1,0:T(8,128)(2,1)} %bitcast.6), channel_id=1, source_target_pairs={{0,8},{4,12},{8,16},{12,20},{16,24},{20,28},{24,32},{28,36},{32,40... | collective-permute-start | bytes 442376 | tf_op jit(solution)/shard_map/ppermute | solution.py:23
  3.2 13.7 %collective-permute-start.2 = (bf16[576,128]{1,0:T(8,128)(2,1)}, bf16[576,128]{1,0:T(8,128)(2,1)S(1)}, u32[]{:S(2)}, u32[]{:S(2)}) collective-permute-start(bf16[576,128]{1,0:T(8,128)(2,1)} %bitcast.7), channel_id=1, source_target_pairs={{0,4},{4,16},{8,12},{12,24},{16,20},{20,32},{24,28},{28,40},{32,36... | collective-permute-start | bytes 442376 | tf_op jit(solution)/shard_map/ppermute | solution.py:23
  13.1 3.8 %collective-permute-start.1 = (bf16[576,128]{1,0:T(8,128)(2,1)S(1)}, bf16[576,128]{1,0:T(8,128)(2,1)S(1)}, u32[]{:S(2)}, u32[]{:S(2)}) collective-permute-start(bf16[576,128]{1,0:T(8,128)(2,1)S(1)} %collective-permute-done.key_ref.refs_2_), channel_id=1, source_target_pairs={{0,4},{4,0},{8,12},{12,8},{16,20},{20,16},{24,28},{28,24},{32,36},... | collective-permute-start | bytes 442376 | tf_op jit(solution)/shard_map/ppermute | solution.py:23
  20.7 2.6 %collective-permute-start.3 = (bf16[576,256]{1,0:T(8,128)(2,1)S(1)}, bf16[576,256]{1,0:T(8,128)(2,1)S(1)}, u32[]{:S(2)}, u32[]{:S(2)}) collective-permute-start(bf16[576,256]{1,0:T(8,128)(2,1)S(1)} %get-tuple-element.41), channel_id=1, source_target_pairs={{0,4},{4,0},{8,12},{12,8},{16,20},{20,16},{24,28},{28,24},{32,36},... | collective-permute-start | bytes 884744 | tf_op jit(solution)/shard_map/ppermute | solution.py:23
  23.5 9.4 %collective-permute-start.4 = (bf16[144,384]{1,0:T(8,128)(2,1)S(1)}, bf16[144,384]{1,0:T(8,128)(2,1)S(1)}, u32[]{:S(2)}, u32[]{:S(2)}) collective-permute-start(bf16[144,384]{1,0:T(8,128)(2,1)S(1)} %get-tuple-element.43), channel_id=1, source_target_pairs={{0,1},{1,2},{2,3},{3,0},{4,5},{5,6},{6,7},{7,4},{8,9},{9,10},{10,1... | collective-permute-start | bytes 331784 | tf_op jit(solution)/shard_map/ppermute | solution.py:23
  24.9 8.1 %collective-permute-start.5 = (bf16[144,384]{1,0:T(8,128)(2,1)S(1)}, bf16[144,384]{1,0:T(8,128)(2,1)S(1)}, u32[]{:S(2)}, u32[]{:S(2)}) collective-permute-start(bf16[144,384]{1,0:T(8,128)(2,1)S(1)} %get-tuple-element.44), channel_id=1, source_target_pairs={{0,2},{1,3},{2,0},{3,1},{4,6},{5,7},{6,4},{7,5},{8,10},{9,11},{10,... | collective-permute-start | bytes 331784 | tf_op jit(solution)/shard_map/ppermute | solution.py:23
  27.5 5.5 %collective-permute-start.6 = (bf16[144,384]{1,0:T(8,128)(2,1)S(1)}, bf16[144,384]{1,0:T(8,128)(2,1)S(1)}, u32[]{:S(2)}, u32[]{:S(2)}) collective-permute-start(bf16[144,384]{1,0:T(8,128)(2,1)S(1)} %get-tuple-element.45), channel_id=1, source_target_pairs={{0,3},{1,0},{2,1},{3,2},{4,7},{5,4},{6,5},{7,6},{8,11},{9,8},{10,9... | collective-permute-start | bytes 331784 | tf_op jit(solution)/shard_map/ppermute | solution.py:23
  33.1 3.8 %collective-permute-start.7 = (bf16[144,128]{1,0:T(8,128)(2,1)S(1)}, bf16[144,128]{1,0:T(8,128)(2,1)S(1)}, u32[]{:S(2)}, u32[]{:S(2)}) collective-permute-start(bf16[144,128]{1,0:T(8,128)(2,1)S(1)} %get-tuple-element.47), channel_id=1, source_target_pairs={{0,248},{4,252},{8,0},{12,4},{16,8},{20,12},{24,16},{28,20},{32,24... | collective-permute-start | bytes 110600 | tf_op jit(solution)/shard_map/ppermute | solution.py:23
  34.5 4.0 %collective-permute-start.8 = (bf16[144,128]{1,0:T(8,128)(2,1)S(1)}, bf16[144,128]{1,0:T(8,128)(2,1)S(1)}, u32[]{:S(2)}, u32[]{:S(2)}) collective-permute-start(bf16[144,128]{1,0:T(8,128)(2,1)S(1)} %get-tuple-element.48), channel_id=1, source_target_pairs={{0,248},{4,244},{8,0},{12,252},{16,8},{20,4},{24,16},{28,12},{32,2... | collective-permute-start | bytes 110600 | tf_op jit(solution)/shard_map/ppermute | solution.py:23

commit v5 on v4

--- a/solution.py
+++ b/solution.py
@@ -53,9 +53,18 @@
     return dot(keys, q_cols) * (scale * math.log2(math.e)) + mask
 
 
+def partial_softmax(score, grad_weight, term_ref, stats_ref, span):
+    top = jnp.max(score, axis=0, keepdims=True)
+    terms = jnp.exp2(score - top)
+    term_ref[:, span] = terms
+    stats_ref[0:1, span] = top
+    stats_ref[1:2, span] = jnp.sum(terms, axis=0, keepdims=True)
+    stats_ref[2:3, span] = jnp.sum(terms * grad_weight, axis=0, keepdims=True)
+
+
 def own_kernel(scale, key_from, entries_from, start_from, g_from, q_from, *refs):
-    score_ref, grad_ref, q_ref, g_ref, mask_ref, key_ref, token_ref = refs[:7]
-    entries_ref, start_ref, buffer_ref, sems = refs[7:]
+    term_ref, grad_ref, stats_ref, q_ref, g_ref, mask_ref, key_ref, token_ref = refs[:8]
+    entries_ref, start_ref, buffer_ref, sems = refs[8:]
     tokens, heads, latent_width = g_from.shape
     g_chunks, q_chunks = COPIES
     tables = [
@@ -104,57 +113,91 @@
     for n, copy in enumerate(q_copies):
         copy.wait()
         q_cols = lanes(q_ref[n * part_heads : (n + 1) * part_heads])
-        score_ref[:, n * span : (n + 1) * span] = scores_of(scale, keys, mask, q_cols)
-
-
-def back_kernel(scale, mask_ref, key_ref, q_ref, g_ref, _, score_ref, grad_ref):
+        columns = slice(n * span, (n + 1) * span)
+        score = scores_of(scale, keys, mask, q_cols)
+        partial_softmax(score, grad_ref[:, columns], term_ref, stats_ref, columns)
+
+
+def back_kernel(scale, mask_ref, key_ref, q_ref, g_ref, _, term_ref, grad_ref, stats_ref):
     block = key_ref.shape[1]
     mask = mask_ref[2 * block : 3 * block, :]
     keys = key_ref[...].T
-    score_ref[...] = scores_of(scale, keys, mask, lanes(q_ref))
-    grad_ref[...] = dot(keys[:, : g_ref.shape[1]], g_ref[...], NT)
+    score = scores_of(scale, keys, mask, lanes(q_ref))
+    grad_weight = dot(keys[:, : g_ref.shape[1]], g_ref[...], NT)
+    grad_ref[...] = grad_weight
+    partial_softmax(score, grad_weight, term_ref, stats_ref, slice(None))
+
+
+def store_weights(terms, grad_weight, factor, delta, weight_ref, score_ref, span):
+    weight = terms * factor
+    grad_score = (weight * (grad_weight - delta)).astype(BF16)
+    weight = weight.astype(BF16)
+    size = weight_ref.shape[2]
+    for n in range(weight_ref.shape[0]):
+        weight_ref[n, span, :] = weight[:, n * size : (n + 1) * size]
+        score_ref[n, span, :] = grad_score[:, n * size : (n + 1) * size]
+    return weight, grad_score
+
+
+def key_grads(scale, q_cols, g_rows, weight, grad_score, grad_ref):
+    grad_ref[...] = dot(q_cols, grad_score, NT) * scale
+    grad_ref[: g_rows.shape[1], :] += dot(weight, g_rows).T
 
 
 def weights_kernel(scale, mask_ref, *refs):
-    swap_ref, cross_ref, q_ref, g_ref, *known, weight_ref, score_ref, out_ref, grad_ref = refs
+    swap_ref, cross_ref, q_ref, g_ref, *known = refs[:6]
+    weight_ref, score_ref, factors_ref, out_ref, grad_ref = refs[6:]
     keys = jnp.concatenate([swap_ref[...].T, cross_ref[...].T], axis=0)
     mask = mask_ref[: keys.shape[0], :]
     q_cols = lanes(q_ref)
-    width = g_ref.shape[1]
-    parts = [(scores_of(scale, keys, mask, q_cols), dot(keys[:, :width], g_ref[...], NT))]
-    parts += [(known[n][...], known[n + 1][...]) for n in range(0, len(known), 2)]
-    top = functools.reduce(jnp.maximum, [jnp.max(s, axis=0, keepdims=True) for s, _ in parts])
-    terms = [jnp.exp2(s - top) for s, _ in parts]
-    total = sum(jnp.sum(t, axis=0, keepdims=True) for t in terms)
+    score = scores_of(scale, keys, mask, q_cols)
+    grad_weight = dot(keys[:, : g_ref.shape[1]], g_ref[...], NT)
+    top = jnp.max(score, axis=0, keepdims=True)
+    for stats_ref in known:
+        top = jnp.maximum(top, stats_ref[0:1, :])
+    terms = jnp.exp2(score - top)
+    total = jnp.sum(terms, axis=0, keepdims=True)
+    delta = jnp.sum(terms * grad_weight, axis=0, keepdims=True)
+    factors = []
+    for stats_ref in known:
+        factors.append(jnp.exp2(stats_ref[0:1, :] - top))
+        total = total + factors[-1] * stats_ref[1:2, :]
+        delta = delta + factors[-1] * stats_ref[2:3, :]
     inverse = 1.0 / total
-    delta = inverse * sum(
-        jnp.sum(t * g, axis=0, keepdims=True) for t, (_, g) in zip(terms, parts, strict=True)
+    delta = delta * inverse
+    factors_ref[0:1, :] = delta
+    for n, factor in enumerate(factors):
+        factors_ref[n + 1 : n + 2, :] = factor * inverse
+    weight, grad_score = store_weights(
+        terms, grad_weight, inverse, delta, weight_ref, score_ref, slice(None)
     )
-    size = weight_ref.shape[2]
+    key_grads(scale, q_cols, g_ref[...], weight, grad_score, grad_ref)
+    out_ref[...] = grad_ref[...].astype(BF16)
+
+
+def keys_kernel(scale, q_ref, g_ref, factors_ref, *refs):
+    *known, weight_ref, score_ref, grad_ref = refs
+    delta = factors_ref[0:1, :]
+    weights, grad_scores = [], []
     first = 0
-    for t, (_, grad_weight) in zip(terms, parts, strict=True):
-        weight = t * inverse
-        grad_score = (weight * (grad_weight - delta)).astype(BF16)
-        weight = weight.astype(BF16)
-        if first == 0:
-            grad_ref[...] = dot(q_cols, grad_score, NT) * scale
-            grad_ref[:width, :] += dot(weight, g_ref[...]).T
-            out_ref[...] = grad_ref[...].astype(BF16)
-        last = first + t.shape[0]
-        for n in range(weight_ref.shape[0]):
-            weight_ref[n, first:last, :] = weight[:, n * size : (n + 1) * size]
-            score_ref[n, first:last, :] = grad_score[:, n * size : (n + 1) * size]
+    for n in range(len(known) // 2):
+        term_ref, block_grad_ref = known[2 * n : 2 * n + 2]
+        last = first + term_ref.shape[0]
+        weight, grad_score = store_weights(
+            term_ref[...],
+            block_grad_ref[...],
+            factors_ref[n + 1 : n + 2, :],
+            delta,
+            weight_ref,
+            score_ref,
+            slice(first, last),
+        )
+        weights.append(weight)
+        grad_scores.append(grad_score)
         first = last
-
-
-def keys_kernel(scale, q_ref, g_ref, weight_ref, score_ref, grad_ref):
-    first = weight_ref.shape[1] // 2
-    steps = range(weight_ref.shape[0])
-    width = g_ref.shape[1]
-    grad_score = jnp.concatenate([score_ref[n, first:, :] for n in steps], axis=1)
-    weight = jnp.concatenate([weight_ref[n, first:, :] for n in steps], axis=1)
-    grad_ref[...] = dot(lanes(q_ref), grad_score, NT) * scale
-    grad_ref[:width, :] += dot(weight, g_ref[...]).T
+    weight = jnp.concatenate(weights, axis=0)
+    grad_score = jnp.concatenate(grad_scores, axis=0)
+    key_grads(scale, lanes(q_ref), g_ref[...], weight, grad_score, grad_ref)
 
 
 def split_kernel(kept_ref, swap_ref, *refs):
@@ -182,8 +225,10 @@
 
 def forward_kernel(scale, *refs):
     key_refs = refs[:SLOTS]
-    weight_ref, score_ref, att_to, gq_to, cols_ref, rows_ref = refs[SLOTS : SLOTS + 6]
-    by_head_ref, att_ref, gq_ref, sems = refs[SLOTS + 6 :]
+    weight_refs = refs[SLOTS : SLOTS + 2]
+    score_refs = refs[SLOTS + 2 : SLOTS + 4]
+    att_to, gq_to, cols_ref, rows_ref, by_head_ref, att_ref, gq_ref, sems = refs[SLOTS + 4 :]
+    joined = lambda parts, step: jnp.concatenate([part[step] for part in parts], axis=0)
     block = key_refs[0].shape[1]
     tokens, heads, latent_width = att_ref.shape
     steps = heads // PART
@@ -197,7 +242,7 @@
         copies[-1].start()
 
     def grad_queries(step):
-        grad = dot(cols_ref[...], score_ref[step]) * scale
+        grad = dot(cols_ref[...], joined(score_refs, step)) * scale
         for n in range(PART):
             gq_ref[step * PART + n] = grad[:, n * block : (n + 1) * block]
         send(gq_ref, gq_to, step * PART, PART)
@@ -208,7 +253,7 @@
     grad_queries(0)
     span = PART * block
     for step in range(steps):
-        att = dot(weight_ref[step].T, rows_ref[...])
+        att = dot(joined(weight_refs, step).T, rows_ref[...])
         by_head_ref[step * span : (step + 1) * span, :] = att.astype(BF16)
     few = 256 // heads
     order = regroup(few, heads)
@@ -272,12 +317,13 @@
         bytes_accessed=4 * MIB,
         transcendentals=0,
     )
+    block_shapes = [pltpu.VMEM((n, heads * block), F32) for n in (block, block, 8)]
     in_hbm = lambda x: pltpu.with_memory_space_constraint(x, pltpu.HBM)
-    own_score, own_grad, q_t, g_rows, mask, own_t, token = pl.pallas_call(
+    own_terms, own_grad, own_stats, q_t, g_rows, mask, own_t, token = pl.pallas_call(
         functools.partial(own_kernel, scale),
         in_specs=[anywhere] * 5,
-        out_specs=[vmem] * 7,
-        out_shape=[pltpu.VMEM((block, heads * block), F32)] * 2
+        out_specs=[vmem] * 8,
+        out_shape=block_shapes
         + [
             pltpu.VMEM((heads, width, block), BF16),
             pltpu.VMEM((heads * block, latent_width), BF16),
@@ -302,27 +348,29 @@
         in_hbm(queries.transpose(1, 2, 0)),
     )
     g_rows, mask, own_t = keep(g_rows), keep(mask), keep(own_t)
-    own_score, own_grad, q_t = keep(own_score), keep(own_grad), keep(q_t)
+    own_parts = [keep(x) for x in (own_terms, own_grad, own_stats)]
+    q_t = keep(q_t)
     back, token = lax.optimization_barrier((back, token))
     swapped = moved(back, "ctx", lambda s: s ^ 1)
-    back_score, back_grad = pl.pallas_call(
+    back_parts = pl.pallas_call(
         functools.partial(back_kernel, scale),
         in_specs=[vmem] * 4 + [anywhere],
-        out_specs=[vmem] * 2,
-        out_shape=[pltpu.VMEM((block, heads * block), F32)] * 2,
+        out_specs=[vmem] * 3,
+        out_shape=block_shapes,
         compiler_params=limit(16),
         cost_estimate=block_cost,
         name="back",
     )(mask, keep(back), q_t, g_rows, token)
-    back_score, back_grad = keep(back_score), keep(back_grad)
+    back_parts = [keep(x) for x in back_parts]
     window = [keep(swapped), keep(crossed), keep(back), own_t]
 
-    weight, grad_score, to_swap = pl.pallas_call(
+    half_shapes = [pltpu.VMEM((steps, keys // 2, rows), BF16)] * 2
+    new_weight, new_score, factors, to_swap = pl.pallas_call(
         functools.partial(weights_kernel, scale),
-        in_specs=[vmem] * 9,
-        out_specs=[vmem] * 3,
-        out_shape=[pltpu.VMEM((steps, keys, rows), BF16)] * 2
-        + [pltpu.VMEM((width, keys // 2), BF16)],
+        in_specs=[vmem] * 7,
+        out_specs=[vmem] * 4,
+        out_shape=half_shapes
+        + [pltpu.VMEM((8, heads * block), F32), pltpu.VMEM((width, keys // 2), BF16)],
         scratch_shapes=[pltpu.VMEM((width, keys // 2), F32)],
         compiler_params=limit(28),
         cost_estimate=pl.CostEstimate(
@@ -331,23 +379,24 @@
             transcendentals=heads * block * keys,
         ),
         name="weights",
-    )(mask, *window[:2], q_t, g_rows, back_score, back_grad, own_score, own_grad)
-    weight, grad_score = keep(weight), keep(grad_score)
+    )(mask, *window[:2], q_t, g_rows, back_parts[2], own_parts[2])
+    new_weight, new_score = keep(new_weight), keep(new_score)
     from_swap = moved(to_swap, "ctx", lambda s: s ^ 1)
 
-    kept = pl.pallas_call(
+    kept_weight, kept_score, kept = pl.pallas_call(
         functools.partial(keys_kernel, scale),
-        in_specs=[vmem] * 4,
-        out_specs=vmem,
-        out_shape=pltpu.VMEM((width, keys // 2), F32),
-        compiler_params=limit(16),
+        in_specs=[vmem] * 7,
+        out_specs=[vmem] * 3,
+        out_shape=half_shapes + [pltpu.VMEM((width, keys // 2), F32)],
+        compiler_params=limit(24),
         cost_estimate=pl.CostEstimate(
             flops=heads * block * keys * (width + latent_width),
             bytes_accessed=8 * MIB,
             transcendentals=0,
         ),
         name="keys",
-    )(q_t, g_rows, weight, grad_score)
+    )(q_t, g_rows, keep(factors), *back_parts[:2], *own_parts[:2])
+    kept_weight, kept_score = keep(kept_weight), keep(kept_score)
 
     own, *pieces = pl.pallas_call(
         split_kernel,
@@ -364,7 +413,7 @@
 
     att, gq = pl.pallas_call(
         functools.partial(forward_kernel, scale),
-        in_specs=[vmem] * (SLOTS + 2),
+        in_specs=[vmem] * (SLOTS + 4),
         out_specs=[anywhere] * 2,
         out_shape=[
             pltpu.HBM((block, heads, latent_width), BF16),
@@ -385,7 +434,7 @@
             transcendentals=0,
         ),
         name="forward",
-    )(*window, weight, grad_score)
+    )(*window, new_weight, kept_weight, new_score, kept_score)
 
     to_far, to_back, rest = pl.pallas_call(
         merge_kernel,

time: 39.3 us -> 38.5 us (0.980)
  Pallas kernels: 15.7 us -> 15 us
    pallas_call x1, Pallas kernels: 3.81 us -> 2.99 us  [shards(): pl.pallas_call(functools.partial(weights_kernel, scale), in_specs=[vmem]...]
  transfers between devices with their start and end apart: 9 -> 9, of which waited for: 2 -> 2; matrix products, arithmetic and copies ran while one was open for 0% -> 0% of each run, Pallas kernels for 28% -> 29%
where the time goes in v5:
time: 38.5 us; the launch traced here: 38.4 us
  starting transfers between devices  19 us (49%)
  Pallas kernels  15 us (39%)
  waiting for transfers between devices  3.64 us (9%)
  between operations  0.73 us (2%)
    ppermute x9, starting transfers between devices, moved(): lax.ppermute(value, axis, [(s, target(s) % count) for s in range(count)])  19 us
    pallas_call x1, Pallas kernels, shards(): pl.pallas_call(functools.partial(forward_kernel, scale), in_specs=[vmem]...  4.37 us
    pallas_call x1, Pallas kernels, shards(): pl.pallas_call(functools.partial(own_kernel, scale), in_specs=[anywhere]...  4.08 us
    ppermute x9, waiting for transfers between devices, moved(): lax.ppermute(value, axis, [(s, target(s) % count) for s in range(count)])  3.64 us
    pallas_call x1, Pallas kernels, shards(): pl.pallas_call(functools.partial(weights_kernel, scale), in_specs=[vmem]...  2.99 us
    pallas_call x1, Pallas kernels, shards(): pl.pallas_call(functools.partial(keys_kernel, scale), in_specs=[vmem] * 7...  1.43 us
    pallas_call x1, Pallas kernels, shards(): pl.pallas_call(functools.partial(back_kernel, scale), in_specs=[vmem] * 4...  1.28 us
  transfers between devices with their start and end apart: 9, of which 2 were waited for; matrix products, arithmetic and copies ran while one was open for 0% of the time, Pallas kernels for 29%

profile of v5, /device:TPU:1, one launch (start us, length us, event | category | flops | bytes accessed | tf_op | source)
XLA Modules:
  0.0 38.4 jit_solution(823298971643319235)
XLA Ops:
  0.6 2.5 %collective-permute-start = (bf16[576,128]{1,0:T(8,128)(2,1)}, bf16[576,128]{1,0:T(8,128)(2,1)S(1)}, u32[]{:S(2)}, u32[]{:S(2)}) collective-permute-start(bf16[576,128]{1,0:T(8,128)(2,1)} %bitcast.6), channel_id=1, source_target_pairs={{0,8},{4,12},{8,16},{12,20},{16,24},{20,28},{24,32},{28,36},{32,40... | collective-permute-start | bytes 442376 | tf_op jit(solution)/shard_map/ppermute | solution.py:23
  3.2 3.8 %collective-permute-start.2 = (bf16[576,128]{1,0:T(8,128)(2,1)}, bf16[576,128]{1,0:T(8,128)(2,1)S(1)}, u32[]{:S(2)}, u32[]{:S(2)}) collective-permute-start(bf16[576,128]{1,0:T(8,128)(2,1)} %bitcast.7), channel_id=1, source_target_pairs={{0,4},{4,16},{8,12},{12,24},{16,20},{20,32},{24,28},{28,40},{32,36... | collective-permute-start | bytes 442376 | tf_op jit(solution)/shard_map/ppermute | solution.py:23
  7.0 4.1 %own.1 = (f32[128,2048]{1,0:T(8,128)S(1)}, f32[128,2048]{1,0:T(8,128)S(1)}, f32[8,2048]{1,0:T(8,128)S(1)}, bf16[16,576,128]{2,1,0:T(8,128)(2,1)S(1)}, bf16[2048,...) custom-call(bf16[576,128]{1,0:T(8,128)(2,1)} %bitcast.8, ...), custom_call_target="tpu_custom_call" | custom-call | flops 570425344 | bytes 4194304 | tf_op jit(solution)/shard_map/own/pallas_call | solution.py:322
  11.1 2.0 %collective-permute-done.key_ref.refs_2_ = bf16[576,128]{1,0:T(8,128)(2,1)S(1)} collective-permute-done((bf16[576,128]{1,0:T(8,128)(2,1)}, bf16[576,128]{1,0:T(8,128)(2,1)S(1)}, u32[]{:S(2)}, u32[]{:S(2)}) %collective-permute-start) | collective-permute-done | bytes 147488 | tf_op jit(solution)/shard_map/ppermute | solution.py:23
  13.1 2.5 %collective-permute-start.1 = (bf16[576,128]{1,0:T(8,128)(2,1)S(1)}, bf16[576,128]{1,0:T(8,128)(2,1)S(1)}, u32[]{:S(2)}, u32[]{:S(2)}) collective-permute-start(bf16[576,128]{1,0:T(8,128)(2,1)S(1)} %collective-permute-done.key_ref.refs_2_), channel_id=1, source_target_pairs={{0,4},{4,0},{8,12},{12,8},{16,20},{20,16},{24,28},{28,24},{32,36},... | collective-permute-start | bytes 442376 | tf_op jit(solution)/shard_map/ppermute | solution.py:23
  15.6 1.3 %back.1 = (f32[128,2048]{1,0:T(8,128)S(1)}, f32[128,2048]{1,0:T(8,128)S(1)}, f32[8,2048]{1,0:T(8,128)S(1)}) custom-call(f32[512,128]{1,0:T(8,128)S(1)} %get-tuple-element.35.mask_ref, bf16[576,128]{1,0:T(8,128)(2,1)S(1)} %collective-permute-done.key_ref.refs_2_, bf16[16,576,128]{2,1,0:T(8,128)(2,1)S(1)} %get-tuple-element.36.q_ref.refs_2_, ...), custom_call_target="tpu_custom_call" | custom-call | flops 570425344 | bytes 4194304 | tf_op jit(solution)/shard_map/back/pallas_call | solution.py:355
  16.9 0.0 collective-permute-done.2.refs_1_
  16.9 0.0 collective-permute-done.1.refs_0_
  16.9 3.0 %weights.1 = (bf16[4,256,512]{2,1,0:T(8,128)(2,1)S(1)}, bf16[4,256,512]{2,1,0:T(8,128)(2,1)S(1)}, f32[8,2048]{1,0:T(8,128)S(1)}, bf16[576,256]{1,0:T(8,128)(2,1)S(1)}) custom-call(f32[512,128]{1,0:T(8,128)S(1)} %get-tuple-element.35.mask_ref, bf16[576,128]{1,0:T(8,128)(2,1)S(1)} %collective-permute-done.1.refs_0_, ...), custom_call_target="tpu_custom_call" | custom-call | flops 2281701376 | bytes 12582912 | tf_op jit(solution)/shard_map/weights/pallas_call | solution.py:368
  19.9 1.2 %collective-permute-start.3 = (bf16[576,256]{1,0:T(8,128)(2,1)S(1)}, bf16[576,256]{1,0:T(8,128)(2,1)S(1)}, u32[]{:S(2)}, u32[]{:S(2)}) collective-permute-start(bf16[576,256]{1,0:T(8,128)(2,1)S(1)} %get-tuple-element.53), channel_id=1, source_target_pairs={{0,4},{4,0},{8,12},{12,8},{16,20},{20,16},{24,28},{28,24},{32,36},... | collective-permute-start | bytes 884744 | tf_op jit(solution)/shard_map/ppermute | solution.py:23
  21.1 1.4 %keys.1 = (bf16[4,256,512]{2,1,0:T(8,128)(2,1)S(1)}, bf16[4,256,512]{2,1,0:T(8,128)(2,1)S(1)}, f32[576,256]{1,0:T(8,128)S(1)}) custom-call(bf16[16,576,128]{2,1,0:T(8,128)(2,1)S(1)} %get-tuple-element.36.q_ref.refs_2_, bf16[2048,512]{1,0:T(8,128)(2,1)S(1)} %get-tuple-element.37.g_ref.refs_3_, f32[8,2048]{1,0:T(8,128)S(1)} %get-tuple-element.42.factors_ref, ...), custom_call_target="tpu_custom_call" | custom-call | flops 1140850688 | bytes 8388608 | tf_op jit(solution)/shard_map/keys/pallas_call | solution.py:386
  22.5 0.0 collective-permute-done.3.swap_ref
  22.6 0.2 split.1
  22.7 1.4 %collective-permute-start.4 = (bf16[144,384]{1,0:T(8,128)(2,1)S(1)}, bf16[144,384]{1,0:T(8,128)(2,1)S(1)}, u32[]{:S(2)}, u32[]{:S(2)}) collective-permute-start(bf16[144,384]{1,0:T(8,128)(2,1)S(1)} %get-tuple-element.55), channel_id=1, source_target_pairs={{0,1},{1,2},{2,3},{3,0},{4,5},{5,6},{6,7},{7,4},{8,9},{9,10},{10,1... | collective-permute-start | bytes 331784 | tf_op jit(solution)/shard_map/ppermute | solution.py:23
  24.1 2.6 %collective-permute-start.5 = (bf16[144,384]{1,0:T(8,128)(2,1)S(1)}, bf16[144,384]{1,0:T(8,128)(2,1)S(1)}, u32[]{:S(2)}, u32[]{:S(2)}) collective-permute-start(bf16[144,384]{1,0:T(8,128)(2,1)S(1)} %get-tuple-element.56), channel_id=1, source_target_pairs={{0,2},{1,3},{2,0},{3,1},{4,6},{5,7},{6,4},{7,5},{8,10},{9,11},{10,... | collective-permute-start | bytes 331784 | tf_op jit(solution)/shard_map/ppermute | solution.py:23
  26.7 1.1 %collective-permute-start.6 = (bf16[144,384]{1,0:T(8,128)(2,1)S(1)}, bf16[144,384]{1,0:T(8,128)(2,1)S(1)}, u32[]{:S(2)}, u32[]{:S(2)}) collective-permute-start(bf16[144,384]{1,0:T(8,128)(2,1)S(1)} %get-tuple-element.57), channel_id=1, source_target_pairs={{0,3},{1,0},{2,1},{3,2},{4,7},{5,4},{6,5},{7,6},{8,11},{9,8},{10,9... | collective-permute-start | bytes 331784 | tf_op jit(solution)/shard_map/ppermute | solution.py:23
  27.8 4.4 %forward.1 = (bf16[128,16,512]{2,1,0:T(8,128)(2,1)}, f32[16,576,128]{2,1,0:T(8,128)}) custom-call(bf16[576,128]{1,0:T(8,128)(2,1)S(1)} %collective-permute-done.1.refs_0_, bf16[576,128]{1,0:T(8,128)(2,1)S(1)} %collective-permute-done.2.refs_1_, bf16[576,128]{1,0:T(8,128)(2,1)S(1)} %collective-permute-done.key_ref.refs_2_, ...), custom_call_target="tpu_custom_call" | custom-call | flops 2281701376 | bytes 12582912 | tf_op jit(solution)/shard_map/forward/pallas_call | solution.py:414
  32.2 0.0 collective-permute-done.4.refs_0_
  32.2 0.0 collective-permute-done.5.refs_1_
  32.2 0.0 collective-permute-done.6.refs_2_
  32.2 0.1 merge.1
  32.3 1.5 %collective-permute-start.7 = (bf16[144,128]{1,0:T(8,128)(2,1)S(1)}, bf16[144,128]{1,0:T(8,128)(2,1)S(1)}, u32[]{:S(2)}, u32[]{:S(2)}) collective-permute-start(bf16[144,128]{1,0:T(8,128)(2,1)S(1)} %get-tuple-element.59), channel_id=1, source_target_pairs={{0,248},{4,252},{8,0},{12,4},{16,8},{20,12},{24,16},{28,20},{32,24... | collective-permute-start | bytes 110600 | tf_op jit(solution)/shard_map/ppermute | solution.py:23
  33.7 2.4 %collective-permute-start.8 = (bf16[144,128]{1,0:T(8,128)(2,1)S(1)}, bf16[144,128]{1,0:T(8,128)(2,1)S(1)}, u32[]{:S(2)}, u32[]{:S(2)}) collective-permute-start(bf16[144,128]{1,0:T(8,128)(2,1)S(1)} %get-tuple-element.60), channel_id=1, source_target_pairs={{0,248},{4,244},{8,0},{12,252},{16,8},{20,4},{24,16},{28,12},{32,2... | collective-permute-start | bytes 110600 | tf_op jit(solution)/shard_map/ppermute | solution.py:23
  36.1 0.0 collective-permute-done.7.refs_1_
  36.1 1.6 %collective-permute-done.8.refs_2_ = bf16[144,128]{1,0:T(8,128)(2,1)S(1)} collective-permute-done((bf16[144,128]{1,0:T(8,128)(2,1)S(1)}, bf16[144,128]{1,0:T(8,128)(2,1)S(1)}, u32[]{:S(2)}, u32[]{:S(2)}) %collective-permute-start.8) | collective-permute-done | bytes 36896 | tf_op jit(solution)/shard_map/ppermute | solution.py:23
  37.7 0.6 %total.1 = f32[144,128]{1,0:T(8,128)} custom-call(f32[144,128]{1,0:T(8,128)S(1)} %get-tuple-element.58.refs_0_, bf16[144,128]{1,0:T(8,128)(2,1)S(1)} %collective-permute-done.7.refs_1_, bf16[144,128]{1,0:T(8,128)(2,1)S(1)} %collective-permute-done.8.refs_2_), custom_call_target="tpu_custom_call" | custom-call | tf_op jit(solution)/shard_map/total/pallas_call | solution.py:449
Async XLA Ops:
  0.6 12.5 %collective-permute-start = (bf16[576,128]{1,0:T(8,128)(2,1)}, bf16[576,128]{1,0:T(8,128)(2,1)S(1)}, u32[]{:S(2)}, u32[]{:S(2)}) collective-permute-start(bf16[576,128]{1,0:T(8,128)(2,1)} %bitcast.6), channel_id=1, source_target_pairs={{0,8},{4,12},{8,16},{12,20},{16,24},{20,28},{24,32},{28,36},{32,40... | collective-permute-start | bytes 442376 | tf_op jit(solution)/shard_map/ppermute | solution.py:23
  3.2 13.7 %collective-permute-start.2 = (bf16[576,128]{1,0:T(8,128)(2,1)}, bf16[576,128]{1,0:T(8,128)(2,1)S(1)}, u32[]{:S(2)}, u32[]{:S(2)}) collective-permute-start(bf16[576,128]{1,0:T(8,128)(2,1)} %bitcast.7), channel_id=1, source_target_pairs={{0,4},{4,16},{8,12},{12,24},{16,20},{20,32},{24,28},{28,40},{32,36... | collective-permute-start | bytes 442376 | tf_op jit(solution)/shard_map/ppermute | solution.py:23
  13.1 3.8 %collective-permute-start.1 = (bf16[576,128]{1,0:T(8,128)(2,1)S(1)}, bf16[576,128]{1,0:T(8,128)(2,1)S(1)}, u32[]{:S(2)}, u32[]{:S(2)}) collective-permute-start(bf16[576,128]{1,0:T(8,128)(2,1)S(1)} %collective-permute-done.key_ref.refs_2_), channel_id=1, source_target_pairs={{0,4},{4,0},{8,12},{12,8},{16,20},{20,16},{24,28},{28,24},{32,36},... | collective-permute-start | bytes 442376 | tf_op jit(solution)/shard_map/ppermute | solution.py:23
  19.9 2.6 %collective-permute-start.3 = (bf16[576,256]{1,0:T(8,128)(2,1)S(1)}, bf16[576,256]{1,0:T(8,128)(2,1)S(1)}, u32[]{:S(2)}, u32[]{:S(2)}) collective-permute-start(bf16[576,256]{1,0:T(8,128)(2,1)S(1)} %get-tuple-element.53), channel_id=1, source_target_pairs={{0,4},{4,0},{8,12},{12,8},{16,20},{20,16},{24,28},{28,24},{32,36},... | collective-permute-start | bytes 884744 | tf_op jit(solution)/shard_map/ppermute | solution.py:23
  22.7 9.4 %collective-permute-start.4 = (bf16[144,384]{1,0:T(8,128)(2,1)S(1)}, bf16[144,384]{1,0:T(8,128)(2,1)S(1)}, u32[]{:S(2)}, u32[]{:S(2)}) collective-permute-start(bf16[144,384]{1,0:T(8,128)(2,1)S(1)} %get-tuple-element.55), channel_id=1, source_target_pairs={{0,1},{1,2},{2,3},{3,0},{4,5},{5,6},{6,7},{7,4},{8,9},{9,10},{10,1... | collective-permute-start | bytes 331784 | tf_op jit(solution)/shard_map/ppermute | solution.py:23
  24.1 8.1 %collective-permute-start.5 = (bf16[144,384]{1,0:T(8,128)(2,1)S(1)}, bf16[144,384]{1,0:T(8,128)(2,1)S(1)}, u32[]{:S(2)}, u32[]{:S(2)}) collective-permute-start(bf16[144,384]{1,0:T(8,128)(2,1)S(1)} %get-tuple-element.56), channel_id=1, source_target_pairs={{0,2},{1,3},{2,0},{3,1},{4,6},{5,7},{6,4},{7,5},{8,10},{9,11},{10,... | collective-permute-start | bytes 331784 | tf_op jit(solution)/shard_map/ppermute | solution.py:23
  26.7 5.5 %collective-permute-start.6 = (bf16[144,384]{1,0:T(8,128)(2,1)S(1)}, bf16[144,384]{1,0:T(8,128)(2,1)S(1)}, u32[]{:S(2)}, u32[]{:S(2)}) collective-permute-start(bf16[144,384]{1,0:T(8,128)(2,1)S(1)} %get-tuple-element.57), channel_id=1, source_target_pairs={{0,3},{1,0},{2,1},{3,2},{4,7},{5,4},{6,5},{7,6},{8,11},{9,8},{10,9... | collective-permute-start | bytes 331784 | tf_op jit(solution)/shard_map/ppermute | solution.py:23
  32.3 3.8 %collective-permute-start.7 = (bf16[144,128]{1,0:T(8,128)(2,1)S(1)}, bf16[144,128]{1,0:T(8,128)(2,1)S(1)}, u32[]{:S(2)}, u32[]{:S(2)}) collective-permute-start(bf16[144,128]{1,0:T(8,128)(2,1)S(1)} %get-tuple-element.59), channel_id=1, source_target_pairs={{0,248},{4,252},{8,0},{12,4},{16,8},{20,12},{24,16},{28,20},{32,24... | collective-permute-start | bytes 110600 | tf_op jit(solution)/shard_map/ppermute | solution.py:23
  33.7 4.0 %collective-permute-start.8 = (bf16[144,128]{1,0:T(8,128)(2,1)S(1)}, bf16[144,128]{1,0:T(8,128)(2,1)S(1)}, u32[]{:S(2)}, u32[]{:S(2)}) collective-permute-start(bf16[144,128]{1,0:T(8,128)(2,1)S(1)} %get-tuple-element.60), channel_id=1, source_target_pairs={{0,248},{4,244},{8,0},{12,252},{16,8},{20,4},{24,16},{28,12},{32,2... | collective-permute-start | bytes 110600 | tf_op jit(solution)/shard_map/ppermute | solution.py:23

commit v6 on v5

--- a/solution.py
+++ b/solution.py
@@ -12,7 +12,7 @@
 BF16 = jnp.bfloat16
 SLOTS = 4
 PART = 4
-COPIES = (4, 2)
+COPIES = (2, 1)
 MIB = 1 << 20
 NN = (((1,), (0,)), ((), ()))
 NT = (((1,), (1,)), ((), ()))

time: 38.5 us -> 38.5 us (level)
  waiting for transfers between devices: 3.64 us -> 4.05 us
  Pallas kernels: 15 us -> 14.6 us
    ppermute x9, waiting for transfers between devices: 3.64 us -> 4.05 us  [moved(): lax.ppermute(value, axis, [(s, target(s) % count) for s in range(count)])]
    pallas_call x1, Pallas kernels: 4.08 us -> 3.67 us  [shards(): pl.pallas_call(functools.partial(own_kernel, scale), in_specs=[anywhere]...]
  transfers between devices with their start and end apart: 9 -> 9, of which waited for: 2 -> 2; matrix products, arithmetic and copies ran while one was open for 0% -> 0% of each run, Pallas kernels for 29% -> 28%
where the time goes in v6:
time: 38.5 us; the launch traced here: 38.4 us
  starting transfers between devices  19 us (49%)
  Pallas kernels  14.6 us (38%)
  waiting for transfers between devices  4.05 us (11%)
  between operations  0.73 us (2%)
    ppermute x9, starting transfers between devices, moved(): lax.ppermute(value, axis, [(s, target(s) % count) for s in range(count)])  19 us
    pallas_call x1, Pallas kernels, shards(): pl.pallas_call(functools.partial(forward_kernel, scale), in_specs=[vmem]...  4.37 us
    ppermute x9, waiting for transfers between devices, moved(): lax.ppermute(value, axis, [(s, target(s) % count) for s in range(count)])  4.05 us
    pallas_call x1, Pallas kernels, shards(): pl.pallas_call(functools.partial(own_kernel, scale), in_specs=[anywhere]...  3.67 us
    pallas_call x1, Pallas kernels, shards(): pl.pallas_call(functools.partial(weights_kernel, scale), in_specs=[vmem]...  2.99 us
    pallas_call x1, Pallas kernels, shards(): pl.pallas_call(functools.partial(keys_kernel, scale), in_specs=[vmem] * 7...  1.43 us
    pallas_call x1, Pallas kernels, shards(): pl.pallas_call(functools.partial(back_kernel, scale), in_specs=[vmem] * 4...  1.28 us
  transfers between devices with their start and end apart: 9, of which 2 were waited for; matrix products, arithmetic and copies ran while one was open for 0% of the time, Pallas kernels for 28%

profile of v6, /device:TPU:1, one launch (start us, length us, event | category | flops | bytes accessed | tf_op | source)
XLA Modules:
  0.0 38.4 jit_solution(16341445485066895600)
XLA Ops:
  0.6 2.5 %collective-permute-start = (bf16[576,128]{1,0:T(8,128)(2,1)}, bf16[576,128]{1,0:T(8,128)(2,1)S(1)}, u32[]{:S(2)}, u32[]{:S(2)}) collective-permute-start(bf16[576,128]{1,0:T(8,128)(2,1)} %bitcast.6), channel_id=1, source_target_pairs={{0,8},{4,12},{8,16},{12,20},{16,24},{20,28},{24,32},{28,36},{32,40... | collective-permute-start | bytes 442376 | tf_op jit(solution)/shard_map/ppermute | solution.py:23
  3.2 3.8 %collective-permute-start.2 = (bf16[576,128]{1,0:T(8,128)(2,1)}, bf16[576,128]{1,0:T(8,128)(2,1)S(1)}, u32[]{:S(2)}, u32[]{:S(2)}) collective-permute-start(bf16[576,128]{1,0:T(8,128)(2,1)} %bitcast.7), channel_id=1, source_target_pairs={{0,4},{4,16},{8,12},{12,24},{16,20},{20,32},{24,28},{28,40},{32,36... | collective-permute-start | bytes 442376 | tf_op jit(solution)/shard_map/ppermute | solution.py:23
  7.0 3.7 %own.1 = (f32[128,2048]{1,0:T(8,128)S(1)}, f32[128,2048]{1,0:T(8,128)S(1)}, f32[8,2048]{1,0:T(8,128)S(1)}, bf16[16,576,128]{2,1,0:T(8,128)(2,1)S(1)}, bf16[2048,...) custom-call(bf16[576,128]{1,0:T(8,128)(2,1)} %bitcast.8, ...), custom_call_target="tpu_custom_call" | custom-call | flops 570425344 | bytes 4194304 | tf_op jit(solution)/shard_map/own/pallas_call | solution.py:322
  10.7 2.4 %collective-permute-done.key_ref.refs_2_ = bf16[576,128]{1,0:T(8,128)(2,1)S(1)} collective-permute-done((bf16[576,128]{1,0:T(8,128)(2,1)}, bf16[576,128]{1,0:T(8,128)(2,1)S(1)}, u32[]{:S(2)}, u32[]{:S(2)}) %collective-permute-start) | collective-permute-done | bytes 147488 | tf_op jit(solution)/shard_map/ppermute | solution.py:23
  13.1 2.5 %collective-permute-start.1 = (bf16[576,128]{1,0:T(8,128)(2,1)S(1)}, bf16[576,128]{1,0:T(8,128)(2,1)S(1)}, u32[]{:S(2)}, u32[]{:S(2)}) collective-permute-start(bf16[576,128]{1,0:T(8,128)(2,1)S(1)} %collective-permute-done.key_ref.refs_2_), channel_id=1, source_target_pairs={{0,4},{4,0},{8,12},{12,8},{16,20},{20,16},{24,28},{28,24},{32,36},... | collective-permute-start | bytes 442376 | tf_op jit(solution)/shard_map/ppermute | solution.py:23
  15.6 1.3 %back.1 = (f32[128,2048]{1,0:T(8,128)S(1)}, f32[128,2048]{1,0:T(8,128)S(1)}, f32[8,2048]{1,0:T(8,128)S(1)}) custom-call(f32[512,128]{1,0:T(8,128)S(1)} %get-tuple-element.35.mask_ref, bf16[576,128]{1,0:T(8,128)(2,1)S(1)} %collective-permute-done.key_ref.refs_2_, bf16[16,576,128]{2,1,0:T(8,128)(2,1)S(1)} %get-tuple-element.36.q_ref.refs_2_, ...), custom_call_target="tpu_custom_call" | custom-call | flops 570425344 | bytes 4194304 | tf_op jit(solution)/shard_map/back/pallas_call | solution.py:355
  16.9 0.0 collective-permute-done.2.refs_1_
  16.9 0.0 collective-permute-done.1.refs_0_
  16.9 3.0 %weights.1 = (bf16[4,256,512]{2,1,0:T(8,128)(2,1)S(1)}, bf16[4,256,512]{2,1,0:T(8,128)(2,1)S(1)}, f32[8,2048]{1,0:T(8,128)S(1)}, bf16[576,256]{1,0:T(8,128)(2,1)S(1)}) custom-call(f32[512,128]{1,0:T(8,128)S(1)} %get-tuple-element.35.mask_ref, bf16[576,128]{1,0:T(8,128)(2,1)S(1)} %collective-permute-done.1.refs_0_, ...), custom_call_target="tpu_custom_call" | custom-call | flops 2281701376 | bytes 12582912 | tf_op jit(solution)/shard_map/weights/pallas_call | solution.py:368
  19.9 1.2 %collective-permute-start.3 = (bf16[576,256]{1,0:T(8,128)(2,1)S(1)}, bf16[576,256]{1,0:T(8,128)(2,1)S(1)}, u32[]{:S(2)}, u32[]{:S(2)}) collective-permute-start(bf16[576,256]{1,0:T(8,128)(2,1)S(1)} %get-tuple-element.53), channel_id=1, source_target_pairs={{0,4},{4,0},{8,12},{12,8},{16,20},{20,16},{24,28},{28,24},{32,36},... | collective-permute-start | bytes 884744 | tf_op jit(solution)/shard_map/ppermute | solution.py:23
  21.1 1.4 %keys.1 = (bf16[4,256,512]{2,1,0:T(8,128)(2,1)S(1)}, bf16[4,256,512]{2,1,0:T(8,128)(2,1)S(1)}, f32[576,256]{1,0:T(8,128)S(1)}) custom-call(bf16[16,576,128]{2,1,0:T(8,128)(2,1)S(1)} %get-tuple-element.36.q_ref.refs_2_, bf16[2048,512]{1,0:T(8,128)(2,1)S(1)} %get-tuple-element.37.g_ref.refs_3_, f32[8,2048]{1,0:T(8,128)S(1)} %get-tuple-element.42.factors_ref, ...), custom_call_target="tpu_custom_call" | custom-call | flops 1140850688 | bytes 8388608 | tf_op jit(solution)/shard_map/keys/pallas_call | solution.py:386
  22.5 0.0 collective-permute-done.3.swap_ref
  22.6 0.2 split.1
  22.7 1.4 %collective-permute-start.4 = (bf16[144,384]{1,0:T(8,128)(2,1)S(1)}, bf16[144,384]{1,0:T(8,128)(2,1)S(1)}, u32[]{:S(2)}, u32[]{:S(2)}) collective-permute-start(bf16[144,384]{1,0:T(8,128)(2,1)S(1)} %get-tuple-element.55), channel_id=1, source_target_pairs={{0,1},{1,2},{2,3},{3,0},{4,5},{5,6},{6,7},{7,4},{8,9},{9,10},{10,1... | collective-permute-start | bytes 331784 | tf_op jit(solution)/shard_map/ppermute | solution.py:23
  24.1 2.6 %collective-permute-start.5 = (bf16[144,384]{1,0:T(8,128)(2,1)S(1)}, bf16[144,384]{1,0:T(8,128)(2,1)S(1)}, u32[]{:S(2)}, u32[]{:S(2)}) collective-permute-start(bf16[144,384]{1,0:T(8,128)(2,1)S(1)} %get-tuple-element.56), channel_id=1, source_target_pairs={{0,2},{1,3},{2,0},{3,1},{4,6},{5,7},{6,4},{7,5},{8,10},{9,11},{10,... | collective-permute-start | bytes 331784 | tf_op jit(solution)/shard_map/ppermute | solution.py:23
  26.7 1.1 %collective-permute-start.6 = (bf16[144,384]{1,0:T(8,128)(2,1)S(1)}, bf16[144,384]{1,0:T(8,128)(2,1)S(1)}, u32[]{:S(2)}, u32[]{:S(2)}) collective-permute-start(bf16[144,384]{1,0:T(8,128)(2,1)S(1)} %get-tuple-element.57), channel_id=1, source_target_pairs={{0,3},{1,0},{2,1},{3,2},{4,7},{5,4},{6,5},{7,6},{8,11},{9,8},{10,9... | collective-permute-start | bytes 331784 | tf_op jit(solution)/shard_map/ppermute | solution.py:23
  27.8 4.4 %forward.1 = (bf16[128,16,512]{2,1,0:T(8,128)(2,1)}, f32[16,576,128]{2,1,0:T(8,128)}) custom-call(bf16[576,128]{1,0:T(8,128)(2,1)S(1)} %collective-permute-done.1.refs_0_, bf16[576,128]{1,0:T(8,128)(2,1)S(1)} %collective-permute-done.2.refs_1_, bf16[576,128]{1,0:T(8,128)(2,1)S(1)} %collective-permute-done.key_ref.refs_2_, ...), custom_call_target="tpu_custom_call" | custom-call | flops 2281701376 | bytes 12582912 | tf_op jit(solution)/shard_map/forward/pallas_call | solution.py:414
  32.2 0.0 collective-permute-done.4.refs_0_
  32.2 0.0 collective-permute-done.5.refs_1_
  32.2 0.0 collective-permute-done.6.refs_2_
  32.2 0.1 merge.1
  32.3 1.5 %collective-permute-start.7 = (bf16[144,128]{1,0:T(8,128)(2,1)S(1)}, bf16[144,128]{1,0:T(8,128)(2,1)S(1)}, u32[]{:S(2)}, u32[]{:S(2)}) collective-permute-start(bf16[144,128]{1,0:T(8,128)(2,1)S(1)} %get-tuple-element.59), channel_id=1, source_target_pairs={{0,248},{4,252},{8,0},{12,4},{16,8},{20,12},{24,16},{28,20},{32,24... | collective-permute-start | bytes 110600 | tf_op jit(solution)/shard_map/ppermute | solution.py:23
  33.7 2.4 %collective-permute-start.8 = (bf16[144,128]{1,0:T(8,128)(2,1)S(1)}, bf16[144,128]{1,0:T(8,128)(2,1)S(1)}, u32[]{:S(2)}, u32[]{:S(2)}) collective-permute-start(bf16[144,128]{1,0:T(8,128)(2,1)S(1)} %get-tuple-element.60), channel_id=1, source_target_pairs={{0,248},{4,244},{8,0},{12,252},{16,8},{20,4},{24,16},{28,12},{32,2... | collective-permute-start | bytes 110600 | tf_op jit(solution)/shard_map/ppermute | solution.py:23
  36.1 0.0 collective-permute-done.7.refs_1_
  36.1 1.6 %collective-permute-done.8.refs_2_ = bf16[144,128]{1,0:T(8,128)(2,1)S(1)} collective-permute-done((bf16[144,128]{1,0:T(8,128)(2,1)S(1)}, bf16[144,128]{1,0:T(8,128)(2,1)S(1)}, u32[]{:S(2)}, u32[]{:S(2)}) %collective-permute-start.8) | collective-permute-done | bytes 36896 | tf_op jit(solution)/shard_map/ppermute | solution.py:23
  37.7 0.6 %total.1 = f32[144,128]{1,0:T(8,128)} custom-call(f32[144,128]{1,0:T(8,128)S(1)} %get-tuple-element.58.refs_0_, bf16[144,128]{1,0:T(8,128)(2,1)S(1)} %collective-permute-done.7.refs_1_, bf16[144,128]{1,0:T(8,128)(2,1)S(1)} %collective-permute-done.8.refs_2_), custom_call_target="tpu_custom_call" | custom-call | tf_op jit(solution)/shard_map/total/pallas_call | solution.py:449
Async XLA Ops:
  0.6 12.5 %collective-permute-start = (bf16[576,128]{1,0:T(8,128)(2,1)}, bf16[576,128]{1,0:T(8,128)(2,1)S(1)}, u32[]{:S(2)}, u32[]{:S(2)}) collective-permute-start(bf16[576,128]{1,0:T(8,128)(2,1)} %bitcast.6), channel_id=1, source_target_pairs={{0,8},{4,12},{8,16},{12,20},{16,24},{20,28},{24,32},{28,36},{32,40... | collective-permute-start | bytes 442376 | tf_op jit(solution)/shard_map/ppermute | solution.py:23
  3.2 13.7 %collective-permute-start.2 = (bf16[576,128]{1,0:T(8,128)(2,1)}, bf16[576,128]{1,0:T(8,128)(2,1)S(1)}, u32[]{:S(2)}, u32[]{:S(2)}) collective-permute-start(bf16[576,128]{1,0:T(8,128)(2,1)} %bitcast.7), channel_id=1, source_target_pairs={{0,4},{4,16},{8,12},{12,24},{16,20},{20,32},{24,28},{28,40},{32,36... | collective-permute-start | bytes 442376 | tf_op jit(solution)/shard_map/ppermute | solution.py:23
  13.1 3.8 %collective-permute-start.1 = (bf16[576,128]{1,0:T(8,128)(2,1)S(1)}, bf16[576,128]{1,0:T(8,128)(2,1)S(1)}, u32[]{:S(2)}, u32[]{:S(2)}) collective-permute-start(bf16[576,128]{1,0:T(8,128)(2,1)S(1)} %collective-permute-done.key_ref.refs_2_), channel_id=1, source_target_pairs={{0,4},{4,0},{8,12},{12,8},{16,20},{20,16},{24,28},{28,24},{32,36},... | collective-permute-start | bytes 442376 | tf_op jit(solution)/shard_map/ppermute | solution.py:23
  19.9 2.6 %collective-permute-start.3 = (bf16[576,256]{1,0:T(8,128)(2,1)S(1)}, bf16[576,256]{1,0:T(8,128)(2,1)S(1)}, u32[]{:S(2)}, u32[]{:S(2)}) collective-permute-start(bf16[576,256]{1,0:T(8,128)(2,1)S(1)} %get-tuple-element.53), channel_id=1, source_target_pairs={{0,4},{4,0},{8,12},{12,8},{16,20},{20,16},{24,28},{28,24},{32,36},... | collective-permute-start | bytes 884744 | tf_op jit(solution)/shard_map/ppermute | solution.py:23
  22.7 9.4 %collective-permute-start.4 = (bf16[144,384]{1,0:T(8,128)(2,1)S(1)}, bf16[144,384]{1,0:T(8,128)(2,1)S(1)}, u32[]{:S(2)}, u32[]{:S(2)}) collective-permute-start(bf16[144,384]{1,0:T(8,128)(2,1)S(1)} %get-tuple-element.55), channel_id=1, source_target_pairs={{0,1},{1,2},{2,3},{3,0},{4,5},{5,6},{6,7},{7,4},{8,9},{9,10},{10,1... | collective-permute-start | bytes 331784 | tf_op jit(solution)/shard_map/ppermute | solution.py:23
  24.1 8.1 %collective-permute-start.5 = (bf16[144,384]{1,0:T(8,128)(2,1)S(1)}, bf16[144,384]{1,0:T(8,128)(2,1)S(1)}, u32[]{:S(2)}, u32[]{:S(2)}) collective-permute-start(bf16[144,384]{1,0:T(8,128)(2,1)S(1)} %get-tuple-element.56), channel_id=1, source_target_pairs={{0,2},{1,3},{2,0},{3,1},{4,6},{5,7},{6,4},{7,5},{8,10},{9,11},{10,... | collective-permute-start | bytes 331784 | tf_op jit(solution)/shard_map/ppermute | solution.py:23
  26.7 5.5 %collective-permute-start.6 = (bf16[144,384]{1,0:T(8,128)(2,1)S(1)}, bf16[144,384]{1,0:T(8,128)(2,1)S(1)}, u32[]{:S(2)}, u32[]{:S(2)}) collective-permute-start(bf16[144,384]{1,0:T(8,128)(2,1)S(1)} %get-tuple-element.57), channel_id=1, source_target_pairs={{0,3},{1,0},{2,1},{3,2},{4,7},{5,4},{6,5},{7,6},{8,11},{9,8},{10,9... | collective-permute-start | bytes 331784 | tf_op jit(solution)/shard_map/ppermute | solution.py:23
  32.3 3.8 %collective-permute-start.7 = (bf16[144,128]{1,0:T(8,128)(2,1)S(1)}, bf16[144,128]{1,0:T(8,128)(2,1)S(1)}, u32[]{:S(2)}, u32[]{:S(2)}) collective-permute-start(bf16[144,128]{1,0:T(8,128)(2,1)S(1)} %get-tuple-element.59), channel_id=1, source_target_pairs={{0,248},{4,252},{8,0},{12,4},{16,8},{20,12},{24,16},{28,20},{32,24... | collective-permute-start | bytes 110600 | tf_op jit(solution)/shard_map/ppermute | solution.py:23
  33.7 4.0 %collective-permute-start.8 = (bf16[144,128]{1,0:T(8,128)(2,1)S(1)}, bf16[144,128]{1,0:T(8,128)(2,1)S(1)}, u32[]{:S(2)}, u32[]{:S(2)}) collective-permute-start(bf16[144,128]{1,0:T(8,128)(2,1)S(1)} %get-tuple-element.60), channel_id=1, source_target_pairs={{0,248},{4,244},{8,0},{12,252},{16,8},{20,4},{24,16},{28,12},{32,2... | collective-permute-start | bytes 110600 | tf_op jit(solution)/shard_map/ppermute | solution.py:23
